TPU v7x, 32 devices: a whole 2x2x4 slice. The times are simulated.
32 devices in a mesh: parts: 2 (over y), shard: 4 (over z), group: 4 (over x, core).
Axes of the slice: x: 2, y: 2, z: 4, core: 2. Of those that a mesh axis runs over, the one named last changes fastest.
Arguments:
- base: bfloat16 [4, 3, 4096, 1536], P('parts', None, 'shard'), parts along dimension 0, may hold values from -6 to 6
- narrow: bfloat16 [64, 3, 4096, 64], P('parts', None, ('shard', 'group')), parts along dimension 0, may hold values from -6 to 6
- wide: bfloat16 [64, 3, 64, 1536], P('parts', None, None, ('shard', 'group')), parts along dimension 0, may hold values from -0.75 to 0.75
- adapted_expert_index: int32 [4], P('parts'), parts along dimension 0, may hold values from 0 to 31, as said below
Outputs:
- merged: bfloat16 [4, 3, 4096, 1536], P('parts', None, 'shard'), parts along dimension 0
There are 2 independent parts, one for each index of `parts`. A program takes and returns all parts, laid end to end along the dimension named above; each array names one. Nothing has to cross between parts.
Inputs may be any that keep to these rules, and one draw needn't show every extreme that they name: `adapted_expert_index`: 2 distinct expert numbers of 0 to 31.
All inputs are finite; a program needn't handle non-finite values.
Results may differ from a plain program's by a relative error of at most 0.001.
Values may be sent and summed in bfloat16 or wider, within the bound.
No kernel may reach another device: no remote copies, remote signals or barrier semaphores. Data moves between devices by JAX's collectives and lax.ppermute only.
A program may use at most 128 MiB of HBM per device.

v0:
```python
import jax
import jax.numpy as jnp
from jax import lax
from jax.sharding import PartitionSpec as P

adapter_scale = 0.5


def on_device(base, narrow, wide, adapted_expert_index):
    chosen_narrow = jnp.take(narrow, adapted_expert_index, axis=0)
    chosen_wide = jnp.take(wide, adapted_expert_index, axis=0)
    local_slim_slice = lax.all_gather(chosen_narrow, "group", axis=2, tiled=True)
    adapter_update = jnp.einsum(
        "epdr,eprf->epdf",
        local_slim_slice,
        lax.all_gather(chosen_wide, ("shard", "group"), axis=3, tiled=True),
        preferred_element_type=jnp.float32,
    )
    return (base.astype(jnp.float32) + adapter_scale * adapter_update).astype(jnp.bfloat16)


def solution(mesh):
    return jax.shard_map(
        on_device,
        mesh=mesh,
        in_specs=(
            P("parts", None, "shard", None),
            P("parts", None, ("shard", "group"), None),
            P("parts", None, None, ("shard", "group")),
            P("parts"),
        ),
        out_specs=P("parts", None, "shard", None),
        check_vma=False,
    )
```

profile of v0, /device:TPU:0, one launch (start us, length us, event | category | flops | bytes accessed | tf_op | source)
XLA Modules:
  0.0 80.7 jit_solution(1099959726171849461)
XLA Ops:
  6.5 0.0 copy-start
  6.5 0.0 all-gather.2.cloned.1.call-start
  6.5 0.8 %compare_and_fusion = pred[2]{0:T(512)(128)(4,1)S(1)} fusion(s32[2]{0:T(128)} %param.7), kind=kLoop, calls=%fused_computation.8 | loop fusion | flops 12 | bytes 10 | tf_op jit(solution)/shard_map/jit(_take)/and | solution.py:10
  7.4 0.8 compare_select_fusion
  8.2 2.0 %gather_fusion.1 = bf16[2,3,64,96]{3,2,1,0:T(8,128)(2,1)S(1)} fusion(bf16[32,3,64,96]{3,2,1,0:T(8,128)(2,1)} %param.6, s32[1024]{0:T(1024)S(1)} %pad_clamp_fusion), kind=kCustom, calls=%fused_computation.1 | custom fusion | bytes 147464 | tf_op jit(solution)/shard_map/jit(_take)/gather | solution.py:11
  10.1 0.1 broadcast_select_fusion.1
  10.2 0.8 copy.6
  11.0 0.0 all-gather.2.cloned.1.call-update
  11.1 0.0 copy-done
  11.1 0.6 gather_fusion
  11.6 0.1 broadcast_select_fusion
  11.7 10.5 %all_gather.6 = bf16[2,3,1024,64]{2,3,1,0:T(8,128)(2,1)} all-gather(bf16[2,3,256,64]{2,3,1,0:T(8,128)(2,1)S(1)} %broadcast_select_fusion), channel_id=1, replica_groups=mesh['parts'=2,'shard'=4,'group'=4] {'group'}, dimensions={2}, use_global_device_ids=true | all-gather | bytes 983040 | tf_op jit(solution)/shard_map/all_gather | solution.py:12
  22.2 34.0 %all-gather.2.cloned.1.call-done = bf16[2,3,64,1536]{2,0,1,3:T(2,128)(2,1)} async-done(((bf16[2,3,64,96]{2,0,1,3:T(2,128)(2,1)}), bf16[2,3,64,1536]{2,0,1,3:T(2,128)(2,1)}) %all-gather.2.cloned.1.call-update) | async-done | bytes 1179664 | tf_op jit(solution)/shard_map/all_gather | solution.py:16
  56.2 17.7 %add_convert_fusion = bf16[2,3,1024,1536]{3,2,1,0:T(8,128)(2,1)} fusion(bf16[2,3,1024,1536]{3,2,1,0:T(8,128)(2,1)} %param.4, bf16[2,3,1024,64]{2,3,1,0:T(8,128)(2,1)} %all_gather.6, bf16[2,3,64,1536]{2,0,1,3:T(2,128)(2,1)} %all-gather.2.cloned.1.call-done), kind=kOutput, calls=%fused_computation.2 | convolution fusion | flops 1245708288 | bytes 39714816 | tf_op jit(solution)/shard_map/epdr,eprf->epdf/dot_general | solution.py:13
  (1 shorter events, 0.0 us)
Async XLA Ops:
  6.5 4.5 %copy-start = (bf16[32,3,256,64]{2,3,1,0:T(8,128)(2,1)S(1)}, bf16[32,3,256,64]{2,3,1,0:T(8,128)(2,1)}, u32[]{:S(2)}) copy-start(bf16[32,3,256,64]{2,3,1,0:T(8,128)(2,1)} %param.5) | copy-start | bytes 9437188
  6.5 49.7 %all-gather.2.cloned.1.call-start = ((), (), s32[]{:S(2)}) async-start(), calls=%async_computation | async-start | bytes 2506752 | tf_op jit(solution)/shard_map/all_gather | solution.py:16
Sparse Core Ops, SparseCore 0:
  11.2 45.0 all-gather.1
where the time goes:
time: 80.9 us; the launch traced here: 80.7 us
  waiting for transfers between devices  34 us (42%)
  matrix products  17.7 us (22%)
  between operations  13.4 us (17%)
  blocking collectives  10.5 us (13%)
  local copies, waits for them, and re-layouts  3.34 us (4%)
  other arithmetic  1.79 us (2%)
    all_gather x1, waiting for transfers between devices, on_device(): lax.all_gather(chosen_wide, ('shard', 'group'), axis=3, tiled=True)  34 us
    dot_general x1, matrix products, on_device(): jnp.einsum('epdr,eprf->epdf', local_slim_slice, lax.all_gather(chosen_wid...  17.7 us
    all_gather x1, blocking collectives, on_device(): lax.all_gather(chosen_narrow, 'group', axis=2, tiled=True)  10.5 us
    gather x1, local copies, waits for them, and re-layouts, on_device(): chosen_wide = jnp.take(wide, adapted_expert_index, axis=0)  1.97 us
  transfers between devices with their start and end apart: 1, of which 1 were waited for; matrix products, arithmetic and copies ran while one was open for 1% of the time, Pallas kernels for 0%

commit v1 on v0

v1 whole, which is shorter than its diff:
```python
import functools

import jax
import jax.numpy as jnp
from jax import lax
from jax.experimental import pallas as pl
from jax.experimental.pallas import tpu as pltpu
from jax.sharding import PartitionSpec as P

adapter_scale = 0.5
out_slots = 4


def select_kernel(index_ref, narrow_ref, wide_ref, n_out, w_out, n_buf, w_buf, sems):
    experts = index_ref.shape[0]
    rank = narrow_ref.shape[2]
    copies = []
    for e in range(experts):
        i = index_ref[e]
        rows = pl.ds(e * rank, rank)
        copies.append(pltpu.make_async_copy(narrow_ref.at[i], n_buf.at[:, rows], sems.at[e, 0]))
        copies.append(pltpu.make_async_copy(wide_ref.at[i], w_buf.at[:, rows], sems.at[e, 1]))
    for copy in copies:
        copy.start()
    for copy in copies:
        copy.wait()
    for p in range(n_buf.shape[0]):
        n = n_buf[p].astype(jnp.float32) * adapter_scale
        n_out[p] = n.T.astype(n_out.dtype)
        w_out[p] = w_buf[p].astype(jnp.float32).T.astype(w_out.dtype)


def select(narrow, wide, index):
    experts = index.shape[0]
    _, projections, rank, rows = narrow.shape
    columns = wide.shape[3]
    deep = experts * rank
    return pl.pallas_call(
        select_kernel,
        out_shape=(
            jax.ShapeDtypeStruct((projections, rows, deep), narrow.dtype),
            jax.ShapeDtypeStruct((projections, columns, deep), wide.dtype),
        ),
        in_specs=[
            pl.BlockSpec(memory_space=pltpu.SMEM),
            pl.BlockSpec(memory_space=pl.ANY),
            pl.BlockSpec(memory_space=pl.ANY),
        ],
        out_specs=[pl.BlockSpec(memory_space=pltpu.VMEM)] * 2,
        scratch_shapes=[
            pltpu.VMEM((projections, deep, rows), narrow.dtype),
            pltpu.VMEM((projections, deep, columns), wide.dtype),
            pltpu.SemaphoreType.DMA((experts, 2)),
        ],
        compiler_params=pltpu.CompilerParams(vmem_limit_bytes=4 * 2**20),
        name="select",
    )(index, narrow, wide)


def merge_kernel(n_order, w_order, rank, *refs):
    base_ref = refs[0]
    n_refs = refs[1 : 1 + len(n_order)]
    w_refs = refs[1 + len(n_order) : 1 + len(n_order) + len(w_order)]
    out_ref, w_all, out_buf, sems = refs[1 + len(n_order) + len(w_order) :]
    experts, projections = base_ref.shape[:2]
    rows = n_refs[0].shape[1]
    columns = w_refs[0].shape[1]
    wide_columns = base_ref.shape[3]
    step_columns = 256 if wide_columns % 256 == 0 else wide_columns
    s, g = lax.axis_index("shard"), lax.axis_index("group")

    for w_ref, place in zip(w_refs, w_order):
        at = pl.multiple_of(place(s, g) * columns, columns)
        for p in range(projections):
            w_all[p, pl.ds(at, columns), :] = w_ref[p]

    lane_expert = lax.broadcasted_iota(jnp.int32, (rows, n_refs[0].shape[2]), 1) // rank
    step = 0
    copies = []
    for p in range(projections):
        for n_ref, place in zip(n_refs, n_order):
            at = pl.multiple_of(place(s, g) * rows, rows)
            for e in range(experts):
                slot = step % out_slots
                if step >= out_slots:
                    copies[step - out_slots].wait()
                n = n_ref[p]
                n = jnp.where(lane_expert == e, n, jnp.zeros_like(n))
                for f in range(0, wide_columns, step_columns):
                    delta = lax.dot_general(
                        n,
                        w_all[p, f : f + step_columns],
                        (((1,), (1,)), ((), ())),
                        preferred_element_type=jnp.float32,
                    )
                    b = base_ref[e, p, pl.ds(at, rows), f : f + step_columns]
                    out_buf[slot, :, f : f + step_columns] = (b.astype(jnp.float32) + delta).astype(out_buf.dtype)
                copy = pltpu.make_async_copy(out_buf.at[slot], out_ref.at[e, p, pl.ds(at, rows)], sems.at[slot])
                copy.start()
                copies.append(copy)
                step += 1
    for copy in copies[max(0, step - out_slots) :]:
        copy.wait()


def merge(base, n_parts, w_parts, n_order, w_order, rank):
    experts, projections, width, wide_columns = base.shape
    _, rows, deep = n_parts[0].shape
    in_vmem = pl.BlockSpec(memory_space=pltpu.VMEM)
    return pl.pallas_call(
        functools.partial(merge_kernel, n_order, w_order, rank),
        out_shape=jax.ShapeDtypeStruct(base.shape, base.dtype),
        in_specs=[in_vmem] * (1 + len(n_parts) + len(w_parts)),
        out_specs=pl.BlockSpec(memory_space=pl.ANY),
        scratch_shapes=[
            pltpu.VMEM((projections, wide_columns, deep), base.dtype),
            pltpu.VMEM((out_slots, rows, wide_columns), base.dtype),
            pltpu.SemaphoreType.DMA((out_slots,)),
        ],
        compiler_params=pltpu.CompilerParams(vmem_limit_bytes=30 * 2**20),
        cost_estimate=pl.CostEstimate(
            flops=2 * base.size * rank, bytes_accessed=4 * base.size, transcendentals=0
        ),
        name="merge",
    )(base, *n_parts, *w_parts)


def on_device(shards, groups, base, narrow, wide, adapted_expert_index):
    rank = narrow.shape[3]
    n, w = select(jnp.swapaxes(narrow, 2, 3), wide, adapted_expert_index)
    axes = ("shard", "group")

    def send(x, shift, flip):
        pairs = []
        for s in range(shards):
            for g in range(groups):
                pairs.append((s * groups + g, (s + shift) % shards * groups + (g ^ flip)))
        return lax.ppermute(x, axes, pairs)

    if groups == 4:
        w_line = [w] + [send(w, shift, 0) for shift in range(1, shards)]
        n_pair = [n, send(n, 0, 2)]
        w_two = w_line + [send(x, 0, 2) for x in w_line]
        n_parts = n_pair + [send(x, 0, 1) for x in n_pair]
        w_parts = w_two + [send(x, 0, 1) for x in w_two]
        n_order = [lambda s, g, m=m: g ^ m for m in (0, 2, 1, 3)]
        w_order = [
            lambda s, g, m=m, k=k: lax.rem(s + (shards - k), shards) * groups + (g ^ m)
            for m in (0, 2, 1, 3)
            for k in range(shards)
        ]
    else:
        n_parts = [lax.all_gather(n, "group", axis=1, tiled=True)]
        w_parts = [lax.all_gather(w, axes, axis=1, tiled=True)]
        n_order = w_order = [lambda s, g: 0]
    return merge(base, n_parts, w_parts, n_order, w_order, rank)


def solution(mesh):
    return jax.shard_map(
        functools.partial(on_device, mesh.shape["shard"], mesh.shape["group"]),
        mesh=mesh,
        in_specs=(
            P("parts", None, "shard", None),
            P("parts", None, ("shard", "group"), None),
            P("parts", None, None, ("shard", "group")),
            P("parts"),
        ),
        out_specs=P("parts", None, "shard", None),
        check_vma=False,
    )
```

time: 80.9 us -> 46.2 us (0.57)
  waiting for transfers between devices: 34 us -> 11.7 us
  matrix products: 17.7 us -> 0 us
  between operations: 13.4 us -> 0.05 us
  starting transfers between devices: 0.01 us -> 13.2 us
  Pallas kernels: 0 us -> 10.6 us
  blocking collectives: 10.5 us -> 0 us
  local copies, waits for them, and re-layouts: 3.34 us -> 10.3 us
  other arithmetic: 1.79 us -> 0 us
    all_gather x1 -> x0, waiting for transfers between devices: 34 us -> none  [on_device(): lax.all_gather(chosen_wide, ('shard', 'group'), axis=3, tiled=True)]
    dot_general x1 -> x0, matrix products: 17.7 us -> none  [on_device(): jnp.einsum('epdr,eprf->epdf', local_slim_slice, lax.all_gather(chosen_wid...]
    ppermute x0 -> x18, starting transfers between devices: none -> 13.2 us  [send(): return lax.ppermute(x, axes, pairs)]
    ppermute x0 -> x18, waiting for transfers between devices: none -> 11.7 us  [send(): return lax.ppermute(x, axes, pairs)]
    pallas_call x0 -> x2, Pallas kernels: none -> 10.6 us  [the longest x1 9.76 us: merge(): pl.pallas_call(functools.partial(merge_kernel, n_order, w_order, rank), o...]
    all_gather x1 -> x0, blocking collectives: 10.5 us -> none  [on_device(): lax.all_gather(chosen_narrow, 'group', axis=2, tiled=True)]
    unnamed x2 -> x8, local copies, waits for them, and re-layouts: 0.01 us -> 10.3 us
    gather x2 -> x0, local copies, waits for them, and re-layouts: 2.53 us -> none  [the longest x1 1.97 us: on_device(): chosen_wide = jnp.take(wide, adapted_expert_index, axis=0)]
  transfers between devices with their start and end apart: 1 -> 18, of which waited for: 1 -> 7; matrix products, arithmetic and copies ran while one was open for 1% -> 0% of each run, Pallas kernels for 0% -> 0%
where the time goes in v1:
time: 46.2 us; the launch traced here: 45.9 us
  starting transfers between devices  13.2 us (29%)
  waiting for transfers between devices  11.7 us (25%)
  Pallas kernels  10.6 us (23%)
  local copies, waits for them, and re-layouts  10.3 us (22%)
    ppermute x18, starting transfers between devices, send(): return lax.ppermute(x, axes, pairs)  13.2 us
    ppermute x18, waiting for transfers between devices, send(): return lax.ppermute(x, axes, pairs)  11.7 us
    unnamed x8, local copies, waits for them, and re-layouts  10.3 us
    pallas_call x1, Pallas kernels, merge(): pl.pallas_call(functools.partial(merge_kernel, n_order, w_order, rank), o...  9.76 us
  transfers between devices with their start and end apart: 18, of which 7 were waited for; matrix products, arithmetic and copies ran while one was open for 0% of the time, Pallas kernels for 0%

profile of v1, /device:TPU:0, one launch (start us, length us, event | category | flops | bytes accessed | tf_op | source)
XLA Modules:
  0.0 45.9 jit_solution(17933948483424501411)
XLA Ops:
  0.0 0.0 copy-start.1
  0.0 1.9 %copy-done.1 = bf16[32,3,256,64]{2,3,1,0:T(8,128)(2,1)S(1)} copy-done((bf16[32,3,256,64]{2,3,1,0:T(8,128)(2,1)S(1)}, bf16[32,3,256,64]{2,3,1,0:T(8,128)(2,1)}, u32[]{:S(2)}) %copy-start.1) | copy-done | bytes 3145752
  1.9 0.0 copy-start.2
  1.9 1.4 %copy-done.2 = bf16[32,3,64,96]{3,2,1,0:T(8,128)(2,1)S(1)} copy-done((bf16[32,3,64,96]{3,2,1,0:T(8,128)(2,1)S(1)}, bf16[32,3,64,96]{3,2,1,0:T(8,128)(2,1)}, u32[]{:S(2)}) %copy-start.2) | copy-done | bytes 1179672
  3.3 0.0 copy-start.3
  3.3 0.7 %copy-done.3 = s32[2]{0:T(128)S(1)} copy-done((s32[2]{0:T(128)S(1)}, s32[2]{0:T(128)}, u32[]{:S(2)}) %copy-start.3) | copy-done | bytes 32
  4.0 0.9 %select.1 = (bf16[3,256,128]{2,1,0:T(8,128)(2,1)S(1)}, bf16[3,96,128]{2,1,0:T(8,128)(2,1)S(1)}) custom-call(s32[2]{0:T(128)S(1)} %copy-done.3, bf16[32,3,64,256]{3,2,1,0:T(8,128)(2,1)S(1)} %bitcast.1, bf16[32,3,64,96]{3,2,1,0:T(8,128)(2,1)S(1)} %copy-done.2), custom_call_target="tpu_custom_call" | custom-call | tf_op jit(solution)/shard_map/select/pallas_call | solution.py:38
  4.8 3.0 %collective-permute-start = (bf16[3,256,128]{2,1,0:T(8,128)(2,1)S(1)}, bf16[3,256,128]{2,1,0:T(8,128)(2,1)S(1)}, u32[]{:S(2)}, u32[]{:S(2)}) collective-permute-start(bf16[3,256,128]{2,1,0:T(8,128)(2,1)S(1)} %get-tuple-element.7.refs_1_), channel_id=1, source_target_pairs={{0,2},{1,3},{2,0},{3,1},{4,6},{5,7},{6,4},{7,5},{8,10},{9,11},{10,... | collective-permute-start | bytes 589832 | tf_op jit(solution)/shard_map/ppermute | solution.py:138
  7.8 0.0 collective-permute-start.10
  7.8 0.2 collective-permute-start.6
  8.0 4.0 %collective-permute-start.5 = (bf16[3,96,128]{2,1,0:T(8,128)(2,1)S(1)}, bf16[3,96,128]{2,1,0:T(8,128)(2,1)S(1)}, u32[]{:S(2)}, u32[]{:S(2)}) collective-permute-start(bf16[3,96,128]{2,1,0:T(8,128)(2,1)S(1)} %get-tuple-element.8.refs_5_), channel_id=1, source_target_pairs={{0,12},{1,13},{2,14},{3,15},{4,0},{5,1},{6,2},{7,3},{8,4},{9,5},{1... | collective-permute-start | bytes 221192 | tf_op jit(solution)/shard_map/ppermute | solution.py:138
  12.0 0.0 collective-permute-start.4
  12.0 0.0 collective-permute-done.10.refs_13_
  12.0 1.0 %collective-permute-start.3 = (bf16[3,96,128]{2,1,0:T(8,128)(2,1)S(1)}, bf16[3,96,128]{2,1,0:T(8,128)(2,1)S(1)}, u32[]{:S(2)}, u32[]{:S(2)}) collective-permute-start(bf16[3,96,128]{2,1,0:T(8,128)(2,1)S(1)} %get-tuple-element.8.refs_5_), channel_id=1, source_target_pairs={{0,4},{1,5},{2,6},{3,7},{4,8},{5,9},{6,10},{7,11},{8,12},{9,13},{1... | collective-permute-start | bytes 221192 | tf_op jit(solution)/shard_map/ppermute | solution.py:138
  13.0 1.3 %collective-permute-done.6.refs_9_ = bf16[3,96,128]{2,1,0:T(8,128)(2,1)S(1)} collective-permute-done((bf16[3,96,128]{2,1,0:T(8,128)(2,1)S(1)}, bf16[3,96,128]{2,1,0:T(8,128)(2,1)S(1)}, u32[]{:S(2)}, u32[]{:S(2)}) %collective-permute-start.6) | collective-permute-done | bytes 73760 | tf_op jit(solution)/shard_map/ppermute | solution.py:138
  14.3 0.0 collective-permute-start.14
  14.3 0.3 collective-permute-done.5.refs_8_
  14.7 0.2 collective-permute-start.13
  14.8 4.7 %collective-permute-done.4.refs_7_ = bf16[3,96,128]{2,1,0:T(8,128)(2,1)S(1)} collective-permute-done((bf16[3,96,128]{2,1,0:T(8,128)(2,1)S(1)}, bf16[3,96,128]{2,1,0:T(8,128)(2,1)S(1)}, u32[]{:S(2)}, u32[]{:S(2)}) %collective-permute-start.4) | collective-permute-done | bytes 73760 | tf_op jit(solution)/shard_map/ppermute | solution.py:138
  19.5 1.5 %collective-permute-start.9 = (bf16[3,96,128]{2,1,0:T(8,128)(2,1)S(1)}, bf16[3,96,128]{2,1,0:T(8,128)(2,1)S(1)}, u32[]{:S(2)}, u32[]{:S(2)}) collective-permute-start(bf16[3,96,128]{2,1,0:T(8,128)(2,1)S(1)} %collective-permute-done.5.refs_8_), channel_id=1, source_target_pairs={{0,2},{1,3},{2,0},{3,1},{4,6},{5,7},{6,4},{7,5},{8,10},{9,11},{10,... | collective-permute-start | bytes 221192 | tf_op jit(solution)/shard_map/ppermute | solution.py:138
  21.0 0.0 collective-permute-done.3.refs_6_
  21.0 0.0 collective-permute-start.12
  21.0 0.0 collective-permute-done.14.refs_17_
  21.0 0.5 %collective-permute-start.1 = (bf16[3,256,128]{2,1,0:T(8,128)(2,1)S(1)}, bf16[3,256,128]{2,1,0:T(8,128)(2,1)S(1)}, u32[]{:S(2)}, u32[]{:S(2)}) collective-permute-start(bf16[3,256,128]{2,1,0:T(8,128)(2,1)S(1)} %get-tuple-element.7.refs_1_), channel_id=1, source_target_pairs={{0,1},{1,0},{2,3},{3,2},{4,5},{5,4},{6,7},{7,6},{8,9},{9,8},{10,11... | collective-permute-start | bytes 589832 | tf_op jit(solution)/shard_map/ppermute | solution.py:138
  21.5 0.0 collective-permute-done.refs_2_
  21.5 0.1 collective-permute-start.2
  21.6 0.0 collective-permute-done.13.refs_16_
  21.6 0.5 %collective-permute-start.8 = (bf16[3,96,128]{2,1,0:T(8,128)(2,1)S(1)}, bf16[3,96,128]{2,1,0:T(8,128)(2,1)S(1)}, u32[]{:S(2)}, u32[]{:S(2)}) collective-permute-start(bf16[3,96,128]{2,1,0:T(8,128)(2,1)S(1)} %collective-permute-done.4.refs_7_), channel_id=1, source_target_pairs={{0,2},{1,3},{2,0},{3,1},{4,6},{5,7},{6,4},{7,5},{8,10},{9,11},{10,... | collective-permute-start | bytes 221192 | tf_op jit(solution)/shard_map/ppermute | solution.py:138
  22.1 1.7 %collective-permute-done.9.refs_12_ = bf16[3,96,128]{2,1,0:T(8,128)(2,1)S(1)} collective-permute-done((bf16[3,96,128]{2,1,0:T(8,128)(2,1)S(1)}, bf16[3,96,128]{2,1,0:T(8,128)(2,1)S(1)}, u32[]{:S(2)}, u32[]{:S(2)}) %collective-permute-start.9) | collective-permute-done | bytes 73760 | tf_op jit(solution)/shard_map/ppermute | solution.py:138
  23.9 0.0 collective-permute-start.11
  23.9 0.0 collective-permute-done.12.refs_15_
  23.9 1.7 %collective-permute-start.7 = (bf16[3,96,128]{2,1,0:T(8,128)(2,1)S(1)}, bf16[3,96,128]{2,1,0:T(8,128)(2,1)S(1)}, u32[]{:S(2)}, u32[]{:S(2)}) collective-permute-start(bf16[3,96,128]{2,1,0:T(8,128)(2,1)S(1)} %collective-permute-done.3.refs_6_), channel_id=1, source_target_pairs={{0,2},{1,3},{2,0},{3,1},{4,6},{5,7},{6,4},{7,5},{8,10},{9,11},{10,... | collective-permute-start | bytes 221192 | tf_op jit(solution)/shard_map/ppermute | solution.py:138
  25.6 0.6 %collective-permute-done.8.refs_11_ = bf16[3,96,128]{2,1,0:T(8,128)(2,1)S(1)} collective-permute-done((bf16[3,96,128]{2,1,0:T(8,128)(2,1)S(1)}, bf16[3,96,128]{2,1,0:T(8,128)(2,1)S(1)}, u32[]{:S(2)}, u32[]{:S(2)}) %collective-permute-start.8) | collective-permute-done | bytes 73760 | tf_op jit(solution)/shard_map/ppermute | solution.py:138
  26.2 0.0 collective-permute-start.17
  26.2 0.0 collective-permute-done.11.refs_14_
  26.2 0.5 %collective-permute-start.16 = (bf16[3,96,128]{2,1,0:T(8,128)(2,1)S(1)}, bf16[3,96,128]{2,1,0:T(8,128)(2,1)S(1)}, u32[]{:S(2)}, u32[]{:S(2)}) collective-permute-start(bf16[3,96,128]{2,1,0:T(8,128)(2,1)S(1)} %collective-permute-done.8.refs_11_), channel_id=1, source_target_pairs={{0,1},{1,0},{2,3},{3,2},{4,5},{5,4},{6,7},{7,6},{8,9},{9,8},{10,11... | collective-permute-start | bytes 221192 | tf_op jit(solution)/shard_map/ppermute | solution.py:138
  26.7 1.8 %collective-permute-done.7.refs_10_ = bf16[3,96,128]{2,1,0:T(8,128)(2,1)S(1)} collective-permute-done((bf16[3,96,128]{2,1,0:T(8,128)(2,1)S(1)}, bf16[3,96,128]{2,1,0:T(8,128)(2,1)S(1)}, u32[]{:S(2)}, u32[]{:S(2)}) %collective-permute-start.7) | collective-permute-done | bytes 73760 | tf_op jit(solution)/shard_map/ppermute | solution.py:138
  28.5 0.0 collective-permute-start.15
  28.6 0.0 collective-permute-done.1.refs_3_
  28.6 0.0 collective-permute-done.17.refs_20_
  28.6 0.0 collective-permute-done.16.refs_19_
  28.6 1.2 %collective-permute-done.15.refs_18_ = bf16[3,96,128]{2,1,0:T(8,128)(2,1)S(1)} collective-permute-done((bf16[3,96,128]{2,1,0:T(8,128)(2,1)S(1)}, bf16[3,96,128]{2,1,0:T(8,128)(2,1)S(1)}, u32[]{:S(2)}, u32[]{:S(2)}) %collective-permute-start.15) | collective-permute-done | bytes 73760 | tf_op jit(solution)/shard_map/ppermute | solution.py:138
  29.8 0.0 collective-permute-done.2.refs_4_
  29.8 0.0 copy-start
  29.8 6.4 %copy-done = bf16[2,3,1024,1536]{3,2,1,0:T(8,128)(2,1)S(1)} copy-done((bf16[2,3,1024,1536]{3,2,1,0:T(8,128)(2,1)S(1)}, bf16[2,3,1024,1536]{3,2,1,0:T(8,128)(2,1)}, u32[]{:S(2)}) %copy-start) | copy-done | bytes 18874392
  36.2 9.8 %merge.1 = bf16[2,3,1024,1536]{3,2,1,0:T(8,128)(2,1)} custom-call(bf16[2,3,1024,1536]{3,2,1,0:T(8,128)(2,1)S(1)} %copy-done, bf16[3,256,128]{2,1,0:T(8,128)(2,1)S(1)} %get-tuple-element.7.refs_1_, bf16[3,256,128]{2,1,0:T(8,128)(2,1)S(1)} %collective-permute-done.refs_2_, bf16[3,256,128]{2,1,0:T(8,128)(2,1)S(1)} %collective-permute-done.1.refs_3_, ...), custom_call_target="tpu_custom_call" | custom-call | flops 1207959552 | bytes 37748736 | tf_op jit(solution)/shard_map/merge/pallas_call | solution.py:110
Async XLA Ops:
  0.0 1.9 %copy-start.1 = (bf16[32,3,256,64]{2,3,1,0:T(8,128)(2,1)S(1)}, bf16[32,3,256,64]{2,3,1,0:T(8,128)(2,1)}, u32[]{:S(2)}) copy-start(bf16[32,3,256,64]{2,3,1,0:T(8,128)(2,1)} %param.5) | copy-start | bytes 9437188
  1.9 1.4 %copy-start.2 = (bf16[32,3,64,96]{3,2,1,0:T(8,128)(2,1)S(1)}, bf16[32,3,64,96]{3,2,1,0:T(8,128)(2,1)}, u32[]{:S(2)}) copy-start(bf16[32,3,64,96]{3,2,1,0:T(8,128)(2,1)} %wide_ref.1) | copy-start | bytes 3538948
  3.3 0.7 %copy-start.3 = (s32[2]{0:T(128)S(1)}, s32[2]{0:T(128)}, u32[]{:S(2)}) copy-start(s32[2]{0:T(128)} %index_ref.1) | copy-start | bytes 28
  4.8 16.7 %collective-permute-start = (bf16[3,256,128]{2,1,0:T(8,128)(2,1)S(1)}, bf16[3,256,128]{2,1,0:T(8,128)(2,1)S(1)}, u32[]{:S(2)}, u32[]{:S(2)}) collective-permute-start(bf16[3,256,128]{2,1,0:T(8,128)(2,1)S(1)} %get-tuple-element.7.refs_1_), channel_id=1, source_target_pairs={{0,2},{1,3},{2,0},{3,1},{4,6},{5,7},{6,4},{7,5},{8,10},{9,11},{10,... | collective-permute-start | bytes 589832 | tf_op jit(solution)/shard_map/ppermute | solution.py:138
  7.8 4.1 %collective-permute-start.10 = (bf16[3,96,128]{2,1,0:T(8,128)(2,1)S(1)}, bf16[3,96,128]{2,1,0:T(8,128)(2,1)S(1)}, u32[]{:S(2)}, u32[]{:S(2)}) collective-permute-start(bf16[3,96,128]{2,1,0:T(8,128)(2,1)S(1)} %get-tuple-element.8.refs_5_), channel_id=1, source_target_pairs={{0,1},{1,0},{2,3},{3,2},{4,5},{5,4},{6,7},{7,6},{8,9},{9,8},{10,11... | collective-permute-start | bytes 221192 | tf_op jit(solution)/shard_map/ppermute | solution.py:138
  7.8 6.5 %collective-permute-start.6 = (bf16[3,96,128]{2,1,0:T(8,128)(2,1)S(1)}, bf16[3,96,128]{2,1,0:T(8,128)(2,1)S(1)}, u32[]{:S(2)}, u32[]{:S(2)}) collective-permute-start(bf16[3,96,128]{2,1,0:T(8,128)(2,1)S(1)} %get-tuple-element.8.refs_5_), channel_id=1, source_target_pairs={{0,2},{1,3},{2,0},{3,1},{4,6},{5,7},{6,4},{7,5},{8,10},{9,11},{10,... | collective-permute-start | bytes 221192 | tf_op jit(solution)/shard_map/ppermute | solution.py:138
  8.0 6.6 %collective-permute-start.5 = (bf16[3,96,128]{2,1,0:T(8,128)(2,1)S(1)}, bf16[3,96,128]{2,1,0:T(8,128)(2,1)S(1)}, u32[]{:S(2)}, u32[]{:S(2)}) collective-permute-start(bf16[3,96,128]{2,1,0:T(8,128)(2,1)S(1)} %get-tuple-element.8.refs_5_), channel_id=1, source_target_pairs={{0,12},{1,13},{2,14},{3,15},{4,0},{5,1},{6,2},{7,3},{8,4},{9,5},{1... | collective-permute-start | bytes 221192 | tf_op jit(solution)/shard_map/ppermute | solution.py:138
  12.0 7.5 %collective-permute-start.4 = (bf16[3,96,128]{2,1,0:T(8,128)(2,1)S(1)}, bf16[3,96,128]{2,1,0:T(8,128)(2,1)S(1)}, u32[]{:S(2)}, u32[]{:S(2)}) collective-permute-start(bf16[3,96,128]{2,1,0:T(8,128)(2,1)S(1)} %get-tuple-element.8.refs_5_), channel_id=1, source_target_pairs={{0,8},{1,9},{2,10},{3,11},{4,12},{5,13},{6,14},{7,15},{8,0},{9,1},... | collective-permute-start | bytes 221192 | tf_op jit(solution)/shard_map/ppermute | solution.py:138
  12.0 9.0 %collective-permute-start.3 = (bf16[3,96,128]{2,1,0:T(8,128)(2,1)S(1)}, bf16[3,96,128]{2,1,0:T(8,128)(2,1)S(1)}, u32[]{:S(2)}, u32[]{:S(2)}) collective-permute-start(bf16[3,96,128]{2,1,0:T(8,128)(2,1)S(1)} %get-tuple-element.8.refs_5_), channel_id=1, source_target_pairs={{0,4},{1,5},{2,6},{3,7},{4,8},{5,9},{6,10},{7,11},{8,12},{9,13},{1... | collective-permute-start | bytes 221192 | tf_op jit(solution)/shard_map/ppermute | solution.py:138
  14.3 6.7 %collective-permute-start.14 = (bf16[3,96,128]{2,1,0:T(8,128)(2,1)S(1)}, bf16[3,96,128]{2,1,0:T(8,128)(2,1)S(1)}, u32[]{:S(2)}, u32[]{:S(2)}) collective-permute-start(bf16[3,96,128]{2,1,0:T(8,128)(2,1)S(1)} %collective-permute-done.6.refs_9_), channel_id=1, source_target_pairs={{0,1},{1,0},{2,3},{3,2},{4,5},{5,4},{6,7},{7,6},{8,9},{9,8},{10,11... | collective-permute-start | bytes 221192 | tf_op jit(solution)/shard_map/ppermute | solution.py:138
  14.7 6.9 %collective-permute-start.13 = (bf16[3,96,128]{2,1,0:T(8,128)(2,1)S(1)}, bf16[3,96,128]{2,1,0:T(8,128)(2,1)S(1)}, u32[]{:S(2)}, u32[]{:S(2)}) collective-permute-start(bf16[3,96,128]{2,1,0:T(8,128)(2,1)S(1)} %collective-permute-done.5.refs_8_), channel_id=1, source_target_pairs={{0,1},{1,0},{2,3},{3,2},{4,5},{5,4},{6,7},{7,6},{8,9},{9,8},{10,11... | collective-permute-start | bytes 221192 | tf_op jit(solution)/shard_map/ppermute | solution.py:138
  19.5 4.4 %collective-permute-start.9 = (bf16[3,96,128]{2,1,0:T(8,128)(2,1)S(1)}, bf16[3,96,128]{2,1,0:T(8,128)(2,1)S(1)}, u32[]{:S(2)}, u32[]{:S(2)}) collective-permute-start(bf16[3,96,128]{2,1,0:T(8,128)(2,1)S(1)} %collective-permute-done.5.refs_8_), channel_id=1, source_target_pairs={{0,2},{1,3},{2,0},{3,1},{4,6},{5,7},{6,4},{7,5},{8,10},{9,11},{10,... | collective-permute-start | bytes 221192 | tf_op jit(solution)/shard_map/ppermute | solution.py:138
  21.0 2.9 %collective-permute-start.12 = (bf16[3,96,128]{2,1,0:T(8,128)(2,1)S(1)}, bf16[3,96,128]{2,1,0:T(8,128)(2,1)S(1)}, u32[]{:S(2)}, u32[]{:S(2)}) collective-permute-start(bf16[3,96,128]{2,1,0:T(8,128)(2,1)S(1)} %collective-permute-done.4.refs_7_), channel_id=1, source_target_pairs={{0,1},{1,0},{2,3},{3,2},{4,5},{5,4},{6,7},{7,6},{8,9},{9,8},{10,11... | collective-permute-start | bytes 221192 | tf_op jit(solution)/shard_map/ppermute | solution.py:138
  21.0 7.5 %collective-permute-start.1 = (bf16[3,256,128]{2,1,0:T(8,128)(2,1)S(1)}, bf16[3,256,128]{2,1,0:T(8,128)(2,1)S(1)}, u32[]{:S(2)}, u32[]{:S(2)}) collective-permute-start(bf16[3,256,128]{2,1,0:T(8,128)(2,1)S(1)} %get-tuple-element.7.refs_1_), channel_id=1, source_target_pairs={{0,1},{1,0},{2,3},{3,2},{4,5},{5,4},{6,7},{7,6},{8,9},{9,8},{10,11... | collective-permute-start | bytes 589832 | tf_op jit(solution)/shard_map/ppermute | solution.py:138
  21.5 8.3 %collective-permute-start.2 = (bf16[3,256,128]{2,1,0:T(8,128)(2,1)S(1)}, bf16[3,256,128]{2,1,0:T(8,128)(2,1)S(1)}, u32[]{:S(2)}, u32[]{:S(2)}) collective-permute-start(bf16[3,256,128]{2,1,0:T(8,128)(2,1)S(1)} %collective-permute-done.refs_2_), channel_id=1, source_target_pairs={{0,1},{1,0},{2,3},{3,2},{4,5},{5,4},{6,7},{7,6},{8,9},{9,8},{10,11... | collective-permute-start | bytes 589832 | tf_op jit(solution)/shard_map/ppermute | solution.py:138
  21.6 4.6 %collective-permute-start.8 = (bf16[3,96,128]{2,1,0:T(8,128)(2,1)S(1)}, bf16[3,96,128]{2,1,0:T(8,128)(2,1)S(1)}, u32[]{:S(2)}, u32[]{:S(2)}) collective-permute-start(bf16[3,96,128]{2,1,0:T(8,128)(2,1)S(1)} %collective-permute-done.4.refs_7_), channel_id=1, source_target_pairs={{0,2},{1,3},{2,0},{3,1},{4,6},{5,7},{6,4},{7,5},{8,10},{9,11},{10,... | collective-permute-start | bytes 221192 | tf_op jit(solution)/shard_map/ppermute | solution.py:138
  23.9 2.4 %collective-permute-start.11 = (bf16[3,96,128]{2,1,0:T(8,128)(2,1)S(1)}, bf16[3,96,128]{2,1,0:T(8,128)(2,1)S(1)}, u32[]{:S(2)}, u32[]{:S(2)}) collective-permute-start(bf16[3,96,128]{2,1,0:T(8,128)(2,1)S(1)} %collective-permute-done.3.refs_6_), channel_id=1, source_target_pairs={{0,1},{1,0},{2,3},{3,2},{4,5},{5,4},{6,7},{7,6},{8,9},{9,8},{10,11... | collective-permute-start | bytes 221192 | tf_op jit(solution)/shard_map/ppermute | solution.py:138
  23.9 4.7 %collective-permute-start.7 = (bf16[3,96,128]{2,1,0:T(8,128)(2,1)S(1)}, bf16[3,96,128]{2,1,0:T(8,128)(2,1)S(1)}, u32[]{:S(2)}, u32[]{:S(2)}) collective-permute-start(bf16[3,96,128]{2,1,0:T(8,128)(2,1)S(1)} %collective-permute-done.3.refs_6_), channel_id=1, source_target_pairs={{0,2},{1,3},{2,0},{3,1},{4,6},{5,7},{6,4},{7,5},{8,10},{9,11},{10,... | collective-permute-start | bytes 221192 | tf_op jit(solution)/shard_map/ppermute | solution.py:138
  26.2 2.3 %collective-permute-start.17 = (bf16[3,96,128]{2,1,0:T(8,128)(2,1)S(1)}, bf16[3,96,128]{2,1,0:T(8,128)(2,1)S(1)}, u32[]{:S(2)}, u32[]{:S(2)}) collective-permute-start(bf16[3,96,128]{2,1,0:T(8,128)(2,1)S(1)} %collective-permute-done.9.refs_12_), channel_id=1, source_target_pairs={{0,1},{1,0},{2,3},{3,2},{4,5},{5,4},{6,7},{7,6},{8,9},{9,8},{10,11... | collective-permute-start | bytes 221192 | tf_op jit(solution)/shard_map/ppermute | solution.py:138
  26.2 2.3 %collective-permute-start.16 = (bf16[3,96,128]{2,1,0:T(8,128)(2,1)S(1)}, bf16[3,96,128]{2,1,0:T(8,128)(2,1)S(1)}, u32[]{:S(2)}, u32[]{:S(2)}) collective-permute-start(bf16[3,96,128]{2,1,0:T(8,128)(2,1)S(1)} %collective-permute-done.8.refs_11_), channel_id=1, source_target_pairs={{0,1},{1,0},{2,3},{3,2},{4,5},{5,4},{6,7},{7,6},{8,9},{9,8},{10,11... | collective-permute-start | bytes 221192 | tf_op jit(solution)/shard_map/ppermute | solution.py:138
  28.5 1.3 %collective-permute-start.15 = (bf16[3,96,128]{2,1,0:T(8,128)(2,1)S(1)}, bf16[3,96,128]{2,1,0:T(8,128)(2,1)S(1)}, u32[]{:S(2)}, u32[]{:S(2)}) collective-permute-start(bf16[3,96,128]{2,1,0:T(8,128)(2,1)S(1)} %collective-permute-done.7.refs_10_), channel_id=1, source_target_pairs={{0,1},{1,0},{2,3},{3,2},{4,5},{5,4},{6,7},{7,6},{8,9},{9,8},{10,11... | collective-permute-start | bytes 221192 | tf_op jit(solution)/shard_map/ppermute | solution.py:138
  29.8 6.4 %copy-start = (bf16[2,3,1024,1536]{3,2,1,0:T(8,128)(2,1)S(1)}, bf16[2,3,1024,1536]{3,2,1,0:T(8,128)(2,1)}, u32[]{:S(2)}) copy-start(bf16[2,3,1024,1536]{3,2,1,0:T(8,128)(2,1)} %refs_0_.1) | copy-start | bytes 56623108

commit v2 on v1

--- a/solution.py
+++ b/solution.py
@@ -11,12 +11,15 @@
 out_slots = 4
 
 
-def select_kernel(index_ref, narrow_ref, wide_ref, n_out, w_out, n_buf, w_buf, sems):
+def select_kernel(index_ref, narrow_ref, wide_ref, n_out, w_out, index, n_buf, w_buf, index_sem, sems):
     experts = index_ref.shape[0]
     rank = narrow_ref.shape[2]
+    index_copy = pltpu.make_async_copy(index_ref, index, index_sem)
+    index_copy.start()
+    index_copy.wait()
     copies = []
     for e in range(experts):
-        i = index_ref[e]
+        i = index[e]
         rows = pl.ds(e * rank, rank)
         copies.append(pltpu.make_async_copy(narrow_ref.at[i], n_buf.at[:, rows], sems.at[e, 0]))
         copies.append(pltpu.make_async_copy(wide_ref.at[i], w_buf.at[:, rows], sems.at[e, 1]))
@@ -27,10 +30,12 @@
     for p in range(n_buf.shape[0]):
         n = n_buf[p].astype(jnp.float32) * adapter_scale
         n_out[p] = n.T.astype(n_out.dtype)
-        w_out[p] = w_buf[p].astype(jnp.float32).T.astype(w_out.dtype)
+        w = w_buf[p].astype(jnp.float32).T.astype(w_out.dtype)
+        for k in range(w_out.shape[0]):
+            w_out[k, p] = w
 
 
-def select(narrow, wide, index):
+def select(narrow, wide, index, copies):
     experts = index.shape[0]
     _, projections, rank, rows = narrow.shape
     columns = wide.shape[3]
@@ -39,22 +44,39 @@
         select_kernel,
         out_shape=(
             jax.ShapeDtypeStruct((projections, rows, deep), narrow.dtype),
-            jax.ShapeDtypeStruct((projections, columns, deep), wide.dtype),
+            jax.ShapeDtypeStruct((copies, projections, columns, deep), wide.dtype),
         ),
-        in_specs=[
-            pl.BlockSpec(memory_space=pltpu.SMEM),
-            pl.BlockSpec(memory_space=pl.ANY),
-            pl.BlockSpec(memory_space=pl.ANY),
-        ],
+        in_specs=[pl.BlockSpec(memory_space=pltpu.HBM)] * 3,
         out_specs=[pl.BlockSpec(memory_space=pltpu.VMEM)] * 2,
         scratch_shapes=[
+            pltpu.SMEM((experts,), index.dtype),
             pltpu.VMEM((projections, deep, rows), narrow.dtype),
             pltpu.VMEM((projections, deep, columns), wide.dtype),
+            pltpu.SemaphoreType.DMA,
             pltpu.SemaphoreType.DMA((experts, 2)),
         ],
         compiler_params=pltpu.CompilerParams(vmem_limit_bytes=4 * 2**20),
         name="select",
-    )(index, narrow, wide)
+    )(*[pltpu.with_memory_space_constraint(x, pltpu.HBM) for x in (index, narrow, wide)])
+
+
+def load_kernel(base_ref, out_ref, sem):
+    copy = pltpu.make_async_copy(base_ref, out_ref, sem)
+    copy.start()
+    copy.wait()
+
+
+def load(base):
+    return pl.pallas_call(
+        load_kernel,
+        out_shape=jax.ShapeDtypeStruct(base.shape, base.dtype),
+        in_specs=[pl.BlockSpec(memory_space=pltpu.HBM)],
+        out_specs=pl.BlockSpec(memory_space=pltpu.VMEM),
+        scratch_shapes=[pltpu.SemaphoreType.DMA],
+        compiler_params=pltpu.CompilerParams(vmem_limit_bytes=24 * 2**20),
+        cost_estimate=pl.CostEstimate(flops=0, bytes_accessed=2 * base.size, transcendentals=0),
+        name="load",
+    )(base)
 
 
 def merge_kernel(n_order, w_order, rank, *refs):
@@ -64,22 +86,23 @@
     out_ref, w_all, out_buf, sems = refs[1 + len(n_order) + len(w_order) :]
     experts, projections = base_ref.shape[:2]
     rows = n_refs[0].shape[1]
-    columns = w_refs[0].shape[1]
+    pieces, _, columns, _ = w_refs[0].shape
     wide_columns = base_ref.shape[3]
     step_columns = 256 if wide_columns % 256 == 0 else wide_columns
-    s, g = lax.axis_index("shard"), lax.axis_index("group")
+    g = lax.axis_index("group")
 
     for w_ref, place in zip(w_refs, w_order):
-        at = pl.multiple_of(place(s, g) * columns, columns)
-        for p in range(projections):
-            w_all[p, pl.ds(at, columns), :] = w_ref[p]
+        for k in range(pieces):
+            at = pl.multiple_of(place(k, g) * columns, columns)
+            for p in range(projections):
+                w_all[p, pl.ds(at, columns), :] = w_ref[k, p]
 
     lane_expert = lax.broadcasted_iota(jnp.int32, (rows, n_refs[0].shape[2]), 1) // rank
     step = 0
     copies = []
     for p in range(projections):
         for n_ref, place in zip(n_refs, n_order):
-            at = pl.multiple_of(place(s, g) * rows, rows)
+            at = pl.multiple_of(place(g) * rows, rows)
             for e in range(experts):
                 slot = step % out_slots
                 if step >= out_slots:
@@ -127,33 +150,28 @@
 
 def on_device(shards, groups, base, narrow, wide, adapted_expert_index):
     rank = narrow.shape[3]
-    n, w = select(jnp.swapaxes(narrow, 2, 3), wide, adapted_expert_index)
+    by_hand = groups == 4
+    n, w = select(jnp.swapaxes(narrow, 2, 3), wide, adapted_expert_index, shards if by_hand else 1)
     axes = ("shard", "group")
 
-    def send(x, shift, flip):
-        pairs = []
-        for s in range(shards):
-            for g in range(groups):
-                pairs.append((s * groups + g, (s + shift) % shards * groups + (g ^ flip)))
-        return lax.ppermute(x, axes, pairs)
+    def flip(x, bit):
+        pairs = [(g, g ^ bit) for g in range(groups)]
+        return lax.ppermute(x, "group", pairs)
 
-    if groups == 4:
-        w_line = [w] + [send(w, shift, 0) for shift in range(1, shards)]
-        n_pair = [n, send(n, 0, 2)]
-        w_two = w_line + [send(x, 0, 2) for x in w_line]
-        n_parts = n_pair + [send(x, 0, 1) for x in n_pair]
-        w_parts = w_two + [send(x, 0, 1) for x in w_two]
-        n_order = [lambda s, g, m=m: g ^ m for m in (0, 2, 1, 3)]
-        w_order = [
-            lambda s, g, m=m, k=k: lax.rem(s + (shards - k), shards) * groups + (g ^ m)
-            for m in (0, 2, 1, 3)
-            for k in range(shards)
-        ]
+    if by_hand:
+        n_x = flip(n, 2)
+        w_line = lax.all_to_all(w, "shard", 0, 0)
+        w_x = flip(w_line, 2)
+        n_parts = [n, n_x, flip(n, 1), flip(n_x, 1)]
+        w_parts = [w_line, w_x, flip(w_line, 1), flip(w_x, 1)]
+        n_order = [lambda g, m=m: g ^ m for m in (0, 2, 1, 3)]
+        w_order = [lambda k, g, m=m: k * groups + (g ^ m) for m in (0, 2, 1, 3)]
     else:
         n_parts = [lax.all_gather(n, "group", axis=1, tiled=True)]
-        w_parts = [lax.all_gather(w, axes, axis=1, tiled=True)]
-        n_order = w_order = [lambda s, g: 0]
-    return merge(base, n_parts, w_parts, n_order, w_order, rank)
+        w_parts = [lax.all_gather(w, axes, axis=2, tiled=True)]
+        n_order = [lambda g: 0]
+        w_order = [lambda k, g: 0]
+    return merge(load(base), n_parts, w_parts, n_order, w_order, rank)
 
 
 def solution(mesh):

time: 46.2 us -> 44.8 us (0.970)
  blocking collectives: 0 us -> 15.7 us
  starting transfers between devices: 13.2 us -> 2.54 us
  local copies, waits for them, and re-layouts: 10.3 us -> 0 us
  Pallas kernels: 10.6 us -> 17.9 us
  waiting for transfers between devices: 11.7 us -> 8.39 us
    all_to_all x0 -> x1, blocking collectives: none -> 15.7 us  [on_device(): w_line = lax.all_to_all(w, 'shard', 0, 0)]
    ppermute x18 -> x6, starting transfers between devices: 13.2 us -> 2.54 us  [flip(): return lax.ppermute(x, 'group', pairs)]
    unnamed x8 -> x0, local copies, waits for them, and re-layouts: 10.3 us -> none
    pallas_call x0 -> x1, Pallas kernels: none -> 6.37 us  [load(): pl.pallas_call(load_kernel, out_shape=jax.ShapeDtypeStruct(base.shape, ba...]
    ppermute x18 -> x6, waiting for transfers between devices: 11.7 us -> 8.39 us  [flip(): return lax.ppermute(x, 'group', pairs)]
    pallas_call x1, Pallas kernels: 0.88 us -> 1.84 us  [select(): pl.pallas_call(select_kernel, out_shape=(jax.ShapeDtypeStruct((projection...]
  transfers between devices with their start and end apart: 18 -> 6, of which waited for: 7 -> 2; matrix products, arithmetic and copies ran while one was open for 0% -> 0% of each run, Pallas kernels for 0% -> 14%
where the time goes in v2:
time: 44.8 us; the launch traced here: 44.6 us
  Pallas kernels  17.9 us (40%)
  blocking collectives  15.7 us (35%)
  waiting for transfers between devices  8.39 us (19%)
  starting transfers between devices  2.54 us (6%)
    all_to_all x1, blocking collectives, on_device(): w_line = lax.all_to_all(w, 'shard', 0, 0)  15.7 us
    pallas_call x1, Pallas kernels, merge(): pl.pallas_call(functools.partial(merge_kernel, n_order, w_order, rank), o...  9.67 us
    ppermute x6, waiting for transfers between devices, flip(): return lax.ppermute(x, 'group', pairs)  8.39 us
    pallas_call x1, Pallas kernels, load(): pl.pallas_call(load_kernel, out_shape=jax.ShapeDtypeStruct(base.shape, ba...  6.37 us
    ppermute x6, starting transfers between devices, flip(): return lax.ppermute(x, 'group', pairs)  2.54 us
    pallas_call x1, Pallas kernels, select(): pl.pallas_call(select_kernel, out_shape=(jax.ShapeDtypeStruct((projection...  1.84 us
  transfers between devices with their start and end apart: 6, of which 2 were waited for; matrix products, arithmetic and copies ran while one was open for 0% of the time, Pallas kernels for 14%

profile of v2, /device:TPU:0, one launch (start us, length us, event | category | flops | bytes accessed | tf_op | source)
XLA Modules:
  0.0 44.6 jit_solution(15812697650420503531)
XLA Ops:
  0.0 1.8 %select.1 = (bf16[3,256,128]{2,1,0:T(8,128)(2,1)S(1)}, bf16[4,3,96,128]{3,2,1,0:T(8,128)(2,1)S(1)}) custom-call(s32[2]{0:T(128)} %index_ref.1, bf16[32,3,64,256]{3,2,1,0:T(8,128)(2,1)} %bitcast.1, bf16[32,3,64,96]{3,2,1,0:T(8,128)(2,1)} %wide_ref.1), custom_call_target="tpu_custom_call" | custom-call | tf_op jit(solution)/shard_map/select/pallas_call | solution.py:43
  1.9 15.7 %all_to_all.5.refs_5_ = bf16[4,3,96,128]{3,2,1,0:T(8,128)(2,1)S(1)} all-to-all(bf16[4,3,96,128]{3,2,1,0:T(8,128)(2,1)S(1)} %get-tuple-element.8), channel_id=1, replica_groups=mesh['parts'=2,'shard'=4,'group'=4] {'shard'}, dimensions={0} | all-to-all | bytes 589824 | tf_op jit(solution)/shard_map/all_to_all | solution.py:163
  17.5 1.5 %collective-permute-start.3 = (bf16[4,3,96,128]{3,2,1,0:T(8,128)(2,1)S(1)}, bf16[4,3,96,128]{3,2,1,0:T(8,128)(2,1)S(1)}, u32[]{:S(2)}, u32[]{:S(2)}) collective-permute-start(bf16[4,3,96,128]{3,2,1,0:T(8,128)(2,1)S(1)} %all_to_all.5.refs_5_), channel_id=1, source_target_pairs={{0,2},{1,3},{2,0},{3,1},{4,6},{5,7},{6,4},{7,5},{8,10},{9,11},{10,... | collective-permute-start | bytes 884744 | tf_op jit(solution)/shard_map/ppermute | solution.py:159
  19.0 0.5 %collective-permute-start = (bf16[3,256,128]{2,1,0:T(8,128)(2,1)S(1)}, bf16[3,256,128]{2,1,0:T(8,128)(2,1)S(1)}, u32[]{:S(2)}, u32[]{:S(2)}) collective-permute-start(bf16[3,256,128]{2,1,0:T(8,128)(2,1)S(1)} %get-tuple-element.7.refs_1_), channel_id=1, source_target_pairs={{0,2},{1,3},{2,0},{3,1},{4,6},{5,7},{6,4},{7,5},{8,10},{9,11},{10,... | collective-permute-start | bytes 589832 | tf_op jit(solution)/shard_map/ppermute | solution.py:159
  19.6 0.0 collective-permute-start.4
  19.6 6.8 %collective-permute-done.3.refs_6_ = bf16[4,3,96,128]{3,2,1,0:T(8,128)(2,1)S(1)} collective-permute-done((bf16[4,3,96,128]{3,2,1,0:T(8,128)(2,1)S(1)}, bf16[4,3,96,128]{3,2,1,0:T(8,128)(2,1)S(1)}, u32[]{:S(2)}, u32[]{:S(2)}) %collective-permute-start.3) | collective-permute-done | bytes 294944 | tf_op jit(solution)/shard_map/ppermute | solution.py:159
  26.4 0.0 collective-permute-start.5
  26.4 0.5 %collective-permute-start.1 = (bf16[3,256,128]{2,1,0:T(8,128)(2,1)S(1)}, bf16[3,256,128]{2,1,0:T(8,128)(2,1)S(1)}, u32[]{:S(2)}, u32[]{:S(2)}) collective-permute-start(bf16[3,256,128]{2,1,0:T(8,128)(2,1)S(1)} %get-tuple-element.7.refs_1_), channel_id=1, source_target_pairs={{0,1},{1,0},{2,3},{3,2},{4,5},{5,4},{6,7},{7,6},{8,9},{9,8},{10,11... | collective-permute-start | bytes 589832 | tf_op jit(solution)/shard_map/ppermute | solution.py:159
  26.9 1.6 %collective-permute-done.refs_2_ = bf16[3,256,128]{2,1,0:T(8,128)(2,1)S(1)} collective-permute-done((bf16[3,256,128]{2,1,0:T(8,128)(2,1)S(1)}, bf16[3,256,128]{2,1,0:T(8,128)(2,1)S(1)}, u32[]{:S(2)}, u32[]{:S(2)}) %collective-permute-start) | collective-permute-done | bytes 196640 | tf_op jit(solution)/shard_map/ppermute | solution.py:159
  28.5 0.0 collective-permute-start.2
  28.5 6.4 %load.1.refs_0_ = bf16[2,3,1024,1536]{3,2,1,0:T(8,128)(2,1)S(1)} custom-call(bf16[2,3,1024,1536]{3,2,1,0:T(8,128)(2,1)} %base_ref.1), custom_call_target="tpu_custom_call" | custom-call | bytes 18874368 | tf_op jit(solution)/shard_map/load/pallas_call | solution.py:70
  34.8 0.0 collective-permute-done.1.refs_3_
  34.9 0.0 collective-permute-done.2.refs_4_
  34.9 0.0 collective-permute-done.4.refs_7_
  34.9 0.0 collective-permute-done.5.refs_8_
  34.9 9.7 %merge.1 = bf16[2,3,1024,1536]{3,2,1,0:T(8,128)(2,1)} custom-call(bf16[2,3,1024,1536]{3,2,1,0:T(8,128)(2,1)S(1)} %load.1.refs_0_, bf16[3,256,128]{2,1,0:T(8,128)(2,1)S(1)} %get-tuple-element.7.refs_1_, bf16[3,256,128]{2,1,0:T(8,128)(2,1)S(1)} %collective-permute-done.refs_2_, bf16[3,256,128]{2,1,0:T(8,128)(2,1)S(1)} %collective-permute-done.1.refs_3_, ...), custom_call_target="tpu_custom_call" | custom-call | flops 1207959552 | bytes 37748736 | tf_op jit(solution)/shard_map/merge/pallas_call | solution.py:133
Async XLA Ops:
  17.5 8.8 %collective-permute-start.3 = (bf16[4,3,96,128]{3,2,1,0:T(8,128)(2,1)S(1)}, bf16[4,3,96,128]{3,2,1,0:T(8,128)(2,1)S(1)}, u32[]{:S(2)}, u32[]{:S(2)}) collective-permute-start(bf16[4,3,96,128]{3,2,1,0:T(8,128)(2,1)S(1)} %all_to_all.5.refs_5_), channel_id=1, source_target_pairs={{0,2},{1,3},{2,0},{3,1},{4,6},{5,7},{6,4},{7,5},{8,10},{9,11},{10,... | collective-permute-start | bytes 884744 | tf_op jit(solution)/shard_map/ppermute | solution.py:159
  19.0 9.4 %collective-permute-start = (bf16[3,256,128]{2,1,0:T(8,128)(2,1)S(1)}, bf16[3,256,128]{2,1,0:T(8,128)(2,1)S(1)}, u32[]{:S(2)}, u32[]{:S(2)}) collective-permute-start(bf16[3,256,128]{2,1,0:T(8,128)(2,1)S(1)} %get-tuple-element.7.refs_1_), channel_id=1, source_target_pairs={{0,2},{1,3},{2,0},{3,1},{4,6},{5,7},{6,4},{7,5},{8,10},{9,11},{10,... | collective-permute-start | bytes 589832 | tf_op jit(solution)/shard_map/ppermute | solution.py:159
  19.6 15.3 %collective-permute-start.4 = (bf16[4,3,96,128]{3,2,1,0:T(8,128)(2,1)S(1)}, bf16[4,3,96,128]{3,2,1,0:T(8,128)(2,1)S(1)}, u32[]{:S(2)}, u32[]{:S(2)}) collective-permute-start(bf16[4,3,96,128]{3,2,1,0:T(8,128)(2,1)S(1)} %all_to_all.5.refs_5_), channel_id=1, source_target_pairs={{0,1},{1,0},{2,3},{3,2},{4,5},{5,4},{6,7},{7,6},{8,9},{9,8},{10,11... | collective-permute-start | bytes 884744 | tf_op jit(solution)/shard_map/ppermute | solution.py:159
  26.4 8.5 %collective-permute-start.5 = (bf16[4,3,96,128]{3,2,1,0:T(8,128)(2,1)S(1)}, bf16[4,3,96,128]{3,2,1,0:T(8,128)(2,1)S(1)}, u32[]{:S(2)}, u32[]{:S(2)}) collective-permute-start(bf16[4,3,96,128]{3,2,1,0:T(8,128)(2,1)S(1)} %collective-permute-done.3.refs_6_), channel_id=1, source_target_pairs={{0,1},{1,0},{2,3},{3,2},{4,5},{5,4},{6,7},{7,6},{8,9},{9,8},{10,11... | collective-permute-start | bytes 884744 | tf_op jit(solution)/shard_map/ppermute | solution.py:159
  26.4 8.5 %collective-permute-start.1 = (bf16[3,256,128]{2,1,0:T(8,128)(2,1)S(1)}, bf16[3,256,128]{2,1,0:T(8,128)(2,1)S(1)}, u32[]{:S(2)}, u32[]{:S(2)}) collective-permute-start(bf16[3,256,128]{2,1,0:T(8,128)(2,1)S(1)} %get-tuple-element.7.refs_1_), channel_id=1, source_target_pairs={{0,1},{1,0},{2,3},{3,2},{4,5},{5,4},{6,7},{7,6},{8,9},{9,8},{10,11... | collective-permute-start | bytes 589832 | tf_op jit(solution)/shard_map/ppermute | solution.py:159
  28.5 6.4 %collective-permute-start.2 = (bf16[3,256,128]{2,1,0:T(8,128)(2,1)S(1)}, bf16[3,256,128]{2,1,0:T(8,128)(2,1)S(1)}, u32[]{:S(2)}, u32[]{:S(2)}) collective-permute-start(bf16[3,256,128]{2,1,0:T(8,128)(2,1)S(1)} %collective-permute-done.refs_2_), channel_id=1, source_target_pairs={{0,1},{1,0},{2,3},{3,2},{4,5},{5,4},{6,7},{7,6},{8,9},{9,8},{10,11... | collective-permute-start | bytes 589832 | tf_op jit(solution)/shard_map/ppermute | solution.py:159

commit v3 on v0

v3 whole, which is shorter than its diff:
```python
import functools

import jax
import jax.numpy as jnp
from jax import lax
from jax.experimental import pallas as pl
from jax.experimental.pallas import tpu as pltpu
from jax.sharding import PartitionSpec as P

adapter_scale = 0.5
out_slots = 3
in_vmem = pl.BlockSpec(memory_space=pltpu.VMEM)
in_hbm = pl.BlockSpec(memory_space=pltpu.HBM)
anywhere = pl.BlockSpec(memory_space=pl.ANY)
mib = 2**20


def select_kernel(index_ref, narrow_ref, wide_ref, both_out, w_out, index, n_buf, w_buf, index_sem, sems):
    experts = index_ref.shape[0]
    rank = narrow_ref.shape[2]
    rows = n_buf.shape[2]
    index_copy = pltpu.make_async_copy(index_ref, index, index_sem)
    index_copy.start()
    index_copy.wait()
    n_copies, w_copies = [], []
    for e in range(experts):
        i = index[e]
        ranks = pl.ds(e * rank, rank)
        w_copies.append(pltpu.make_async_copy(wide_ref.at[i], w_buf.at[:, ranks], sems.at[e, 1]))
        n_copies.append(pltpu.make_async_copy(narrow_ref.at[i], n_buf.at[:, ranks], sems.at[e, 0]))
    for copy in w_copies + n_copies:
        copy.start()
    for copy in w_copies:
        copy.wait()
    for p in range(w_buf.shape[0]):
        w = w_buf[p].astype(jnp.float32).T.astype(w_out.dtype)
        w_out[p] = w
        both_out[p, rows:] = w
    for copy in n_copies:
        copy.wait()
    for p in range(n_buf.shape[0]):
        n = n_buf[p].astype(jnp.float32) * adapter_scale
        both_out[p, :rows] = n.T.astype(both_out.dtype)


def select(narrow, wide, index):
    experts = index.shape[0]
    _, projections, rank, rows = narrow.shape
    columns = wide.shape[3]
    deep = experts * rank
    return pl.pallas_call(
        select_kernel,
        out_shape=(
            jax.ShapeDtypeStruct((projections, rows + columns, deep), narrow.dtype),
            jax.ShapeDtypeStruct((projections, columns, deep), wide.dtype),
        ),
        in_specs=[in_hbm] * 3,
        out_specs=[in_vmem] * 2,
        scratch_shapes=[
            pltpu.SMEM((experts,), index.dtype),
            pltpu.VMEM((projections, deep, rows), narrow.dtype),
            pltpu.VMEM((projections, deep, columns), wide.dtype),
            pltpu.SemaphoreType.DMA,
            pltpu.SemaphoreType.DMA((experts, 2)),
        ],
        compiler_params=pltpu.CompilerParams(vmem_limit_bytes=4 * mib),
        name="select",
    )(*[pltpu.with_memory_space_constraint(x, pltpu.HBM) for x in (index, narrow, wide)])


def load_kernel(base_ref, out_ref, sem):
    copy = pltpu.make_async_copy(base_ref, out_ref, sem)
    copy.start()
    copy.wait()


def load(base):
    return pl.pallas_call(
        load_kernel,
        out_shape=jax.ShapeDtypeStruct(base.shape, base.dtype),
        in_specs=[in_hbm],
        out_specs=in_vmem,
        scratch_shapes=[pltpu.SemaphoreType.DMA],
        compiler_params=pltpu.CompilerParams(vmem_limit_bytes=32 * mib),
        cost_estimate=pl.CostEstimate(flops=0, bytes_accessed=2 * base.size, transcendentals=0),
        name="load",
    )(base)


def pack_kernel(*refs):
    out_ref = refs[-1]
    for k in range(out_ref.shape[0]):
        out_ref[k] = refs[k][...]


def pack(blocks, after):
    block = blocks[0]
    return pl.pallas_call(
        pack_kernel,
        out_shape=jax.ShapeDtypeStruct((len(blocks),) + block.shape, block.dtype),
        in_specs=[in_vmem] * len(blocks) + [anywhere],
        out_specs=in_vmem,
        compiler_params=pltpu.CompilerParams(vmem_limit_bytes=4 * mib),
        name="pack",
    )(*blocks, after)


def merge_kernel(rank, n_pieces, w_pieces, base_ref, *refs):
    out_ref, n_all, w_rows, w_all, out_buf, sems = refs[-6:]
    experts, projections, width, wide_columns = base_ref.shape
    deep = n_all.shape[2]
    f_step = 256 if wide_columns % 256 == 0 else wide_columns
    m_step = 512 if width % 512 == 0 else width
    halves = width // m_step
    tiles = experts * halves
    s, g = lax.axis_index("shard"), lax.axis_index("group")
    lane_expert = lax.broadcasted_iota(jnp.int32, (m_step, deep), 1) // rank

    def out_copy(p, t):
        step = p * tiles + t
        rows = pl.ds(pl.multiple_of((t % halves) * m_step, m_step), m_step)
        slot = lax.rem(step, out_slots)
        return pltpu.make_async_copy(out_buf.at[slot], out_ref.at[t // halves, p, rows], sems.at[slot])

    for p in range(projections):
        for i, pick, first, count, place in n_pieces:
            at = pl.multiple_of(place(s, g) * count, count)
            n_all[p, pl.ds(at, count), :] = refs[i][pick + (p, pl.ds(first, count))]
        for i, pick, first, count, place in w_pieces:
            at = pl.multiple_of(place(s, g) * count, count)
            w_rows[p, pl.ds(at, count), :] = refs[i][pick + (p, pl.ds(first, count))]
        for f in range(0, wide_columns, f_step):
            w_all[p, :, f : f + f_step] = w_rows[p, f : f + f_step].T

        def tile(t, _):
            step = p * tiles + t
            e = t // halves
            rows = pl.ds(pl.multiple_of((t % halves) * m_step, m_step), m_step)
            slot = lax.rem(step, out_slots)

            @pl.when(step >= out_slots)
            def _():
                out_copy(p, t).wait()

            n = n_all[p, rows, :]
            n = jnp.where(lane_expert == e, n, jnp.zeros_like(n))
            for f in range(0, wide_columns, f_step):
                delta = jnp.dot(n, w_all[p, :, f : f + f_step], preferred_element_type=jnp.float32)
                b = base_ref[e, p, rows, f : f + f_step].astype(jnp.float32)
                out_buf[slot, :, f : f + f_step] = (b + delta).astype(out_buf.dtype)
            out_copy(p, t).start()
            return 0

        lax.fori_loop(0, tiles, tile, 0)
    for step in range(max(0, projections * tiles - out_slots), projections * tiles):
        out_copy(step // tiles, step % tiles).wait()


def merge(base, parts, n_pieces, w_pieces, rank):
    experts, projections, width, wide_columns = base.shape
    deep = parts[0].shape[-1]
    m_step = 512 if width % 512 == 0 else width
    return pl.pallas_call(
        functools.partial(merge_kernel, rank, n_pieces, w_pieces),
        out_shape=jax.ShapeDtypeStruct(base.shape, base.dtype),
        in_specs=[in_vmem] * (1 + len(parts)),
        out_specs=anywhere,
        scratch_shapes=[
            pltpu.VMEM((projections, width, deep), base.dtype),
            pltpu.VMEM((projections, wide_columns, deep), base.dtype),
            pltpu.VMEM((projections, deep, wide_columns), base.dtype),
            pltpu.VMEM((out_slots, m_step, wide_columns), base.dtype),
            pltpu.SemaphoreType.DMA((out_slots,)),
        ],
        compiler_params=pltpu.CompilerParams(vmem_limit_bytes=32 * mib),
        cost_estimate=pl.CostEstimate(
            flops=2 * base.size * rank, bytes_accessed=4 * base.size, transcendentals=0
        ),
        name="merge",
    )(base, *parts)


def on_device(shards, groups, base, narrow, wide, adapted_expert_index):
    rank = narrow.shape[3]
    rows, columns = narrow.shape[2], wide.shape[3]
    both, w = select(jnp.swapaxes(narrow, 2, 3), wide, adapted_expert_index)
    base = load(base)
    axes = ("shard", "group")

    if shards != 4 or groups != 4:
        n = lax.all_gather(both[:, :rows], "group", axis=1, tiled=True)
        w = lax.all_gather(w, axes, axis=1, tiled=True)
        whole = lambda s, g: 0
        n_pieces = [(0, (), 0, rows * groups, whole)]
        w_pieces = [(1, (), 0, columns * shards * groups, whole)]
        return merge(base, [n, w], n_pieces, w_pieces, rank)

    def swap(x, axis, bit):
        return lax.ppermute(x, axis, [(i, i ^ bit) for i in range(4)])

    line = pack([swap(w, "shard", k) for k in (1, 2, 3)], base)
    both_x = swap(both, "group", 2)
    line_x = swap(line, "group", 2)
    parts = [both, both_x, line, line_x]
    parts += [swap(x, "group", 1) for x in parts]
    n_pieces, w_pieces = [], []
    for i, m in ((0, 0), (1, 2), (4, 1), (5, 3)):
        n_pieces.append((i, (), 0, rows, lambda s, g, m=m: g ^ m))
        w_pieces.append((i, (), rows, columns, lambda s, g, m=m: s * groups + (g ^ m)))
        for k in (1, 2, 3):
            w_pieces.append((i + 2, (k - 1,), 0, columns, lambda s, g, m=m, k=k: (s ^ k) * groups + (g ^ m)))
    return merge(base, parts, n_pieces, w_pieces, rank)


def solution(mesh):
    return jax.shard_map(
        functools.partial(on_device, mesh.shape["shard"], mesh.shape["group"]),
        mesh=mesh,
        in_specs=(
            P("parts", None, "shard", None),
            P("parts", None, ("shard", "group"), None),
            P("parts", None, None, ("shard", "group")),
            P("parts"),
        ),
        out_specs=P("parts", None, "shard", None),
        check_vma=False,
    )
```

time: 80.9 us -> 32 us (0.40)
  waiting for transfers between devices: 34 us -> 6.76 us
  matrix products: 17.7 us -> 0 us
  Pallas kernels: 0 us -> 16.7 us
  between operations: 13.4 us -> 0.06 us
  blocking collectives: 10.5 us -> 0 us
  starting transfers between devices: 0.01 us -> 8.29 us
  local copies, waits for them, and re-layouts: 3.34 us -> 0 us
  other arithmetic: 1.79 us -> 0 us
    all_gather x1 -> x0, waiting for transfers between devices: 34 us -> none  [on_device(): lax.all_gather(chosen_wide, ('shard', 'group'), axis=3, tiled=True)]
    dot_general x1 -> x0, matrix products: 17.7 us -> none  [on_device(): jnp.einsum('epdr,eprf->epdf', local_slim_slice, lax.all_gather(chosen_wid...]
    pallas_call x0 -> x4, Pallas kernels: none -> 16.7 us  [the longest x1 8.5 us: merge(): pl.pallas_call(functools.partial(merge_kernel, rank, n_pieces, w_pieces),...]
    all_gather x1 -> x0, blocking collectives: 10.5 us -> none  [on_device(): lax.all_gather(chosen_narrow, 'group', axis=2, tiled=True)]
    ppermute x0 -> x9, starting transfers between devices: none -> 8.29 us  [swap(): return lax.ppermute(x, axis, [(i, i ^ bit) for i in range(4)])]
    ppermute x0 -> x9, waiting for transfers between devices: none -> 6.76 us  [swap(): return lax.ppermute(x, axis, [(i, i ^ bit) for i in range(4)])]
    gather x2 -> x0, local copies, waits for them, and re-layouts: 2.53 us -> none  [the longest x1 1.97 us: on_device(): chosen_wide = jnp.take(wide, adapted_expert_index, axis=0)]
    select_n x3 -> x0, other arithmetic: 0.97 us -> none  [the longest x2 0.89 us: on_device(): chosen_narrow = jnp.take(narrow, adapted_expert_index, axis=0)]
  transfers between devices with their start and end apart: 1 -> 9, of which waited for: 1 -> 2; matrix products, arithmetic and copies ran while one was open for 1% -> 0% of each run, Pallas kernels for 0% -> 20%
where the time goes in v3:
time: 32 us; the launch traced here: 31.8 us
  Pallas kernels  16.7 us (52%)
  starting transfers between devices  8.29 us (26%)
  waiting for transfers between devices  6.76 us (21%)
    pallas_call x1, Pallas kernels, merge(): pl.pallas_call(functools.partial(merge_kernel, rank, n_pieces, w_pieces),...  8.5 us
    ppermute x9, starting transfers between devices, swap(): return lax.ppermute(x, axis, [(i, i ^ bit) for i in range(4)])  8.29 us
    ppermute x9, waiting for transfers between devices, swap(): return lax.ppermute(x, axis, [(i, i ^ bit) for i in range(4)])  6.76 us
    pallas_call x1, Pallas kernels, load(): pl.pallas_call(load_kernel, out_shape=jax.ShapeDtypeStruct(base.shape, ba...  6.37 us
    pallas_call x1, Pallas kernels, select(): pl.pallas_call(select_kernel, out_shape=(jax.ShapeDtypeStruct((projection...  1.84 us
  transfers between devices with their start and end apart: 9, of which 2 were waited for; matrix products, arithmetic and copies ran while one was open for 0% of the time, Pallas kernels for 20%

profile of v3, /device:TPU:0, one launch (start us, length us, event | category | flops | bytes accessed | tf_op | source)
XLA Modules:
  0.0 31.8 jit_solution(4048257778677923975)
XLA Ops:
  0.0 1.8 %select.1 = (bf16[3,352,128]{2,1,0:T(8,128)(2,1)S(1)}, bf16[3,96,128]{2,1,0:T(8,128)(2,1)S(1)}) custom-call(s32[2]{0:T(128)} %index_ref.1, bf16[32,3,64,256]{3,2,1,0:T(8,128)(2,1)} %bitcast.1, bf16[32,3,64,96]{3,2,1,0:T(8,128)(2,1)} %wide_ref.1), custom_call_target="tpu_custom_call" | custom-call | tf_op jit(solution)/shard_map/select/pallas_call | solution.py:51
  1.9 3.0 %collective-permute-start = (bf16[3,352,128]{2,1,0:T(8,128)(2,1)S(1)}, bf16[3,352,128]{2,1,0:T(8,128)(2,1)S(1)}, u32[]{:S(2)}, u32[]{:S(2)}) collective-permute-start(bf16[3,352,128]{2,1,0:T(8,128)(2,1)S(1)} %get-tuple-element.7.refs_0_), channel_id=1, source_target_pairs={{0,2},{1,3},{2,0},{3,1},{4,6},{5,7},{6,4},{7,5},{8,10},{9,11},{10,... | collective-permute-start | bytes 811016 | tf_op jit(solution)/shard_map/ppermute | solution.py:199
  4.9 3.6 %collective-permute-start.3 = (bf16[3,96,128]{2,1,0:T(8,128)(2,1)S(1)}, bf16[3,96,128]{2,1,0:T(8,128)(2,1)S(1)}, u32[]{:S(2)}, u32[]{:S(2)}) collective-permute-start(bf16[3,96,128]{2,1,0:T(8,128)(2,1)S(1)} %get-tuple-element.8), channel_id=1, source_target_pairs={{0,12},{4,8},{8,4},{12,0},{1,13},{5,9},{9,5},{13,1},{2,14},{6,10},... | collective-permute-start | bytes 221192 | tf_op jit(solution)/shard_map/ppermute | solution.py:199
  8.5 0.0 collective-permute-start.2
  8.5 0.8 %collective-permute-start.1 = (bf16[3,96,128]{2,1,0:T(8,128)(2,1)S(1)}, bf16[3,96,128]{2,1,0:T(8,128)(2,1)S(1)}, u32[]{:S(2)}, u32[]{:S(2)}) collective-permute-start(bf16[3,96,128]{2,1,0:T(8,128)(2,1)S(1)} %get-tuple-element.8), channel_id=1, source_target_pairs={{0,4},{4,0},{8,12},{12,8},{1,5},{5,1},{9,13},{13,9},{2,6},{6,2},{1... | collective-permute-start | bytes 221192 | tf_op jit(solution)/shard_map/ppermute | solution.py:199
  9.2 6.4 %load.1.refs_3_.base_ref = bf16[2,3,1024,1536]{3,2,1,0:T(8,128)(2,1)S(1)} custom-call(bf16[2,3,1024,1536]{3,2,1,0:T(8,128)(2,1)} %base_ref.1), custom_call_target="tpu_custom_call" | custom-call | bytes 18874368 | tf_op jit(solution)/shard_map/load/pallas_call | solution.py:78
  15.6 0.0 collective-permute-done.3.refs_2_
  15.6 0.0 collective-permute-done.2.refs_1_
  15.6 0.0 collective-permute-done.1.refs_0_
  15.7 0.4 %collective-permute-start.4 = (bf16[3,3,96,128]{3,2,1,0:T(8,128)(2,1)S(1)}, bf16[3,3,96,128]{3,2,1,0:T(8,128)(2,1)S(1)}, u32[]{:S(2)}, u32[]{:S(2)}) collective-permute-start(bf16[3,3,96,128]{3,2,1,0:T(8,128)(2,1)S(1)} %pack.1.refs_2_), channel_id=1, source_target_pairs={{0,2},{1,3},{2,0},{3,1},{4,6},{5,7},{6,4},{7,5},{8,10},{9,11},{10,... | collective-permute-start | bytes 663560 | tf_op jit(solution)/shard_map/ppermute | solution.py:199
  16.1 0.0 collective-permute-start.5
  16.1 0.0 collective-permute-done.refs_1_
  16.1 0.5 %collective-permute-start.6 = (bf16[3,352,128]{2,1,0:T(8,128)(2,1)S(1)}, bf16[3,352,128]{2,1,0:T(8,128)(2,1)S(1)}, u32[]{:S(2)}, u32[]{:S(2)}) collective-permute-start(bf16[3,352,128]{2,1,0:T(8,128)(2,1)S(1)} %collective-permute-done.refs_1_), channel_id=1, source_target_pairs={{0,1},{1,0},{2,3},{3,2},{4,5},{5,4},{6,7},{7,6},{8,9},{9,8},{10,11... | collective-permute-start | bytes 811016 | tf_op jit(solution)/shard_map/ppermute | solution.py:199
  16.6 0.0 collective-permute-start.7
  16.6 5.3 %collective-permute-done.4.refs_3_ = bf16[3,3,96,128]{3,2,1,0:T(8,128)(2,1)S(1)} collective-permute-done((bf16[3,3,96,128]{3,2,1,0:T(8,128)(2,1)S(1)}, bf16[3,3,96,128]{3,2,1,0:T(8,128)(2,1)S(1)}, u32[]{:S(2)}, u32[]{:S(2)}) %collective-permute-start.4) | collective-permute-done | bytes 221216 | tf_op jit(solution)/shard_map/ppermute | solution.py:199
  21.9 0.0 collective-permute-start.8
  21.9 0.0 collective-permute-done.5.refs_4_
  21.9 0.0 collective-permute-done.7.refs_6_
  21.9 1.5 %collective-permute-done.8.refs_7_ = bf16[3,3,96,128]{3,2,1,0:T(8,128)(2,1)S(1)} collective-permute-done((bf16[3,3,96,128]{3,2,1,0:T(8,128)(2,1)S(1)}, bf16[3,3,96,128]{3,2,1,0:T(8,128)(2,1)S(1)}, u32[]{:S(2)}, u32[]{:S(2)}) %collective-permute-start.8) | collective-permute-done | bytes 221216 | tf_op jit(solution)/shard_map/ppermute | solution.py:199
  23.3 0.0 collective-permute-done.6.refs_5_
  23.3 8.5 %merge.1 = bf16[2,3,1024,1536]{3,2,1,0:T(8,128)(2,1)} custom-call(bf16[2,3,1024,1536]{3,2,1,0:T(8,128)(2,1)S(1)} %load.1.refs_3_.base_ref, bf16[3,352,128]{2,1,0:T(8,128)(2,1)S(1)} %get-tuple-element.7.refs_0_, bf16[3,352,128]{2,1,0:T(8,128)(2,1)S(1)} %collective-permute-done.refs_1_, bf16[3,3,96,128]{3,2,1,0:T(8,128)(2,1)S(1)} %pack.1.refs_2_, ...), custom_call_target="tpu_custom_call" | custom-call | flops 1207959552 | bytes 37748736 | tf_op jit(solution)/shard_map/merge/pallas_call | solution.py:163
  (1 shorter events, 0.0 us)
Async XLA Ops:
  1.9 14.2 %collective-permute-start = (bf16[3,352,128]{2,1,0:T(8,128)(2,1)S(1)}, bf16[3,352,128]{2,1,0:T(8,128)(2,1)S(1)}, u32[]{:S(2)}, u32[]{:S(2)}) collective-permute-start(bf16[3,352,128]{2,1,0:T(8,128)(2,1)S(1)} %get-tuple-element.7.refs_0_), channel_id=1, source_target_pairs={{0,2},{1,3},{2,0},{3,1},{4,6},{5,7},{6,4},{7,5},{8,10},{9,11},{10,... | collective-permute-start | bytes 811016 | tf_op jit(solution)/shard_map/ppermute | solution.py:199
  4.9 10.8 %collective-permute-start.3 = (bf16[3,96,128]{2,1,0:T(8,128)(2,1)S(1)}, bf16[3,96,128]{2,1,0:T(8,128)(2,1)S(1)}, u32[]{:S(2)}, u32[]{:S(2)}) collective-permute-start(bf16[3,96,128]{2,1,0:T(8,128)(2,1)S(1)} %get-tuple-element.8), channel_id=1, source_target_pairs={{0,12},{4,8},{8,4},{12,0},{1,13},{5,9},{9,5},{13,1},{2,14},{6,10},... | collective-permute-start | bytes 221192 | tf_op jit(solution)/shard_map/ppermute | solution.py:199
  8.5 7.2 %collective-permute-start.2 = (bf16[3,96,128]{2,1,0:T(8,128)(2,1)S(1)}, bf16[3,96,128]{2,1,0:T(8,128)(2,1)S(1)}, u32[]{:S(2)}, u32[]{:S(2)}) collective-permute-start(bf16[3,96,128]{2,1,0:T(8,128)(2,1)S(1)} %get-tuple-element.8), channel_id=1, source_target_pairs={{0,8},{4,12},{8,0},{12,4},{1,9},{5,13},{9,1},{13,5},{2,10},{6,14},... | collective-permute-start | bytes 221192 | tf_op jit(solution)/shard_map/ppermute | solution.py:199
  8.5 7.2 %collective-permute-start.1 = (bf16[3,96,128]{2,1,0:T(8,128)(2,1)S(1)}, bf16[3,96,128]{2,1,0:T(8,128)(2,1)S(1)}, u32[]{:S(2)}, u32[]{:S(2)}) collective-permute-start(bf16[3,96,128]{2,1,0:T(8,128)(2,1)S(1)} %get-tuple-element.8), channel_id=1, source_target_pairs={{0,4},{4,0},{8,12},{12,8},{1,5},{5,1},{9,13},{13,9},{2,6},{6,2},{1... | collective-permute-start | bytes 221192 | tf_op jit(solution)/shard_map/ppermute | solution.py:199
  15.7 6.2 %collective-permute-start.4 = (bf16[3,3,96,128]{3,2,1,0:T(8,128)(2,1)S(1)}, bf16[3,3,96,128]{3,2,1,0:T(8,128)(2,1)S(1)}, u32[]{:S(2)}, u32[]{:S(2)}) collective-permute-start(bf16[3,3,96,128]{3,2,1,0:T(8,128)(2,1)S(1)} %pack.1.refs_2_), channel_id=1, source_target_pairs={{0,2},{1,3},{2,0},{3,1},{4,6},{5,7},{6,4},{7,5},{8,10},{9,11},{10,... | collective-permute-start | bytes 663560 | tf_op jit(solution)/shard_map/ppermute | solution.py:199
  16.1 5.8 %collective-permute-start.5 = (bf16[3,352,128]{2,1,0:T(8,128)(2,1)S(1)}, bf16[3,352,128]{2,1,0:T(8,128)(2,1)S(1)}, u32[]{:S(2)}, u32[]{:S(2)}) collective-permute-start(bf16[3,352,128]{2,1,0:T(8,128)(2,1)S(1)} %get-tuple-element.7.refs_0_), channel_id=1, source_target_pairs={{0,1},{1,0},{2,3},{3,2},{4,5},{5,4},{6,7},{7,6},{8,9},{9,8},{10,11... | collective-permute-start | bytes 811016 | tf_op jit(solution)/shard_map/ppermute | solution.py:199
  16.1 7.3 %collective-permute-start.6 = (bf16[3,352,128]{2,1,0:T(8,128)(2,1)S(1)}, bf16[3,352,128]{2,1,0:T(8,128)(2,1)S(1)}, u32[]{:S(2)}, u32[]{:S(2)}) collective-permute-start(bf16[3,352,128]{2,1,0:T(8,128)(2,1)S(1)} %collective-permute-done.refs_1_), channel_id=1, source_target_pairs={{0,1},{1,0},{2,3},{3,2},{4,5},{5,4},{6,7},{7,6},{8,9},{9,8},{10,11... | collective-permute-start | bytes 811016 | tf_op jit(solution)/shard_map/ppermute | solution.py:199
  16.6 5.3 %collective-permute-start.7 = (bf16[3,3,96,128]{3,2,1,0:T(8,128)(2,1)S(1)}, bf16[3,3,96,128]{3,2,1,0:T(8,128)(2,1)S(1)}, u32[]{:S(2)}, u32[]{:S(2)}) collective-permute-start(bf16[3,3,96,128]{3,2,1,0:T(8,128)(2,1)S(1)} %pack.1.refs_2_), channel_id=1, source_target_pairs={{0,1},{1,0},{2,3},{3,2},{4,5},{5,4},{6,7},{7,6},{8,9},{9,8},{10,11... | collective-permute-start | bytes 663560 | tf_op jit(solution)/shard_map/ppermute | solution.py:199
  21.9 1.5 %collective-permute-start.8 = (bf16[3,3,96,128]{3,2,1,0:T(8,128)(2,1)S(1)}, bf16[3,3,96,128]{3,2,1,0:T(8,128)(2,1)S(1)}, u32[]{:S(2)}, u32[]{:S(2)}) collective-permute-start(bf16[3,3,96,128]{3,2,1,0:T(8,128)(2,1)S(1)} %collective-permute-done.4.refs_3_), channel_id=1, source_target_pairs={{0,1},{1,0},{2,3},{3,2},{4,5},{5,4},{6,7},{7,6},{8,9},{9,8},{10,11... | collective-permute-start | bytes 663560 | tf_op jit(solution)/shard_map/ppermute | solution.py:199

commit v4 on v0

v4 whole, which is shorter than its diff:
```python
import functools
import typing

import jax
import jax.numpy as jnp
from jax import lax
from jax.experimental import pallas as pl
from jax.experimental.pallas import tpu as pltpu
from jax.sharding import PartitionSpec as P

adapter_scale = 0.5
out_slots = 6
tile_rows = 256
in_vmem = pl.BlockSpec(memory_space=pltpu.VMEM)
in_hbm = pl.BlockSpec(memory_space=pltpu.HBM)
anywhere = pl.BlockSpec(memory_space=pl.ANY)
vmem_limit = 24 * 2**20


def select_kernel(index_ref, narrow_ref, wide_ref, both_out, w_out, index, n_buf, w_buf, index_sem, sems):
    experts = index_ref.shape[0]
    rank = narrow_ref.shape[2]
    rows = n_buf.shape[2]
    index_copy = pltpu.make_async_copy(index_ref, index, index_sem)
    index_copy.start()
    index_copy.wait()
    n_copies, w_copies = [], []
    for e in range(experts):
        i = index[e]
        ranks = pl.ds(e * rank, rank)
        w_copies.append(pltpu.make_async_copy(wide_ref.at[i], w_buf.at[:, ranks], sems.at[e, 1]))
        n_copies.append(pltpu.make_async_copy(narrow_ref.at[i], n_buf.at[:, ranks], sems.at[e, 0]))
    for copy in w_copies + n_copies:
        copy.start()
    for copy in w_copies:
        copy.wait()
    for p in range(w_buf.shape[0]):
        w = w_buf[p].astype(jnp.float32).T.astype(w_out.dtype)
        w_out[p] = w
        both_out[p, rows:] = w
    for copy in n_copies:
        copy.wait()
    for p in range(n_buf.shape[0]):
        n = n_buf[p].astype(jnp.float32) * adapter_scale
        both_out[p, :rows] = n.T.astype(both_out.dtype)


def select(narrow, wide, index):
    experts = index.shape[0]
    _, projections, rank, rows = narrow.shape
    columns = wide.shape[3]
    deep = experts * rank
    return pl.pallas_call(
        select_kernel,
        out_shape=(
            jax.ShapeDtypeStruct((projections, rows + columns, deep), narrow.dtype),
            jax.ShapeDtypeStruct((projections, columns, deep), wide.dtype),
        ),
        in_specs=[in_hbm] * 3,
        out_specs=[in_vmem] * 2,
        scratch_shapes=[
            pltpu.SMEM((experts,), index.dtype),
            pltpu.VMEM((projections, deep, rows), narrow.dtype),
            pltpu.VMEM((projections, deep, columns), wide.dtype),
            pltpu.SemaphoreType.DMA,
            pltpu.SemaphoreType.DMA((experts, 2)),
        ],
        compiler_params=pltpu.CompilerParams(vmem_limit_bytes=vmem_limit),
        name="select",
    )(*[pltpu.with_memory_space_constraint(x, pltpu.HBM) for x in (index, narrow, wide)])


def pack_kernel(count, *refs):
    out_ref = refs[-1]
    at = 0
    for ref in refs[:count]:
        rows = ref.shape[1]
        out_ref[:, at : at + rows] = ref[...]
        at += rows


def pack(blocks, after=()):
    projections, _, deep = blocks[0].shape
    rows = sum(x.shape[1] for x in blocks)
    return pl.pallas_call(
        functools.partial(pack_kernel, len(blocks)),
        out_shape=jax.ShapeDtypeStruct((projections, rows, deep), blocks[0].dtype),
        in_specs=[in_vmem] * len(blocks) + [anywhere] * len(after),
        out_specs=in_vmem,
        compiler_params=pltpu.CompilerParams(vmem_limit_bytes=vmem_limit),
        name="pack",
    )(*blocks, *after)


def merge_kernel(plan, count, base_ref, *refs):
    out_ref, token, n_all, w_rows, w_all, out_buf, sems = refs[-7:]
    experts, _, width, _ = base_ref.shape
    deep, span = w_all.shape
    m_step = out_buf.shape[1]
    f_step = 256 if span % 256 == 0 else span
    strips = width // m_step
    tiles = experts * strips
    s, g = lax.axis_index("shard"), lax.axis_index("group")
    lane_expert = lax.broadcasted_iota(jnp.int32, (m_step, deep), 1) // plan.rank
    first_column = pl.multiple_of(plan.chunk(s) * span, span)

    def out_copy(p, step):
        t = lax.rem(step, tiles)
        rows = pl.ds(pl.multiple_of((t % strips) * m_step, m_step), m_step)
        slot = lax.rem(step, out_slots)
        place = out_ref.at[t // strips, p, rows, pl.ds(first_column, span)]
        return pltpu.make_async_copy(out_buf.at[slot], place, sems.at[slot])

    for done, p in enumerate(plan.projections):
        for i, first, rows, place in plan.n_pieces:
            at = pl.multiple_of(place(s, g) * rows, rows)
            n_all[pl.ds(at, rows), :] = refs[i][p, pl.ds(first, rows)]
        for i, first, rows, place in plan.w_pieces:
            at = pl.multiple_of(place(s, g) * rows, rows)
            w_rows[pl.ds(at, rows), :] = refs[i][p, pl.ds(first, rows)]
        for f in range(0, span, f_step):
            w_all[:, f : f + f_step] = w_rows[f : f + f_step].T

        def tile(step, _):
            t = lax.rem(step, tiles)
            e = t // strips
            rows = pl.ds(pl.multiple_of((t % strips) * m_step, m_step), m_step)
            slot = lax.rem(step, out_slots)

            @pl.when(step >= out_slots)
            def _():
                out_copy(p, step).wait()

            n = n_all[rows, :]
            n = jnp.where(lane_expert == e, n, jnp.zeros_like(n))
            for f in range(0, span, f_step):
                delta = jnp.dot(n, w_all[:, f : f + f_step], preferred_element_type=jnp.float32)
                b = base_ref[e, p, rows, pl.ds(first_column + f, f_step)].astype(jnp.float32)
                out_buf[slot, :, f : f + f_step] = (b + delta).astype(out_buf.dtype)
            out_copy(p, step).start()
            return 0

        lax.fori_loop(done * tiles, (done + 1) * tiles, tile, 0)
    steps = len(plan.projections) * tiles
    for step in range(max(0, steps - out_slots), steps):
        out_copy(plan.projections[-1], step).wait()
    token[...] = jnp.zeros_like(token)


class Plan(typing.NamedTuple):
    rank: int
    projections: tuple
    span: int
    chunk: typing.Callable
    n_pieces: list
    w_pieces: list


def merge(plan, base, parts, out=None, after=()):
    experts, projections, width, _ = base.shape
    deep = parts[0].shape[-1]
    m_step = tile_rows if width % tile_rows == 0 else width
    operands = [base, *parts, *after] + ([] if out is None else [out])
    share = len(plan.projections) * plan.span * experts * width
    return pl.pallas_call(
        functools.partial(merge_kernel, plan, len(parts)),
        out_shape=(jax.ShapeDtypeStruct(base.shape, base.dtype), jax.ShapeDtypeStruct((8, 128), jnp.float32)),
        in_specs=[in_vmem] * (1 + len(parts)) + [anywhere] * (len(operands) - 1 - len(parts)),
        out_specs=(in_hbm, in_vmem),
        scratch_shapes=[
            pltpu.VMEM((width, deep), base.dtype),
            pltpu.VMEM((plan.span, deep), base.dtype),
            pltpu.VMEM((deep, plan.span), base.dtype),
            pltpu.VMEM((out_slots, m_step, plan.span), base.dtype),
            pltpu.SemaphoreType.DMA((out_slots,)),
        ],
        input_output_aliases={} if out is None else {len(operands) - 1: 0},
        compiler_params=pltpu.CompilerParams(vmem_limit_bytes=vmem_limit),
        cost_estimate=pl.CostEstimate(flops=2 * share * plan.rank, bytes_accessed=4 * share, transcendentals=0),
        name="merge",
    )(*operands)


def on_device(shards, groups, base, narrow, wide, adapted_expert_index):
    rank = narrow.shape[3]
    rows, columns = narrow.shape[2], wide.shape[3]
    projections = tuple(range(base.shape[1]))
    both, w = select(jnp.swapaxes(narrow, 2, 3), wide, adapted_expert_index)
    axes = ("shard", "group")

    if shards != 4 or groups != 4:
        n = lax.all_gather(both[:, :rows], "group", axis=1, tiled=True)
        w = lax.all_gather(w, axes, axis=1, tiled=True)
        whole = lambda s, g: 0
        plan = Plan(
            rank,
            projections,
            columns * shards * groups,
            lambda s: 0,
            [(0, 0, rows * groups, whole)],
            [(1, 0, columns * shards * groups, whole)],
        )
        return merge(plan, base, [n, w])[0]

    def swap(x, axis, bit):
        return lax.ppermute(x, axis, [(i, i ^ bit) for i in range(4)])

    base = swap(base, "group", 0)
    w3, w2, w1 = [swap(w, "shard", k) for k in (3, 2, 1)]
    line = pack([w2, w3])
    own_a = pack([both, swap(both, "group", 2), w1, swap(w1, "group", 2)], (line,))
    other_a = swap(own_a, "group", 1)
    line_x = swap(line, "group", 2)
    half = rows + columns
    n_pieces = [
        (i, first, rows, lambda s, g, m=m: g ^ m)
        for i, first, m in ((0, 0, 0), (0, half, 2), (1, 0, 1), (1, half, 3))
    ]

    def w_piece(i, first, k, m):
        return (i, first, columns, lambda s, g: ((s ^ k) % 2) * groups + (g ^ m))

    near, far = [], []
    for i, m in ((0, 0), (1, 1)):
        near += [w_piece(i, rows, 0, m), w_piece(i, half + rows, 0, m ^ 2)]
        near += [w_piece(i, 2 * half, 1, m), w_piece(i, 2 * half + columns, 1, m ^ 2)]
        for at, k in ((0, 2), (1, 3)):
            far += [w_piece(i + 2, at * columns, k, m), w_piece(i + 2, (at + 2) * columns, k, m ^ 2)]
    span = 2 * columns * groups
    near_plan = Plan(rank, projections, span, lambda s: s // 2, n_pieces, near)
    far_plan = Plan(rank, projections, span, lambda s: 1 - s // 2, n_pieces, far)
    parts = [own_a, other_a]
    out, token = merge(near_plan._replace(projections=projections[:2]), base, parts, after=(line,))
    own_b = pack([line, line_x], (token,))
    other_b = swap(own_b, "group", 1)
    out, _ = merge(near_plan._replace(projections=projections[2:]), base, parts, out, after=(own_b,))
    return merge(far_plan, base, parts + [own_b, other_b], out)[0]


def solution(mesh):
    return jax.shard_map(
        functools.partial(on_device, mesh.shape["shard"], mesh.shape["group"]),
        mesh=mesh,
        in_specs=(
            P("parts", None, "shard", None),
            P("parts", None, ("shard", "group"), None),
            P("parts", None, None, ("shard", "group")),
            P("parts"),
        ),
        out_specs=P("parts", None, "shard", None),
        check_vma=False,
    )
```

time: 80.9 us -> 41.4 us (0.51)
  waiting for transfers between devices: 34 us -> 7.9 us
  Pallas kernels: 0 us -> 18.4 us
  matrix products: 17.7 us -> 0 us
  starting transfers between devices: 0.01 us -> 14.8 us
  between operations: 13.4 us -> 0.09 us
  blocking collectives: 10.5 us -> 0 us
  local copies, waits for them, and re-layouts: 3.34 us -> 0 us
  other arithmetic: 1.79 us -> 0 us
    all_gather x1 -> x0, waiting for transfers between devices: 34 us -> none  [on_device(): lax.all_gather(chosen_wide, ('shard', 'group'), axis=3, tiled=True)]
    pallas_call x0 -> x7, Pallas kernels: none -> 18.4 us  [the longest x3 16.5 us: merge(): pl.pallas_call(functools.partial(merge_kernel, plan, len(parts)), out_sha...]
    dot_general x1 -> x0, matrix products: 17.7 us -> none  [on_device(): jnp.einsum('epdr,eprf->epdf', local_slim_slice, lax.all_gather(chosen_wid...]
    ppermute x0 -> x9, starting transfers between devices: none -> 14.8 us  [swap(): return lax.ppermute(x, axis, [(i, i ^ bit) for i in range(4)])]
    all_gather x1 -> x0, blocking collectives: 10.5 us -> none  [on_device(): lax.all_gather(chosen_narrow, 'group', axis=2, tiled=True)]
    ppermute x0 -> x9, waiting for transfers between devices: none -> 7.9 us  [swap(): return lax.ppermute(x, axis, [(i, i ^ bit) for i in range(4)])]
    gather x2 -> x0, local copies, waits for them, and re-layouts: 2.53 us -> none  [the longest x1 1.97 us: on_device(): chosen_wide = jnp.take(wide, adapted_expert_index, axis=0)]
    select_n x3 -> x0, other arithmetic: 0.97 us -> none  [the longest x2 0.89 us: on_device(): chosen_narrow = jnp.take(narrow, adapted_expert_index, axis=0)]
  transfers between devices with their start and end apart: 1 -> 9, of which waited for: 1 -> 4; matrix products, arithmetic and copies ran while one was open for 1% -> 0% of each run, Pallas kernels for 0% -> 26%
where the time goes in v4:
time: 41.4 us; the launch traced here: 41.2 us
  Pallas kernels  18.4 us (44%)
  starting transfers between devices  14.8 us (36%)
  waiting for transfers between devices  7.9 us (19%)
    pallas_call x3, Pallas kernels, merge(): pl.pallas_call(functools.partial(merge_kernel, plan, len(parts)), out_sha...  16.5 us
    ppermute x9, starting transfers between devices, swap(): return lax.ppermute(x, axis, [(i, i ^ bit) for i in range(4)])  14.8 us
    ppermute x9, waiting for transfers between devices, swap(): return lax.ppermute(x, axis, [(i, i ^ bit) for i in range(4)])  7.9 us
    pallas_call x1, Pallas kernels, select(): pl.pallas_call(select_kernel, out_shape=(jax.ShapeDtypeStruct((projection...  1.84 us
  transfers between devices with their start and end apart: 9, of which 4 were waited for; matrix products, arithmetic and copies ran while one was open for 0% of the time, Pallas kernels for 26%

profile of v4, /device:TPU:0, one launch (start us, length us, event | category | flops | bytes accessed | tf_op | source)
XLA Modules:
  0.0 41.2 jit_solution(2195879017128799318)
XLA Ops:
  0.0 6.4 %collective-permute-start = (bf16[2,3,1024,1536]{3,2,1,0:T(8,128)(2,1)}, bf16[2,3,1024,1536]{3,2,1,0:T(8,128)(2,1)S(1)}, u32[]{:S(2)}, u32[]{:S(2)}) collective-permute-start(bf16[2,3,1024,1536]{3,2,1,0:T(8,128)(2,1)} %param.4), channel_id=1, source_target_pairs={{0,0},{1,1},{2,2},{3,3},{4,4},{5,5},{6,6},{7,7},{8,8},{9,9},{10,10... | collective-permute-start | bytes 56623112 | tf_op jit(solution)/shard_map/ppermute | solution.py:206
  6.4 1.8 %select.1 = (bf16[3,352,128]{2,1,0:T(8,128)(2,1)S(1)}, bf16[3,96,128]{2,1,0:T(8,128)(2,1)S(1)}) custom-call(s32[2]{0:T(128)} %index_ref.1, bf16[32,3,64,256]{3,2,1,0:T(8,128)(2,1)} %bitcast.1, bf16[32,3,64,96]{3,2,1,0:T(8,128)(2,1)} %wide_ref.1), custom_call_target="tpu_custom_call" | custom-call | tf_op jit(solution)/shard_map/select/pallas_call | solution.py:53
  8.2 3.0 %collective-permute-start.1 = (bf16[3,352,128]{2,1,0:T(8,128)(2,1)S(1)}, bf16[3,352,128]{2,1,0:T(8,128)(2,1)S(1)}, u32[]{:S(2)}, u32[]{:S(2)}) collective-permute-start(bf16[3,352,128]{2,1,0:T(8,128)(2,1)S(1)} %get-tuple-element.11.refs_0_), channel_id=1, source_target_pairs={{0,2},{1,3},{2,0},{3,1},{4,6},{5,7},{6,4},{7,5},{8,10},{9,11},{10,... | collective-permute-start | bytes 811016 | tf_op jit(solution)/shard_map/ppermute | solution.py:206
  11.2 1.6 %collective-permute-start.2 = (bf16[3,96,128]{2,1,0:T(8,128)(2,1)S(1)}, bf16[3,96,128]{2,1,0:T(8,128)(2,1)S(1)}, u32[]{:S(2)}, u32[]{:S(2)}) collective-permute-start(bf16[3,96,128]{2,1,0:T(8,128)(2,1)S(1)} %get-tuple-element.12), channel_id=1, source_target_pairs={{0,4},{4,0},{8,12},{12,8},{1,5},{5,1},{9,13},{13,9},{2,6},{6,2},{1... | collective-permute-start | bytes 221192 | tf_op jit(solution)/shard_map/ppermute | solution.py:206
  12.8 2.5 %collective-permute-start.5 = (bf16[3,96,128]{2,1,0:T(8,128)(2,1)S(1)}, bf16[3,96,128]{2,1,0:T(8,128)(2,1)S(1)}, u32[]{:S(2)}, u32[]{:S(2)}) collective-permute-start(bf16[3,96,128]{2,1,0:T(8,128)(2,1)S(1)} %get-tuple-element.12), channel_id=1, source_target_pairs={{0,12},{4,8},{8,4},{12,0},{1,13},{5,9},{9,5},{13,1},{2,14},{6,10},... | collective-permute-start | bytes 221192 | tf_op jit(solution)/shard_map/ppermute | solution.py:206
  15.3 0.1 collective-permute-start.4
  15.4 0.2 collective-permute-done.2.refs_2_
  15.6 0.4 collective-permute-start.3
  15.9 3.8 %collective-permute-done.5.refs_1_ = bf16[3,96,128]{2,1,0:T(8,128)(2,1)S(1)} collective-permute-done((bf16[3,96,128]{2,1,0:T(8,128)(2,1)S(1)}, bf16[3,96,128]{2,1,0:T(8,128)(2,1)S(1)}, u32[]{:S(2)}, u32[]{:S(2)}) %collective-permute-start.5) | collective-permute-done | bytes 73760 | tf_op jit(solution)/shard_map/ppermute | solution.py:206
  19.7 2.4 %collective-permute-done.4.refs_0_ = bf16[3,96,128]{2,1,0:T(8,128)(2,1)S(1)} collective-permute-done((bf16[3,96,128]{2,1,0:T(8,128)(2,1)S(1)}, bf16[3,96,128]{2,1,0:T(8,128)(2,1)S(1)}, u32[]{:S(2)}, u32[]{:S(2)}) %collective-permute-start.4) | collective-permute-done | bytes 73760 | tf_op jit(solution)/shard_map/ppermute | solution.py:206
  22.1 0.0 collective-permute-done.3.refs_3_
  22.1 0.0 collective-permute-done.1.refs_1_
  22.2 0.1 collective-permute-start.6
  22.3 0.6 %collective-permute-start.7 = (bf16[3,192,128]{2,1,0:T(8,128)(2,1)S(1)}, bf16[3,192,128]{2,1,0:T(8,128)(2,1)S(1)}, u32[]{:S(2)}, u32[]{:S(2)}) collective-permute-start(bf16[3,192,128]{2,1,0:T(8,128)(2,1)S(1)} %pack.3.refs_4_.refs_2_.refs_0_), channel_id=1, source_target_pairs={{0,2},{1,3},{2,0},{3,1},{4,6},{5,7},{6,4},{7,5},{8,10},{9,11},{10,... | collective-permute-start | bytes 442376 | tf_op jit(solution)/shard_map/ppermute | solution.py:206
  22.9 1.5 %collective-permute-done.6.refs_1_ = bf16[3,896,128]{2,1,0:T(8,128)(2,1)S(1)} collective-permute-done((bf16[3,896,128]{2,1,0:T(8,128)(2,1)S(1)}, bf16[3,896,128]{2,1,0:T(8,128)(2,1)S(1)}, u32[]{:S(2)}, u32[]{:S(2)}) %collective-permute-start.6) | collective-permute-done | bytes 688160 | tf_op jit(solution)/shard_map/ppermute | solution.py:206
  24.4 0.0 collective-permute-done.base_ref
  24.4 5.1 %merge.3 = (bf16[2,3,1024,1536]{3,2,1,0:T(8,128)(2,1)}, f32[8,128]{1,0:T(8,128)S(1)}) custom-call(bf16[2,3,1024,1536]{3,2,1,0:T(8,128)(2,1)S(1)} %collective-permute-done.base_ref, bf16[3,896,128]{2,1,0:T(8,128)(2,1)S(1)} %pack.4.refs_0_, bf16[3,896,128]{2,1,0:T(8,128)(2,1)S(1)} %collective-permute-done.6.refs_1_, ...), custom_call_target="tpu_custom_call" | custom-call | flops 402653184 | bytes 12582912 | tf_op jit(solution)/shard_map/merge/pallas_call | solution.py:165
  29.5 0.0 collective-permute-done.7.refs_1_
  29.6 0.2 collective-permute-start.8
  29.8 3.6 %merge.4 = (bf16[2,3,1024,1536]{3,2,1,0:T(8,128)(2,1)}, f32[8,128]{1,0:T(8,128)}) custom-call(bf16[2,3,1024,1536]{3,2,1,0:T(8,128)(2,1)S(1)} %collective-permute-done.base_ref, bf16[3,896,128]{2,1,0:T(8,128)(2,1)S(1)} %pack.4.refs_0_, bf16[3,896,128]{2,1,0:T(8,128)(2,1)S(1)} %collective-permute-done.6.refs_1_, ...), custom_call_target="tpu_custom_call", output_to_operand_aliasing={{0}: (4, {})} | custom-call | flops 201326592 | bytes 6291456 | tf_op jit(solution)/shard_map/merge/pallas_call | solution.py:165
  33.3 0.0 collective-permute-done.8.refs_3_
  33.3 7.8 %merge.5 = (bf16[2,3,1024,1536]{3,2,1,0:T(8,128)(2,1)}, f32[8,128]{1,0:T(8,128)}) custom-call(bf16[2,3,1024,1536]{3,2,1,0:T(8,128)(2,1)S(1)} %collective-permute-done.base_ref, bf16[3,896,128]{2,1,0:T(8,128)(2,1)S(1)} %pack.4.refs_0_, bf16[3,896,128]{2,1,0:T(8,128)(2,1)S(1)} %collective-permute-done.6.refs_1_, ...), custom_call_target="tpu_custom_call", output_to_operand_aliasing={{0}: (5, {})} | custom-call | flops 603979776 | bytes 18874368 | tf_op jit(solution)/shard_map/merge/pallas_call | solution.py:165
  (3 shorter events, 0.1 us)
Async XLA Ops:
  0.0 24.4 %collective-permute-start = (bf16[2,3,1024,1536]{3,2,1,0:T(8,128)(2,1)}, bf16[2,3,1024,1536]{3,2,1,0:T(8,128)(2,1)S(1)}, u32[]{:S(2)}, u32[]{:S(2)}) collective-permute-start(bf16[2,3,1024,1536]{3,2,1,0:T(8,128)(2,1)} %param.4), channel_id=1, source_target_pairs={{0,0},{1,1},{2,2},{3,3},{4,4},{5,5},{6,6},{7,7},{8,8},{9,9},{10,10... | collective-permute-start | bytes 56623112 | tf_op jit(solution)/shard_map/ppermute | solution.py:206
  8.2 13.9 %collective-permute-start.1 = (bf16[3,352,128]{2,1,0:T(8,128)(2,1)S(1)}, bf16[3,352,128]{2,1,0:T(8,128)(2,1)S(1)}, u32[]{:S(2)}, u32[]{:S(2)}) collective-permute-start(bf16[3,352,128]{2,1,0:T(8,128)(2,1)S(1)} %get-tuple-element.11.refs_0_), channel_id=1, source_target_pairs={{0,2},{1,3},{2,0},{3,1},{4,6},{5,7},{6,4},{7,5},{8,10},{9,11},{10,... | collective-permute-start | bytes 811016 | tf_op jit(solution)/shard_map/ppermute | solution.py:206
  11.2 4.4 %collective-permute-start.2 = (bf16[3,96,128]{2,1,0:T(8,128)(2,1)S(1)}, bf16[3,96,128]{2,1,0:T(8,128)(2,1)S(1)}, u32[]{:S(2)}, u32[]{:S(2)}) collective-permute-start(bf16[3,96,128]{2,1,0:T(8,128)(2,1)S(1)} %get-tuple-element.12), channel_id=1, source_target_pairs={{0,4},{4,0},{8,12},{12,8},{1,5},{5,1},{9,13},{13,9},{2,6},{6,2},{1... | collective-permute-start | bytes 221192 | tf_op jit(solution)/shard_map/ppermute | solution.py:206
  12.8 6.9 %collective-permute-start.5 = (bf16[3,96,128]{2,1,0:T(8,128)(2,1)S(1)}, bf16[3,96,128]{2,1,0:T(8,128)(2,1)S(1)}, u32[]{:S(2)}, u32[]{:S(2)}) collective-permute-start(bf16[3,96,128]{2,1,0:T(8,128)(2,1)S(1)} %get-tuple-element.12), channel_id=1, source_target_pairs={{0,12},{4,8},{8,4},{12,0},{1,13},{5,9},{9,5},{13,1},{2,14},{6,10},... | collective-permute-start | bytes 221192 | tf_op jit(solution)/shard_map/ppermute | solution.py:206
  15.3 6.8 %collective-permute-start.4 = (bf16[3,96,128]{2,1,0:T(8,128)(2,1)S(1)}, bf16[3,96,128]{2,1,0:T(8,128)(2,1)S(1)}, u32[]{:S(2)}, u32[]{:S(2)}) collective-permute-start(bf16[3,96,128]{2,1,0:T(8,128)(2,1)S(1)} %get-tuple-element.12), channel_id=1, source_target_pairs={{0,8},{4,12},{8,0},{12,4},{1,9},{5,13},{9,1},{13,5},{2,10},{6,14},... | collective-permute-start | bytes 221192 | tf_op jit(solution)/shard_map/ppermute | solution.py:206
  15.6 6.5 %collective-permute-start.3 = (bf16[3,96,128]{2,1,0:T(8,128)(2,1)S(1)}, bf16[3,96,128]{2,1,0:T(8,128)(2,1)S(1)}, u32[]{:S(2)}, u32[]{:S(2)}) collective-permute-start(bf16[3,96,128]{2,1,0:T(8,128)(2,1)S(1)} %collective-permute-done.2.refs_2_), channel_id=1, source_target_pairs={{0,2},{1,3},{2,0},{3,1},{4,6},{5,7},{6,4},{7,5},{8,10},{9,11},{10,... | collective-permute-start | bytes 221192 | tf_op jit(solution)/shard_map/ppermute | solution.py:206
  22.2 2.2 %collective-permute-start.6 = (bf16[3,896,128]{2,1,0:T(8,128)(2,1)S(1)}, bf16[3,896,128]{2,1,0:T(8,128)(2,1)S(1)}, u32[]{:S(2)}, u32[]{:S(2)}) collective-permute-start(bf16[3,896,128]{2,1,0:T(8,128)(2,1)S(1)} %pack.4.refs_0_), channel_id=1, source_target_pairs={{0,1},{1,0},{2,3},{3,2},{4,5},{5,4},{6,7},{7,6},{8,9},{9,8},{10,11... | collective-permute-start | bytes 2064392 | tf_op jit(solution)/shard_map/ppermute | solution.py:206
  22.3 7.2 %collective-permute-start.7 = (bf16[3,192,128]{2,1,0:T(8,128)(2,1)S(1)}, bf16[3,192,128]{2,1,0:T(8,128)(2,1)S(1)}, u32[]{:S(2)}, u32[]{:S(2)}) collective-permute-start(bf16[3,192,128]{2,1,0:T(8,128)(2,1)S(1)} %pack.3.refs_4_.refs_2_.refs_0_), channel_id=1, source_target_pairs={{0,2},{1,3},{2,0},{3,1},{4,6},{5,7},{6,4},{7,5},{8,10},{9,11},{10,... | collective-permute-start | bytes 442376 | tf_op jit(solution)/shard_map/ppermute | solution.py:206
  29.6 3.8 %collective-permute-start.8 = (bf16[3,384,128]{2,1,0:T(8,128)(2,1)S(1)}, bf16[3,384,128]{2,1,0:T(8,128)(2,1)S(1)}, u32[]{:S(2)}, u32[]{:S(2)}) collective-permute-start(bf16[3,384,128]{2,1,0:T(8,128)(2,1)S(1)} %pack.5.refs_2_), channel_id=1, source_target_pairs={{0,1},{1,0},{2,3},{3,2},{4,5},{5,4},{6,7},{7,6},{8,9},{9,8},{10,11... | collective-permute-start | bytes 884744 | tf_op jit(solution)/shard_map/ppermute | solution.py:206

commit v5 on v4

--- a/solution.py
+++ b/solution.py
@@ -1,4 +1,5 @@
 import functools
+import math
 import typing
 
 import jax
@@ -9,8 +10,8 @@
 from jax.sharding import PartitionSpec as P
 
 adapter_scale = 0.5
-out_slots = 6
-tile_rows = 256
+out_slots = 3
+tile_rows = 512
 in_vmem = pl.BlockSpec(memory_space=pltpu.VMEM)
 in_hbm = pl.BlockSpec(memory_space=pltpu.HBM)
 anywhere = pl.BlockSpec(memory_space=pl.ANY)
@@ -70,6 +71,26 @@
     )(*[pltpu.with_memory_space_constraint(x, pltpu.HBM) for x in (index, narrow, wide)])
 
 
+def load_kernel(loaded, base_ref, _, out_ref, sem):
+    copy = pltpu.make_async_copy(base_ref.at[:, pl.ds(0, loaded)], out_ref, sem)
+    copy.start()
+    copy.wait()
+
+
+def load(base, loaded, after):
+    shape = base.shape[:1] + (loaded,) + base.shape[2:]
+    return pl.pallas_call(
+        functools.partial(load_kernel, loaded),
+        out_shape=jax.ShapeDtypeStruct(shape, base.dtype),
+        in_specs=[in_hbm, anywhere],
+        out_specs=in_vmem,
+        scratch_shapes=[pltpu.SemaphoreType.DMA],
+        compiler_params=pltpu.CompilerParams(vmem_limit_bytes=vmem_limit),
+        cost_estimate=pl.CostEstimate(flops=0, bytes_accessed=2 * math.prod(shape), transcendentals=0),
+        name="load",
+    )(base, after)
+
+
 def pack_kernel(count, *refs):
     out_ref = refs[-1]
     at = 0
@@ -92,8 +113,13 @@
     )(*blocks, *after)
 
 
-def merge_kernel(plan, count, base_ref, *refs):
-    out_ref, token, n_all, w_rows, w_all, out_buf, sems = refs[-7:]
+def merge_kernel(plan, has_loaded, base_ref, *refs):
+    if has_loaded:
+        loaded_ref, refs = refs[0], refs[1:]
+        loaded = loaded_ref.shape[1]
+    else:
+        loaded = 0
+    out_ref, token, n_all, w_rows, w_all, out_buf, sems, late_buf, late_sems = refs[-9:]
     experts, _, width, _ = base_ref.shape
     deep, span = w_all.shape
     m_step = out_buf.shape[1]
@@ -102,48 +128,64 @@
     tiles = experts * strips
     s, g = lax.axis_index("shard"), lax.axis_index("group")
     lane_expert = lax.broadcasted_iota(jnp.int32, (m_step, deep), 1) // plan.rank
-    first_column = pl.multiple_of(plan.chunk(s) * span, span)
-
-    def out_copy(p, step):
-        t = lax.rem(step, tiles)
-        rows = pl.ds(pl.multiple_of((t % strips) * m_step, m_step), m_step)
-        slot = lax.rem(step, out_slots)
-        place = out_ref.at[t // strips, p, rows, pl.ds(first_column, span)]
-        return pltpu.make_async_copy(out_buf.at[slot], place, sems.at[slot])
-
-    for done, p in enumerate(plan.projections):
-        for i, first, rows, place in plan.n_pieces:
-            at = pl.multiple_of(place(s, g) * rows, rows)
-            n_all[pl.ds(at, rows), :] = refs[i][p, pl.ds(first, rows)]
-        for i, first, rows, place in plan.w_pieces:
-            at = pl.multiple_of(place(s, g) * rows, rows)
-            w_rows[pl.ds(at, rows), :] = refs[i][p, pl.ds(first, rows)]
-        for f in range(0, span, f_step):
-            w_all[:, f : f + f_step] = w_rows[f : f + f_step].T
-
-        def tile(step, _):
+    late = [p for p in plan.projections if p >= loaded]
+
+    def merge_chunk(first_column):
+        columns = pl.ds(first_column, span)
+
+        def late_copy(p):
+            at = p - late[0]
+            return pltpu.make_async_copy(base_ref.at[:, p, :, columns], late_buf.at[at], late_sems.at[at])
+
+        def out_copy(p, step):
             t = lax.rem(step, tiles)
-            e = t // strips
             rows = pl.ds(pl.multiple_of((t % strips) * m_step, m_step), m_step)
             slot = lax.rem(step, out_slots)
-
-            @pl.when(step >= out_slots)
-            def _():
-                out_copy(p, step).wait()
-
-            n = n_all[rows, :]
-            n = jnp.where(lane_expert == e, n, jnp.zeros_like(n))
+            return pltpu.make_async_copy(out_buf.at[slot], out_ref.at[t // strips, p, rows, columns], sems.at[slot])
+
+        for p in late:
+            late_copy(p).start()
+        for done, p in enumerate(plan.projections):
+            for i, first, rows, place in plan.n_pieces:
+                at = pl.multiple_of(place(s, g) * rows, rows)
+                n_all[pl.ds(at, rows), :] = refs[i][p, pl.ds(first, rows)]
+            for i, first, rows, place in plan.w_pieces:
+                at = pl.multiple_of(place(s, g) * rows, rows)
+                w_rows[pl.ds(at, rows), :] = refs[i][p, pl.ds(first, rows)]
             for f in range(0, span, f_step):
-                delta = jnp.dot(n, w_all[:, f : f + f_step], preferred_element_type=jnp.float32)
-                b = base_ref[e, p, rows, pl.ds(first_column + f, f_step)].astype(jnp.float32)
-                out_buf[slot, :, f : f + f_step] = (b + delta).astype(out_buf.dtype)
-            out_copy(p, step).start()
-            return 0
-
-        lax.fori_loop(done * tiles, (done + 1) * tiles, tile, 0)
-    steps = len(plan.projections) * tiles
-    for step in range(max(0, steps - out_slots), steps):
-        out_copy(plan.projections[-1], step).wait()
+                w_all[:, f : f + f_step] = w_rows[f : f + f_step].T
+            if p in late:
+                late_copy(p).wait()
+
+            def tile(step, _):
+                t = lax.rem(step, tiles)
+                e = t // strips
+                rows = pl.ds(pl.multiple_of((t % strips) * m_step, m_step), m_step)
+                slot = lax.rem(step, out_slots)
+
+                @pl.when(step >= out_slots)
+                def _():
+                    out_copy(p, step).wait()
+
+                n = n_all[rows, :]
+                n = jnp.where(lane_expert == e, n, jnp.zeros_like(n))
+                for f in range(0, span, f_step):
+                    delta = jnp.dot(n, w_all[:, f : f + f_step], preferred_element_type=jnp.float32)
+                    if p in late:
+                        b = late_buf[p - late[0], e, rows, f : f + f_step]
+                    else:
+                        b = loaded_ref[e, p, rows, first_column + f : first_column + f + f_step]
+                    out_buf[slot, :, f : f + f_step] = (b.astype(jnp.float32) + delta).astype(out_buf.dtype)
+                out_copy(p, step).start()
+                return 0
+
+            lax.fori_loop(done * tiles, (done + 1) * tiles, tile, 0)
+        steps = len(plan.projections) * tiles
+        for step in range(max(0, steps - out_slots), steps):
+            out_copy(plan.projections[-1], step).wait()
+
+    for c in range(plan.chunks):
+        pl.when(plan.chunk(s) == c)(functools.partial(merge_chunk, c * span))
     token[...] = jnp.zeros_like(token)
 
 
@@ -151,21 +193,25 @@
     rank: int
     projections: tuple
     span: int
+    chunks: int
     chunk: typing.Callable
     n_pieces: list
     w_pieces: list
 
 
-def merge(plan, base, parts, out=None, after=()):
-    experts, projections, width, _ = base.shape
+def merge(plan, base, parts, loaded=None, out=None, after=()):
+    experts, _, width, _ = base.shape
     deep = parts[0].shape[-1]
     m_step = tile_rows if width % tile_rows == 0 else width
-    operands = [base, *parts, *after] + ([] if out is None else [out])
     share = len(plan.projections) * plan.span * experts * width
+    in_place = [] if loaded is None else [loaded]
+    late = len([p for p in plan.projections if loaded is None or p >= loaded.shape[1]])
+    extra = [*after] + ([] if out is None else [out])
+    operands = [pltpu.with_memory_space_constraint(base, pltpu.HBM), *in_place, *parts, *extra]
     return pl.pallas_call(
-        functools.partial(merge_kernel, plan, len(parts)),
+        functools.partial(merge_kernel, plan, loaded is not None),
         out_shape=(jax.ShapeDtypeStruct(base.shape, base.dtype), jax.ShapeDtypeStruct((8, 128), jnp.float32)),
-        in_specs=[in_vmem] * (1 + len(parts)) + [anywhere] * (len(operands) - 1 - len(parts)),
+        in_specs=[in_hbm] + [in_vmem] * len(in_place + parts) + [anywhere] * len(extra),
         out_specs=(in_hbm, in_vmem),
         scratch_shapes=[
             pltpu.VMEM((width, deep), base.dtype),
@@ -173,6 +219,8 @@
             pltpu.VMEM((deep, plan.span), base.dtype),
             pltpu.VMEM((out_slots, m_step, plan.span), base.dtype),
             pltpu.SemaphoreType.DMA((out_slots,)),
+            pltpu.VMEM((max(late, 1), experts, width if late else 16, plan.span), base.dtype),
+            pltpu.SemaphoreType.DMA((max(late, 1),)),
         ],
         input_output_aliases={} if out is None else {len(operands) - 1: 0},
         compiler_params=pltpu.CompilerParams(vmem_limit_bytes=vmem_limit),
@@ -196,6 +244,7 @@
             rank,
             projections,
             columns * shards * groups,
+            1,
             lambda s: 0,
             [(0, 0, rows * groups, whole)],
             [(1, 0, columns * shards * groups, whole)],
@@ -205,10 +254,11 @@
     def swap(x, axis, bit):
         return lax.ppermute(x, axis, [(i, i ^ bit) for i in range(4)])
 
-    base = swap(base, "group", 0)
-    w3, w2, w1 = [swap(w, "shard", k) for k in (3, 2, 1)]
-    line = pack([w2, w3])
-    own_a = pack([both, swap(both, "group", 2), w1, swap(w1, "group", 2)], (line,))
+    w1 = swap(w, "shard", 1)
+    pair = pack([w, w1])
+    line = swap(pair, "shard", 2)
+    loaded = load(base, len(projections), pair)
+    own_a = pack([both, swap(both, "group", 2), w1, swap(w1, "group", 2)], (loaded, line))
     other_a = swap(own_a, "group", 1)
     line_x = swap(line, "group", 2)
     half = rows + columns
@@ -227,14 +277,14 @@
         for at, k in ((0, 2), (1, 3)):
             far += [w_piece(i + 2, at * columns, k, m), w_piece(i + 2, (at + 2) * columns, k, m ^ 2)]
     span = 2 * columns * groups
-    near_plan = Plan(rank, projections, span, lambda s: s // 2, n_pieces, near)
-    far_plan = Plan(rank, projections, span, lambda s: 1 - s // 2, n_pieces, far)
+    near_plan = Plan(rank, projections, span, 2, lambda s: s // 2, n_pieces, near)
+    far_plan = Plan(rank, projections, span, 2, lambda s: 1 - s // 2, n_pieces, far)
     parts = [own_a, other_a]
-    out, token = merge(near_plan._replace(projections=projections[:2]), base, parts, after=(line,))
+    out, token = merge(near_plan._replace(projections=projections[:2]), base, parts, loaded, after=(line,))
     own_b = pack([line, line_x], (token,))
     other_b = swap(own_b, "group", 1)
-    out, _ = merge(near_plan._replace(projections=projections[2:]), base, parts, out, after=(own_b,))
-    return merge(far_plan, base, parts + [own_b, other_b], out)[0]
+    out, _ = merge(near_plan._replace(projections=projections[2:]), base, parts, loaded, out, after=(own_b,))
+    return merge(far_plan, base, parts + [own_b, other_b], loaded, out)[0]
 
 
 def solution(mesh):

time: 41.4 us -> 35.8 us (0.86)
  starting transfers between devices: 14.8 us -> 9.6 us
  waiting for transfers between devices: 7.9 us -> 3.36 us
  Pallas kernels: 18.4 us -> 22.5 us
    ppermute x9 -> x7, starting transfers between devices: 14.8 us -> 9.6 us  [swap(): return lax.ppermute(x, axis, [(i, i ^ bit) for i in range(4)])]
    ppermute x9 -> x7, waiting for transfers between devices: 7.9 us -> 3.36 us  [swap(): return lax.ppermute(x, axis, [(i, i ^ bit) for i in range(4)])]
    pallas_call x3 -> x4, Pallas kernels: 16.5 us -> 20.6 us  [the longest x3 14.2 us: merge(): pl.pallas_call(functools.partial(merge_kernel, plan, loaded is not None),...]
  transfers between devices with their start and end apart: 9 -> 7, of which waited for: 4 -> 2; matrix products, arithmetic and copies ran while one was open for 0% -> 0% of each run, Pallas kernels for 26% -> 39%
where the time goes in v5:
time: 35.8 us; the launch traced here: 35.6 us
  Pallas kernels  22.5 us (63%)
  starting transfers between devices  9.6 us (27%)
  waiting for transfers between devices  3.36 us (9%)
    pallas_call x3, Pallas kernels, merge(): pl.pallas_call(functools.partial(merge_kernel, plan, loaded is not None),...  14.2 us
    ppermute x7, starting transfers between devices, swap(): return lax.ppermute(x, axis, [(i, i ^ bit) for i in range(4)])  9.6 us
    pallas_call x1, Pallas kernels, load(): pl.pallas_call(functools.partial(load_kernel, loaded), out_shape=jax.Shap...  6.37 us
    ppermute x7, waiting for transfers between devices, swap(): return lax.ppermute(x, axis, [(i, i ^ bit) for i in range(4)])  3.36 us
    pallas_call x1, Pallas kernels, select(): pl.pallas_call(select_kernel, out_shape=(jax.ShapeDtypeStruct((projection...  1.84 us
  transfers between devices with their start and end apart: 7, of which 2 were waited for; matrix products, arithmetic and copies ran while one was open for 0% of the time, Pallas kernels for 39%

profile of v5, /device:TPU:0, one launch (start us, length us, event | category | flops | bytes accessed | tf_op | source)
XLA Modules:
  0.0 35.6 jit_solution(7391095062600078191)
XLA Ops:
  0.0 1.8 %select.1 = (bf16[3,352,128]{2,1,0:T(8,128)(2,1)S(1)}, bf16[3,96,128]{2,1,0:T(8,128)(2,1)S(1)}) custom-call(s32[2]{0:T(128)} %index_ref.1, bf16[32,3,64,256]{3,2,1,0:T(8,128)(2,1)} %bitcast.1, bf16[32,3,64,96]{3,2,1,0:T(8,128)(2,1)} %wide_ref.1), custom_call_target="tpu_custom_call" | custom-call | tf_op jit(solution)/shard_map/select/pallas_call | solution.py:54
  1.9 3.0 %collective-permute-start.1 = (bf16[3,352,128]{2,1,0:T(8,128)(2,1)S(1)}, bf16[3,352,128]{2,1,0:T(8,128)(2,1)S(1)}, u32[]{:S(2)}, u32[]{:S(2)}) collective-permute-start(bf16[3,352,128]{2,1,0:T(8,128)(2,1)S(1)} %get-tuple-element.12.refs_0_), channel_id=1, source_target_pairs={{0,2},{1,3},{2,0},{3,1},{4,6},{5,7},{6,4},{7,5},{8,10},{9,11},{10,... | collective-permute-start | bytes 811016 | tf_op jit(solution)/shard_map/ppermute | solution.py:255
  4.9 1.6 %collective-permute-start = (bf16[3,96,128]{2,1,0:T(8,128)(2,1)S(1)}, bf16[3,96,128]{2,1,0:T(8,128)(2,1)S(1)}, u32[]{:S(2)}, u32[]{:S(2)}) collective-permute-start(bf16[3,96,128]{2,1,0:T(8,128)(2,1)S(1)} %get-tuple-element.11.refs_0_), channel_id=1, source_target_pairs={{0,4},{4,0},{8,12},{12,8},{1,5},{5,1},{9,13},{13,9},{2,6},{6,2},{1... | collective-permute-start | bytes 221192 | tf_op jit(solution)/shard_map/ppermute | solution.py:255
  6.4 2.8 %collective-permute-done.refs_1_.refs_2_ = bf16[3,96,128]{2,1,0:T(8,128)(2,1)S(1)} collective-permute-done((bf16[3,96,128]{2,1,0:T(8,128)(2,1)S(1)}, bf16[3,96,128]{2,1,0:T(8,128)(2,1)S(1)}, u32[]{:S(2)}, u32[]{:S(2)}) %collective-permute-start) | collective-permute-done | bytes 73760 | tf_op jit(solution)/shard_map/ppermute | solution.py:255
  9.2 2.7 %collective-permute-start.3 = (bf16[3,192,128]{2,1,0:T(8,128)(2,1)S(1)}, bf16[3,192,128]{2,1,0:T(8,128)(2,1)S(1)}, u32[]{:S(2)}, u32[]{:S(2)}) collective-permute-start(bf16[3,192,128]{2,1,0:T(8,128)(2,1)S(1)} %pack.3._), channel_id=1, source_target_pairs={{0,8},{4,12},{8,0},{12,4},{1,9},{5,13},{9,1},{13,5},{2,10},{6,14},... | collective-permute-start | bytes 442376 | tf_op jit(solution)/shard_map/ppermute | solution.py:255
  11.9 0.5 %collective-permute-start.2 = (bf16[3,96,128]{2,1,0:T(8,128)(2,1)S(1)}, bf16[3,96,128]{2,1,0:T(8,128)(2,1)S(1)}, u32[]{:S(2)}, u32[]{:S(2)}) collective-permute-start(bf16[3,96,128]{2,1,0:T(8,128)(2,1)S(1)} %collective-permute-done.refs_1_.refs_2_), channel_id=1, source_target_pairs={{0,2},{1,3},{2,0},{3,1},{4,6},{5,7},{6,4},{7,5},{8,10},{9,11},{10,... | collective-permute-start | bytes 221192 | tf_op jit(solution)/shard_map/ppermute | solution.py:255
  12.4 6.4 %load.1.refs_4_.refs_0_ = bf16[2,3,1024,1536]{3,2,1,0:T(8,128)(2,1)S(1)} custom-call(bf16[2,3,1024,1536]{3,2,1,0:T(8,128)(2,1)} %base_ref.7, bf16[3,192,128]{2,1,0:T(8,128)(2,1)S(1)} %pack.3._), custom_call_target="tpu_custom_call" | custom-call | bytes 18874368 | tf_op jit(solution)/shard_map/load/pallas_call | solution.py:82
  18.8 0.0 collective-permute-done.2.refs_3_
  18.8 0.0 collective-permute-done.3.refs_5_.refs_3_.refs_0_
  18.8 0.0 collective-permute-done.1.refs_1_
  18.9 0.1 collective-permute-start.4
  19.0 1.6 %collective-permute-start.5 = (bf16[3,192,128]{2,1,0:T(8,128)(2,1)S(1)}, bf16[3,192,128]{2,1,0:T(8,128)(2,1)S(1)}, u32[]{:S(2)}, u32[]{:S(2)}) collective-permute-start(bf16[3,192,128]{2,1,0:T(8,128)(2,1)S(1)} %collective-permute-done.3.refs_5_.refs_3_.refs_0_), channel_id=1, source_target_pairs={{0,2},{1,3},{2,0},{3,1},{4,6},{5,7},{6,4},{7,5},{8,10},{9,11},{10,... | collective-permute-start | bytes 442376 | tf_op jit(solution)/shard_map/ppermute | solution.py:255
  20.5 0.6 %collective-permute-done.4.refs_2_ = bf16[3,896,128]{2,1,0:T(8,128)(2,1)S(1)} collective-permute-done((bf16[3,896,128]{2,1,0:T(8,128)(2,1)S(1)}, bf16[3,896,128]{2,1,0:T(8,128)(2,1)S(1)}, u32[]{:S(2)}, u32[]{:S(2)}) %collective-permute-start.4) | collective-permute-done | bytes 688160 | tf_op jit(solution)/shard_map/ppermute | solution.py:255
  21.1 4.3 %merge.3 = (bf16[2,3,1024,1536]{3,2,1,0:T(8,128)(2,1)}, f32[8,128]{1,0:T(8,128)S(1)}) custom-call(bf16[2,3,1024,1536]{3,2,1,0:T(8,128)(2,1)} %base_ref.7, bf16[2,3,1024,1536]{3,2,1,0:T(8,128)(2,1)S(1)} %load.1.refs_4_.refs_0_, bf16[3,896,128]{2,1,0:T(8,128)(2,1)S(1)} %pack.4.refs_1_, bf16[3,896,128]{2,1,0:T(8,128)(2,1)S(1)} %collective-permute-done.4.refs_2_, ...), custom_call_target="tpu_custom_call" | custom-call | flops 402653184 | bytes 12582912 | tf_op jit(solution)/shard_map/merge/pallas_call | solution.py:211
  25.4 0.0 collective-permute-done.5.refs_1_
  25.5 0.2 collective-permute-start.6
  25.7 3.2 %merge.4 = (bf16[2,3,1024,1536]{3,2,1,0:T(8,128)(2,1)}, f32[8,128]{1,0:T(8,128)}) custom-call(bf16[2,3,1024,1536]{3,2,1,0:T(8,128)(2,1)} %base_ref.7, bf16[2,3,1024,1536]{3,2,1,0:T(8,128)(2,1)S(1)} %load.1.refs_4_.refs_0_, bf16[3,896,128]{2,1,0:T(8,128)(2,1)S(1)} %pack.4.refs_1_, ...), custom_call_target="tpu_custom_call", output_to_operand_aliasing={{0}: (5, {})} | custom-call | flops 201326592 | bytes 6291456 | tf_op jit(solution)/shard_map/merge/pallas_call | solution.py:211
  28.9 0.0 collective-permute-done.6.refs_4_
  28.9 6.7 %merge.5 = (bf16[2,3,1024,1536]{3,2,1,0:T(8,128)(2,1)}, f32[8,128]{1,0:T(8,128)}) custom-call(bf16[2,3,1024,1536]{3,2,1,0:T(8,128)(2,1)} %base_ref.7, bf16[2,3,1024,1536]{3,2,1,0:T(8,128)(2,1)S(1)} %load.1.refs_4_.refs_0_, bf16[3,896,128]{2,1,0:T(8,128)(2,1)S(1)} %pack.4.refs_1_, ...), custom_call_target="tpu_custom_call", output_to_operand_aliasing={{0}: (6, {})} | custom-call | flops 603979776 | bytes 18874368 | tf_op jit(solution)/shard_map/merge/pallas_call | solution.py:211
  (3 shorter events, 0.1 us)
Async XLA Ops:
  1.9 17.0 %collective-permute-start.1 = (bf16[3,352,128]{2,1,0:T(8,128)(2,1)S(1)}, bf16[3,352,128]{2,1,0:T(8,128)(2,1)S(1)}, u32[]{:S(2)}, u32[]{:S(2)}) collective-permute-start(bf16[3,352,128]{2,1,0:T(8,128)(2,1)S(1)} %get-tuple-element.12.refs_0_), channel_id=1, source_target_pairs={{0,2},{1,3},{2,0},{3,1},{4,6},{5,7},{6,4},{7,5},{8,10},{9,11},{10,... | collective-permute-start | bytes 811016 | tf_op jit(solution)/shard_map/ppermute | solution.py:255
  4.9 4.4 %collective-permute-start = (bf16[3,96,128]{2,1,0:T(8,128)(2,1)S(1)}, bf16[3,96,128]{2,1,0:T(8,128)(2,1)S(1)}, u32[]{:S(2)}, u32[]{:S(2)}) collective-permute-start(bf16[3,96,128]{2,1,0:T(8,128)(2,1)S(1)} %get-tuple-element.11.refs_0_), channel_id=1, source_target_pairs={{0,4},{4,0},{8,12},{12,8},{1,5},{5,1},{9,13},{13,9},{2,6},{6,2},{1... | collective-permute-start | bytes 221192 | tf_op jit(solution)/shard_map/ppermute | solution.py:255
  9.2 9.6 %collective-permute-start.3 = (bf16[3,192,128]{2,1,0:T(8,128)(2,1)S(1)}, bf16[3,192,128]{2,1,0:T(8,128)(2,1)S(1)}, u32[]{:S(2)}, u32[]{:S(2)}) collective-permute-start(bf16[3,192,128]{2,1,0:T(8,128)(2,1)S(1)} %pack.3._), channel_id=1, source_target_pairs={{0,8},{4,12},{8,0},{12,4},{1,9},{5,13},{9,1},{13,5},{2,10},{6,14},... | collective-permute-start | bytes 442376 | tf_op jit(solution)/shard_map/ppermute | solution.py:255
  11.9 6.9 %collective-permute-start.2 = (bf16[3,96,128]{2,1,0:T(8,128)(2,1)S(1)}, bf16[3,96,128]{2,1,0:T(8,128)(2,1)S(1)}, u32[]{:S(2)}, u32[]{:S(2)}) collective-permute-start(bf16[3,96,128]{2,1,0:T(8,128)(2,1)S(1)} %collective-permute-done.refs_1_.refs_2_), channel_id=1, source_target_pairs={{0,2},{1,3},{2,0},{3,1},{4,6},{5,7},{6,4},{7,5},{8,10},{9,11},{10,... | collective-permute-start | bytes 221192 | tf_op jit(solution)/shard_map/ppermute | solution.py:255
  18.9 2.2 %collective-permute-start.4 = (bf16[3,896,128]{2,1,0:T(8,128)(2,1)S(1)}, bf16[3,896,128]{2,1,0:T(8,128)(2,1)S(1)}, u32[]{:S(2)}, u32[]{:S(2)}) collective-permute-start(bf16[3,896,128]{2,1,0:T(8,128)(2,1)S(1)} %pack.4.refs_1_), channel_id=1, source_target_pairs={{0,1},{1,0},{2,3},{3,2},{4,5},{5,4},{6,7},{7,6},{8,9},{9,8},{10,11... | collective-permute-start | bytes 2064392 | tf_op jit(solution)/shard_map/ppermute | solution.py:255
  19.0 6.5 %collective-permute-start.5 = (bf16[3,192,128]{2,1,0:T(8,128)(2,1)S(1)}, bf16[3,192,128]{2,1,0:T(8,128)(2,1)S(1)}, u32[]{:S(2)}, u32[]{:S(2)}) collective-permute-start(bf16[3,192,128]{2,1,0:T(8,128)(2,1)S(1)} %collective-permute-done.3.refs_5_.refs_3_.refs_0_), channel_id=1, source_target_pairs={{0,2},{1,3},{2,0},{3,1},{4,6},{5,7},{6,4},{7,5},{8,10},{9,11},{10,... | collective-permute-start | bytes 442376 | tf_op jit(solution)/shard_map/ppermute | solution.py:255
  25.5 3.4 %collective-permute-start.6 = (bf16[3,384,128]{2,1,0:T(8,128)(2,1)S(1)}, bf16[3,384,128]{2,1,0:T(8,128)(2,1)S(1)}, u32[]{:S(2)}, u32[]{:S(2)}) collective-permute-start(bf16[3,384,128]{2,1,0:T(8,128)(2,1)S(1)} %pack.5.refs_3_), channel_id=1, source_target_pairs={{0,1},{1,0},{2,3},{3,2},{4,5},{5,4},{6,7},{7,6},{8,9},{9,8},{10,11... | collective-permute-start | bytes 884744 | tf_op jit(solution)/shard_map/ppermute | solution.py:255

commit v6 on v4

--- a/solution.py
+++ b/solution.py
@@ -9,8 +9,8 @@
 from jax.sharding import PartitionSpec as P
 
 adapter_scale = 0.5
-out_slots = 6
-tile_rows = 256
+out_slots = 4
+tile_rows = 512
 in_vmem = pl.BlockSpec(memory_space=pltpu.VMEM)
 in_hbm = pl.BlockSpec(memory_space=pltpu.HBM)
 anywhere = pl.BlockSpec(memory_space=pl.ANY)
@@ -70,6 +70,25 @@
     )(*[pltpu.with_memory_space_constraint(x, pltpu.HBM) for x in (index, narrow, wide)])
 
 
+def load_kernel(base_ref, _, out_ref, sem):
+    copy = pltpu.make_async_copy(base_ref, out_ref, sem)
+    copy.start()
+    copy.wait()
+
+
+def load(base, after):
+    return pl.pallas_call(
+        load_kernel,
+        out_shape=jax.ShapeDtypeStruct(base.shape, base.dtype),
+        in_specs=[in_hbm, anywhere],
+        out_specs=in_vmem,
+        scratch_shapes=[pltpu.SemaphoreType.DMA],
+        compiler_params=pltpu.CompilerParams(vmem_limit_bytes=vmem_limit),
+        cost_estimate=pl.CostEstimate(flops=0, bytes_accessed=2 * base.size, transcendentals=0),
+        name="load",
+    )(base, after)
+
+
 def pack_kernel(count, *refs):
     out_ref = refs[-1]
     at = 0
@@ -92,65 +111,72 @@
     )(*blocks, *after)
 
 
-def merge_kernel(plan, count, base_ref, *refs):
+def merge_kernel(plan, base_ref, *refs):
     out_ref, token, n_all, w_rows, w_all, out_buf, sems = refs[-7:]
-    experts, _, width, _ = base_ref.shape
-    deep, span = w_all.shape
+    experts, projections, width, _ = base_ref.shape
+    _, deep, span = w_all.shape
     m_step = out_buf.shape[1]
     f_step = 256 if span % 256 == 0 else span
     strips = width // m_step
     tiles = experts * strips
+    steps = projections * tiles
     s, g = lax.axis_index("shard"), lax.axis_index("group")
     lane_expert = lax.broadcasted_iota(jnp.int32, (m_step, deep), 1) // plan.rank
-    first_column = pl.multiple_of(plan.chunk(s) * span, span)
-
-    def out_copy(p, step):
-        t = lax.rem(step, tiles)
-        rows = pl.ds(pl.multiple_of((t % strips) * m_step, m_step), m_step)
-        slot = lax.rem(step, out_slots)
-        place = out_ref.at[t // strips, p, rows, pl.ds(first_column, span)]
-        return pltpu.make_async_copy(out_buf.at[slot], place, sems.at[slot])
-
-    for done, p in enumerate(plan.projections):
+
+    def prepare(p, _):
         for i, first, rows, place in plan.n_pieces:
             at = pl.multiple_of(place(s, g) * rows, rows)
-            n_all[pl.ds(at, rows), :] = refs[i][p, pl.ds(first, rows)]
+            n_all[p, pl.ds(at, rows), :] = refs[i][p, pl.ds(first, rows)]
         for i, first, rows, place in plan.w_pieces:
             at = pl.multiple_of(place(s, g) * rows, rows)
             w_rows[pl.ds(at, rows), :] = refs[i][p, pl.ds(first, rows)]
         for f in range(0, span, f_step):
-            w_all[:, f : f + f_step] = w_rows[f : f + f_step].T
+            w_all[p, :, f : f + f_step] = w_rows[f : f + f_step].T
+        return 0
+
+    lax.fori_loop(0, projections, prepare, 0)
+
+    def merge_chunk(first_column):
+        columns = pl.ds(first_column, span)
+
+        def out_copy(step):
+            p, t = step // tiles, lax.rem(step, tiles)
+            rows = pl.ds(pl.multiple_of(lax.rem(t, strips) * m_step, m_step), m_step)
+            slot = lax.rem(step, out_slots)
+            return pltpu.make_async_copy(out_buf.at[slot], out_ref.at[t // strips, p, rows, columns], sems.at[slot])
 
         def tile(step, _):
-            t = lax.rem(step, tiles)
+            p, t = step // tiles, lax.rem(step, tiles)
             e = t // strips
-            rows = pl.ds(pl.multiple_of((t % strips) * m_step, m_step), m_step)
+            rows = pl.ds(pl.multiple_of(lax.rem(t, strips) * m_step, m_step), m_step)
             slot = lax.rem(step, out_slots)
 
             @pl.when(step >= out_slots)
             def _():
-                out_copy(p, step).wait()
-
-            n = n_all[rows, :]
+                out_copy(step - out_slots).wait()
+
+            n = n_all[p, rows, :]
             n = jnp.where(lane_expert == e, n, jnp.zeros_like(n))
             for f in range(0, span, f_step):
-                delta = jnp.dot(n, w_all[:, f : f + f_step], preferred_element_type=jnp.float32)
-                b = base_ref[e, p, rows, pl.ds(first_column + f, f_step)].astype(jnp.float32)
-                out_buf[slot, :, f : f + f_step] = (b + delta).astype(out_buf.dtype)
-            out_copy(p, step).start()
+                delta = jnp.dot(n, w_all[p, :, f : f + f_step], preferred_element_type=jnp.float32)
+                b = base_ref[e, p, rows, first_column + f : first_column + f + f_step]
+                out_buf[slot, :, f : f + f_step] = (b.astype(jnp.float32) + delta).astype(out_buf.dtype)
+            out_copy(step).start()
             return 0
 
-        lax.fori_loop(done * tiles, (done + 1) * tiles, tile, 0)
-    steps = len(plan.projections) * tiles
-    for step in range(max(0, steps - out_slots), steps):
-        out_copy(plan.projections[-1], step).wait()
+        lax.fori_loop(0, steps, tile, 0)
+        for step in range(max(0, steps - out_slots), steps):
+            out_copy(jnp.int32(step)).wait()
+
+    for c in range(plan.chunks):
+        pl.when(plan.chunk(s) == c)(functools.partial(merge_chunk, c * span))
     token[...] = jnp.zeros_like(token)
 
 
 class Plan(typing.NamedTuple):
     rank: int
-    projections: tuple
     span: int
+    chunks: int
     chunk: typing.Callable
     n_pieces: list
     w_pieces: list
@@ -160,17 +186,18 @@
     experts, projections, width, _ = base.shape
     deep = parts[0].shape[-1]
     m_step = tile_rows if width % tile_rows == 0 else width
-    operands = [base, *parts, *after] + ([] if out is None else [out])
-    share = len(plan.projections) * plan.span * experts * width
-    return pl.pallas_call(
-        functools.partial(merge_kernel, plan, len(parts)),
+    share = projections * plan.span * experts * width
+    extra = [*after] + ([] if out is None else [out])
+    operands = [base, *parts, *extra]
+    return pl.pallas_call(
+        functools.partial(merge_kernel, plan),
         out_shape=(jax.ShapeDtypeStruct(base.shape, base.dtype), jax.ShapeDtypeStruct((8, 128), jnp.float32)),
-        in_specs=[in_vmem] * (1 + len(parts)) + [anywhere] * (len(operands) - 1 - len(parts)),
+        in_specs=[in_vmem] * (1 + len(parts)) + [anywhere] * len(extra),
         out_specs=(in_hbm, in_vmem),
         scratch_shapes=[
-            pltpu.VMEM((width, deep), base.dtype),
+            pltpu.VMEM((projections, width, deep), base.dtype),
             pltpu.VMEM((plan.span, deep), base.dtype),
-            pltpu.VMEM((deep, plan.span), base.dtype),
+            pltpu.VMEM((projections, deep, plan.span), base.dtype),
             pltpu.VMEM((out_slots, m_step, plan.span), base.dtype),
             pltpu.SemaphoreType.DMA((out_slots,)),
         ],
@@ -184,7 +211,6 @@
 def on_device(shards, groups, base, narrow, wide, adapted_expert_index):
     rank = narrow.shape[3]
     rows, columns = narrow.shape[2], wide.shape[3]
-    projections = tuple(range(base.shape[1]))
     both, w = select(jnp.swapaxes(narrow, 2, 3), wide, adapted_expert_index)
     axes = ("shard", "group")
 
@@ -194,8 +220,8 @@
         whole = lambda s, g: 0
         plan = Plan(
             rank,
-            projections,
             columns * shards * groups,
+            1,
             lambda s: 0,
             [(0, 0, rows * groups, whole)],
             [(1, 0, columns * shards * groups, whole)],
@@ -205,9 +231,9 @@
     def swap(x, axis, bit):
         return lax.ppermute(x, axis, [(i, i ^ bit) for i in range(4)])
 
-    base = swap(base, "group", 0)
     w3, w2, w1 = [swap(w, "shard", k) for k in (3, 2, 1)]
-    line = pack([w2, w3])
+    base = load(base, w1)
+    line = pack([w2, w3], (base,))
     own_a = pack([both, swap(both, "group", 2), w1, swap(w1, "group", 2)], (line,))
     other_a = swap(own_a, "group", 1)
     line_x = swap(line, "group", 2)
@@ -227,14 +253,12 @@
         for at, k in ((0, 2), (1, 3)):
             far += [w_piece(i + 2, at * columns, k, m), w_piece(i + 2, (at + 2) * columns, k, m ^ 2)]
     span = 2 * columns * groups
-    near_plan = Plan(rank, projections, span, lambda s: s // 2, n_pieces, near)
-    far_plan = Plan(rank, projections, span, lambda s: 1 - s // 2, n_pieces, far)
+    near_plan = Plan(rank, span, 2, lambda s: s // 2, n_pieces, near)
+    far_plan = Plan(rank, span, 2, lambda s: 1 - s // 2, n_pieces, far)
     parts = [own_a, other_a]
-    out, token = merge(near_plan._replace(projections=projections[:2]), base, parts, after=(line,))
+    out, token = merge(near_plan, base, parts, after=(line,))
     own_b = pack([line, line_x], (token,))
-    other_b = swap(own_b, "group", 1)
-    out, _ = merge(near_plan._replace(projections=projections[2:]), base, parts, out, after=(own_b,))
-    return merge(far_plan, base, parts + [own_b, other_b], out)[0]
+    return merge(far_plan, base, parts + [own_b, swap(own_b, "group", 1)], out)[0]
 
 
 def solution(mesh):

time: 41.4 us -> 32.1 us (0.78)
  waiting for transfers between devices: 7.9 us -> 2.03 us
  starting transfers between devices: 14.8 us -> 9.54 us
  Pallas kernels: 18.4 us -> 20.3 us
    ppermute x9 -> x8, waiting for transfers between devices: 7.9 us -> 2.03 us  [swap(): return lax.ppermute(x, axis, [(i, i ^ bit) for i in range(4)])]
    ppermute x9 -> x8, starting transfers between devices: 14.8 us -> 9.54 us  [swap(): return lax.ppermute(x, axis, [(i, i ^ bit) for i in range(4)])]
    pallas_call x3, Pallas kernels: 16.5 us -> 18.3 us  [the longest x2 12 us: merge(): pl.pallas_call(functools.partial(merge_kernel, plan), out_shape=(jax.Shap...]
  transfers between devices with their start and end apart: 9 -> 8, of which waited for: 4 -> 3; matrix products, arithmetic and copies ran while one was open for 0% -> 0% of each run, Pallas kernels for 26% -> 38%
where the time goes in v6:
time: 32.1 us; the launch traced here: 31.9 us
  Pallas kernels  20.3 us (63%)
  starting transfers between devices  9.54 us (30%)
  waiting for transfers between devices  2.03 us (6%)
    pallas_call x2, Pallas kernels, merge(): pl.pallas_call(functools.partial(merge_kernel, plan), out_shape=(jax.Shap...  12 us
    ppermute x8, starting transfers between devices, swap(): return lax.ppermute(x, axis, [(i, i ^ bit) for i in range(4)])  9.54 us
    pallas_call x1, Pallas kernels, load(): pl.pallas_call(load_kernel, out_shape=jax.ShapeDtypeStruct(base.shape, ba...  6.37 us
    ppermute x8, waiting for transfers between devices, swap(): return lax.ppermute(x, axis, [(i, i ^ bit) for i in range(4)])  2.03 us
    pallas_call x1, Pallas kernels, select(): pl.pallas_call(select_kernel, out_shape=(jax.ShapeDtypeStruct((projection...  1.84 us
  transfers between devices with their start and end apart: 8, of which 3 were waited for; matrix products, arithmetic and copies ran while one was open for 0% of the time, Pallas kernels for 38%

profile of v6, /device:TPU:0, one launch (start us, length us, event | category | flops | bytes accessed | tf_op | source)
XLA Modules:
  0.0 31.9 jit_solution(880601414013980748)
XLA Ops:
  0.0 1.8 %select.1 = (bf16[3,352,128]{2,1,0:T(8,128)(2,1)S(1)}, bf16[3,96,128]{2,1,0:T(8,128)(2,1)S(1)}) custom-call(s32[2]{0:T(128)} %index_ref.1, bf16[32,3,64,256]{3,2,1,0:T(8,128)(2,1)} %bitcast.1, bf16[32,3,64,96]{3,2,1,0:T(8,128)(2,1)} %wide_ref.1), custom_call_target="tpu_custom_call" | custom-call | tf_op jit(solution)/shard_map/select/pallas_call | solution.py:53
  1.9 3.0 %collective-permute-start.1 = (bf16[3,352,128]{2,1,0:T(8,128)(2,1)S(1)}, bf16[3,352,128]{2,1,0:T(8,128)(2,1)S(1)}, u32[]{:S(2)}, u32[]{:S(2)}) collective-permute-start(bf16[3,352,128]{2,1,0:T(8,128)(2,1)S(1)} %get-tuple-element.11.refs_0_), channel_id=1, source_target_pairs={{0,2},{1,3},{2,0},{3,1},{4,6},{5,7},{6,4},{7,5},{8,10},{9,11},{10,... | collective-permute-start | bytes 811016 | tf_op jit(solution)/shard_map/ppermute | solution.py:232
  4.9 1.6 %collective-permute-start = (bf16[3,96,128]{2,1,0:T(8,128)(2,1)S(1)}, bf16[3,96,128]{2,1,0:T(8,128)(2,1)S(1)}, u32[]{:S(2)}, u32[]{:S(2)}) collective-permute-start(bf16[3,96,128]{2,1,0:T(8,128)(2,1)S(1)} %get-tuple-element.10), channel_id=1, source_target_pairs={{0,4},{4,0},{8,12},{12,8},{1,5},{5,1},{9,13},{13,9},{2,6},{6,2},{1... | collective-permute-start | bytes 221192 | tf_op jit(solution)/shard_map/ppermute | solution.py:232
  6.4 2.5 %collective-permute-start.4 = (bf16[3,96,128]{2,1,0:T(8,128)(2,1)S(1)}, bf16[3,96,128]{2,1,0:T(8,128)(2,1)S(1)}, u32[]{:S(2)}, u32[]{:S(2)}) collective-permute-start(bf16[3,96,128]{2,1,0:T(8,128)(2,1)S(1)} %get-tuple-element.10), channel_id=1, source_target_pairs={{0,12},{4,8},{8,4},{12,0},{1,13},{5,9},{9,5},{13,1},{2,14},{6,10},... | collective-permute-start | bytes 221192 | tf_op jit(solution)/shard_map/ppermute | solution.py:232
  8.9 0.1 collective-permute-start.3
  9.0 0.2 collective-permute-done._.refs_2_
  9.2 0.4 %collective-permute-start.2 = (bf16[3,96,128]{2,1,0:T(8,128)(2,1)S(1)}, bf16[3,96,128]{2,1,0:T(8,128)(2,1)S(1)}, u32[]{:S(2)}, u32[]{:S(2)}) collective-permute-start(bf16[3,96,128]{2,1,0:T(8,128)(2,1)S(1)} %collective-permute-done._.refs_2_), channel_id=1, source_target_pairs={{0,2},{1,3},{2,0},{3,1},{4,6},{5,7},{6,4},{7,5},{8,10},{9,11},{10,... | collective-permute-start | bytes 221192 | tf_op jit(solution)/shard_map/ppermute | solution.py:232
  9.6 6.4 %load.1.refs_2_.base_ref = bf16[2,3,1024,1536]{3,2,1,0:T(8,128)(2,1)S(1)} custom-call(bf16[2,3,1024,1536]{3,2,1,0:T(8,128)(2,1)} %base_ref.1, bf16[3,96,128]{2,1,0:T(8,128)(2,1)S(1)} %collective-permute-done._.refs_2_), custom_call_target="tpu_custom_call" | custom-call | bytes 18874368 | tf_op jit(solution)/shard_map/load/pallas_call | solution.py:80
  15.9 0.0 collective-permute-done.4.refs_1_
  16.0 0.0 collective-permute-done.3.refs_0_
  16.0 0.0 collective-permute-done.2.refs_3_
  16.0 0.0 collective-permute-done.1.refs_1_
  16.1 0.1 collective-permute-start.5
  16.1 1.7 %collective-permute-start.6 = (bf16[3,192,128]{2,1,0:T(8,128)(2,1)S(1)}, bf16[3,192,128]{2,1,0:T(8,128)(2,1)S(1)}, u32[]{:S(2)}, u32[]{:S(2)}) collective-permute-start(bf16[3,192,128]{2,1,0:T(8,128)(2,1)S(1)} %pack.3.refs_4_.refs_2_.refs_0_), channel_id=1, source_target_pairs={{0,2},{1,3},{2,0},{3,1},{4,6},{5,7},{6,4},{7,5},{8,10},{9,11},{10,... | collective-permute-start | bytes 442376 | tf_op jit(solution)/shard_map/ppermute | solution.py:232
  17.9 0.4 %collective-permute-done.5.refs_1_ = bf16[3,896,128]{2,1,0:T(8,128)(2,1)S(1)} collective-permute-done((bf16[3,896,128]{2,1,0:T(8,128)(2,1)S(1)}, bf16[3,896,128]{2,1,0:T(8,128)(2,1)S(1)}, u32[]{:S(2)}, u32[]{:S(2)}) %collective-permute-start.5) | collective-permute-done | bytes 688160 | tf_op jit(solution)/shard_map/ppermute | solution.py:232
  18.3 5.7 %merge.2 = (bf16[2,3,1024,1536]{3,2,1,0:T(8,128)(2,1)}, f32[8,128]{1,0:T(8,128)S(1)}) custom-call(bf16[2,3,1024,1536]{3,2,1,0:T(8,128)(2,1)S(1)} %load.1.refs_2_.base_ref, bf16[3,896,128]{2,1,0:T(8,128)(2,1)S(1)} %pack.4.refs_0_, bf16[3,896,128]{2,1,0:T(8,128)(2,1)S(1)} %collective-permute-done.5.refs_1_, bf16[3,192,128]{2,1,0:T(8,128)(2,1)S(1)} %pack.3.refs_4_.refs_2_.refs_0_), custom_call_target="tpu_custom_call" | custom-call | flops 603979776 | bytes 18874368 | tf_op jit(solution)/shard_map/merge/pallas_call | solution.py:192
  24.0 0.0 collective-permute-done.6.refs_1_
  24.0 0.2 collective-permute-start.7
  24.2 1.4 %collective-permute-done.7.refs_3_ = bf16[3,384,128]{2,1,0:T(8,128)(2,1)S(1)} collective-permute-done((bf16[3,384,128]{2,1,0:T(8,128)(2,1)S(1)}, bf16[3,384,128]{2,1,0:T(8,128)(2,1)S(1)}, u32[]{:S(2)}, u32[]{:S(2)}) %collective-permute-start.7) | collective-permute-done | bytes 294944 | tf_op jit(solution)/shard_map/ppermute | solution.py:232
  25.7 6.3 %merge.3 = (bf16[2,3,1024,1536]{3,2,1,0:T(8,128)(2,1)}, f32[8,128]{1,0:T(8,128)}) custom-call(bf16[2,3,1024,1536]{3,2,1,0:T(8,128)(2,1)S(1)} %load.1.refs_2_.base_ref, bf16[3,896,128]{2,1,0:T(8,128)(2,1)S(1)} %pack.4.refs_0_, bf16[3,896,128]{2,1,0:T(8,128)(2,1)S(1)} %collective-permute-done.5.refs_1_, ...), custom_call_target="tpu_custom_call", output_to_operand_aliasing={{0}: (5, {})} | custom-call | flops 603979776 | bytes 18874368 | tf_op jit(solution)/shard_map/merge/pallas_call | solution.py:192
  (3 shorter events, 0.1 us)
Async XLA Ops:
  1.9 14.1 %collective-permute-start.1 = (bf16[3,352,128]{2,1,0:T(8,128)(2,1)S(1)}, bf16[3,352,128]{2,1,0:T(8,128)(2,1)S(1)}, u32[]{:S(2)}, u32[]{:S(2)}) collective-permute-start(bf16[3,352,128]{2,1,0:T(8,128)(2,1)S(1)} %get-tuple-element.11.refs_0_), channel_id=1, source_target_pairs={{0,2},{1,3},{2,0},{3,1},{4,6},{5,7},{6,4},{7,5},{8,10},{9,11},{10,... | collective-permute-start | bytes 811016 | tf_op jit(solution)/shard_map/ppermute | solution.py:232
  4.9 4.4 %collective-permute-start = (bf16[3,96,128]{2,1,0:T(8,128)(2,1)S(1)}, bf16[3,96,128]{2,1,0:T(8,128)(2,1)S(1)}, u32[]{:S(2)}, u32[]{:S(2)}) collective-permute-start(bf16[3,96,128]{2,1,0:T(8,128)(2,1)S(1)} %get-tuple-element.10), channel_id=1, source_target_pairs={{0,4},{4,0},{8,12},{12,8},{1,5},{5,1},{9,13},{13,9},{2,6},{6,2},{1... | collective-permute-start | bytes 221192 | tf_op jit(solution)/shard_map/ppermute | solution.py:232
  6.4 9.5 %collective-permute-start.4 = (bf16[3,96,128]{2,1,0:T(8,128)(2,1)S(1)}, bf16[3,96,128]{2,1,0:T(8,128)(2,1)S(1)}, u32[]{:S(2)}, u32[]{:S(2)}) collective-permute-start(bf16[3,96,128]{2,1,0:T(8,128)(2,1)S(1)} %get-tuple-element.10), channel_id=1, source_target_pairs={{0,12},{4,8},{8,4},{12,0},{1,13},{5,9},{9,5},{13,1},{2,14},{6,10},... | collective-permute-start | bytes 221192 | tf_op jit(solution)/shard_map/ppermute | solution.py:232
  8.9 7.1 %collective-permute-start.3 = (bf16[3,96,128]{2,1,0:T(8,128)(2,1)S(1)}, bf16[3,96,128]{2,1,0:T(8,128)(2,1)S(1)}, u32[]{:S(2)}, u32[]{:S(2)}) collective-permute-start(bf16[3,96,128]{2,1,0:T(8,128)(2,1)S(1)} %get-tuple-element.10), channel_id=1, source_target_pairs={{0,8},{4,12},{8,0},{12,4},{1,9},{5,13},{9,1},{13,5},{2,10},{6,14},... | collective-permute-start | bytes 221192 | tf_op jit(solution)/shard_map/ppermute | solution.py:232
  9.2 6.8 %collective-permute-start.2 = (bf16[3,96,128]{2,1,0:T(8,128)(2,1)S(1)}, bf16[3,96,128]{2,1,0:T(8,128)(2,1)S(1)}, u32[]{:S(2)}, u32[]{:S(2)}) collective-permute-start(bf16[3,96,128]{2,1,0:T(8,128)(2,1)S(1)} %collective-permute-done._.refs_2_), channel_id=1, source_target_pairs={{0,2},{1,3},{2,0},{3,1},{4,6},{5,7},{6,4},{7,5},{8,10},{9,11},{10,... | collective-permute-start | bytes 221192 | tf_op jit(solution)/shard_map/ppermute | solution.py:232
  16.1 2.2 %collective-permute-start.5 = (bf16[3,896,128]{2,1,0:T(8,128)(2,1)S(1)}, bf16[3,896,128]{2,1,0:T(8,128)(2,1)S(1)}, u32[]{:S(2)}, u32[]{:S(2)}) collective-permute-start(bf16[3,896,128]{2,1,0:T(8,128)(2,1)S(1)} %pack.4.refs_0_), channel_id=1, source_target_pairs={{0,1},{1,0},{2,3},{3,2},{4,5},{5,4},{6,7},{7,6},{8,9},{9,8},{10,11... | collective-permute-start | bytes 2064392 | tf_op jit(solution)/shard_map/ppermute | solution.py:232
  16.1 7.8 %collective-permute-start.6 = (bf16[3,192,128]{2,1,0:T(8,128)(2,1)S(1)}, bf16[3,192,128]{2,1,0:T(8,128)(2,1)S(1)}, u32[]{:S(2)}, u32[]{:S(2)}) collective-permute-start(bf16[3,192,128]{2,1,0:T(8,128)(2,1)S(1)} %pack.3.refs_4_.refs_2_.refs_0_), channel_id=1, source_target_pairs={{0,2},{1,3},{2,0},{3,1},{4,6},{5,7},{6,4},{7,5},{8,10},{9,11},{10,... | collective-permute-start | bytes 442376 | tf_op jit(solution)/shard_map/ppermute | solution.py:232
  24.0 1.6 %collective-permute-start.7 = (bf16[3,384,128]{2,1,0:T(8,128)(2,1)S(1)}, bf16[3,384,128]{2,1,0:T(8,128)(2,1)S(1)}, u32[]{:S(2)}, u32[]{:S(2)}) collective-permute-start(bf16[3,384,128]{2,1,0:T(8,128)(2,1)S(1)} %pack.5.refs_2_), channel_id=1, source_target_pairs={{0,1},{1,0},{2,3},{3,2},{4,5},{5,4},{6,7},{7,6},{8,9},{9,8},{10,11... | collective-permute-start | bytes 884744 | tf_op jit(solution)/shard_map/ppermute | solution.py:232

commit v7 on v6

--- a/solution.py
+++ b/solution.py
@@ -9,7 +9,7 @@
 from jax.sharding import PartitionSpec as P
 
 adapter_scale = 0.5
-out_slots = 4
+out_slots = 3
 tile_rows = 512
 in_vmem = pl.BlockSpec(memory_space=pltpu.VMEM)
 in_hbm = pl.BlockSpec(memory_space=pltpu.HBM)
@@ -70,23 +70,27 @@
     )(*[pltpu.with_memory_space_constraint(x, pltpu.HBM) for x in (index, narrow, wide)])
 
 
-def load_kernel(base_ref, _, out_ref, sem):
-    copy = pltpu.make_async_copy(base_ref, out_ref, sem)
+def load_kernel(p, base_ref, *refs):
+    out_ref, sem = refs[-2:]
+    copy = pltpu.make_async_copy(base_ref.at[:, p], out_ref.at[:, p], sem)
     copy.start()
     copy.wait()
 
 
-def load(base, after):
+def load(base, p, loaded=None, after=()):
+    extra = [*after] + ([] if loaded is None else [loaded])
+    specs = [anywhere] * len(after) + ([] if loaded is None else [in_vmem])
     return pl.pallas_call(
-        load_kernel,
+        functools.partial(load_kernel, p),
         out_shape=jax.ShapeDtypeStruct(base.shape, base.dtype),
-        in_specs=[in_hbm, anywhere],
+        in_specs=[in_hbm] + specs,
         out_specs=in_vmem,
         scratch_shapes=[pltpu.SemaphoreType.DMA],
+        input_output_aliases={} if loaded is None else {len(extra): 0},
         compiler_params=pltpu.CompilerParams(vmem_limit_bytes=vmem_limit),
-        cost_estimate=pl.CostEstimate(flops=0, bytes_accessed=2 * base.size, transcendentals=0),
+        cost_estimate=pl.CostEstimate(flops=0, bytes_accessed=2 * base.size // base.shape[1], transcendentals=0),
         name="load",
-    )(base, after)
+    )(pltpu.with_memory_space_constraint(base, pltpu.HBM), *extra)
 
 
 def pack_kernel(count, *refs):
@@ -111,17 +115,24 @@
     )(*blocks, *after)
 
 
-def merge_kernel(plan, base_ref, *refs):
-    out_ref, token, n_all, w_rows, w_all, out_buf, sems = refs[-7:]
-    experts, projections, width, _ = base_ref.shape
-    _, deep, span = w_all.shape
-    m_step = out_buf.shape[1]
+def merge_kernel(plan, late, *refs):
+    base_ref, held_ref, *refs = refs if late else (None, *refs)
+    n_all, w_all, out_buf, sems, late_sem = refs[-5:]
+    out_ref, token, held_ref = refs[-8:-5] if late else [*refs[-7:-5], held_ref]
+    experts, projections, width, _ = held_ref.shape
+    _, span, deep = w_all.shape
+    m_step = tile_rows if width % tile_rows == 0 else width
     f_step = 256 if span % 256 == 0 else span
-    strips = width // m_step
-    tiles = experts * strips
-    steps = projections * tiles
+    steps = projections * experts
     s, g = lax.axis_index("shard"), lax.axis_index("group")
     lane_expert = lax.broadcasted_iota(jnp.int32, (m_step, deep), 1) // plan.rank
+    first_late = projections - late
+    late_copies = [
+        pltpu.make_async_copy(base_ref.at[:, p], held_ref.at[:, p], late_sem.at[p - first_late])
+        for p in range(first_late, projections)
+    ]
+    for copy in late_copies:
+        copy.start()
 
     def prepare(p, _):
         for i, first, rows, place in plan.n_pieces:
@@ -129,9 +140,7 @@
             n_all[p, pl.ds(at, rows), :] = refs[i][p, pl.ds(first, rows)]
         for i, first, rows, place in plan.w_pieces:
             at = pl.multiple_of(place(s, g) * rows, rows)
-            w_rows[pl.ds(at, rows), :] = refs[i][p, pl.ds(first, rows)]
-        for f in range(0, span, f_step):
-            w_all[p, :, f : f + f_step] = w_rows[f : f + f_step].T
+            w_all[p, pl.ds(at, rows), :] = refs[i][p, pl.ds(first, rows)]
         return 0
 
     lax.fori_loop(0, projections, prepare, 0)
@@ -139,34 +148,47 @@
     def merge_chunk(first_column):
         columns = pl.ds(first_column, span)
 
-        def out_copy(step):
-            p, t = step // tiles, lax.rem(step, tiles)
-            rows = pl.ds(pl.multiple_of(lax.rem(t, strips) * m_step, m_step), m_step)
+        def out_copies(step):
+            p, e = step // experts, lax.rem(step, experts)
             slot = lax.rem(step, out_slots)
-            return pltpu.make_async_copy(out_buf.at[slot], out_ref.at[t // strips, p, rows, columns], sems.at[slot])
+            return [
+                pltpu.make_async_copy(
+                    out_buf.at[slot, pl.ds(m, m_step)],
+                    out_ref.at[e, p, pl.ds(m, m_step), columns],
+                    sems.at[slot, m // m_step],
+                )
+                for m in range(0, width, m_step)
+            ]
 
         def tile(step, _):
-            p, t = step // tiles, lax.rem(step, tiles)
-            e = t // strips
-            rows = pl.ds(pl.multiple_of(lax.rem(t, strips) * m_step, m_step), m_step)
+            p, e = step // experts, lax.rem(step, experts)
             slot = lax.rem(step, out_slots)
 
             @pl.when(step >= out_slots)
             def _():
-                out_copy(step - out_slots).wait()
-
-            n = n_all[p, rows, :]
-            n = jnp.where(lane_expert == e, n, jnp.zeros_like(n))
-            for f in range(0, span, f_step):
-                delta = jnp.dot(n, w_all[p, :, f : f + f_step], preferred_element_type=jnp.float32)
-                b = base_ref[e, p, rows, first_column + f : first_column + f + f_step]
-                out_buf[slot, :, f : f + f_step] = (b.astype(jnp.float32) + delta).astype(out_buf.dtype)
-            out_copy(step).start()
+                for copy in out_copies(step - out_slots):
+                    copy.wait()
+
+            for copy, m in zip(out_copies(step), range(0, width, m_step)):
+                n = n_all[p, m : m + m_step, :]
+                n = jnp.where(lane_expert == e, n, jnp.zeros_like(n))
+                for f in range(0, span, f_step):
+                    delta = lax.dot_general(
+                        n, w_all[p, f : f + f_step], (((1,), (1,)), ((), ())), preferred_element_type=jnp.float32
+                    )
+                    b = held_ref[e, p, m : m + m_step, first_column + f : first_column + f + f_step]
+                    out_buf[slot, m : m + m_step, f : f + f_step] = (b.astype(jnp.float32) + delta).astype(out_buf.dtype)
+                copy.start()
             return 0
 
-        lax.fori_loop(0, steps, tile, 0)
+        lax.fori_loop(0, first_late * experts, tile, 0)
+        if late:
+            for copy in late_copies:
+                copy.wait()
+            lax.fori_loop(first_late * experts, steps, tile, 0)
         for step in range(max(0, steps - out_slots), steps):
-            out_copy(jnp.int32(step)).wait()
+            for copy in out_copies(jnp.int32(step)):
+                copy.wait()
 
     for c in range(plan.chunks):
         pl.when(plan.chunk(s) == c)(functools.partial(merge_chunk, c * span))
@@ -182,26 +204,33 @@
     w_pieces: list
 
 
-def merge(plan, base, parts, out=None, after=()):
-    experts, projections, width, _ = base.shape
+def merge(plan, base, held, parts, late=0, out=None, after=()):
+    experts, projections, width, _ = held.shape
     deep = parts[0].shape[-1]
-    m_step = tile_rows if width % tile_rows == 0 else width
     share = projections * plan.span * experts * width
     extra = [*after] + ([] if out is None else [out])
-    operands = [base, *parts, *extra]
+    source = [pltpu.with_memory_space_constraint(base, pltpu.HBM)] if late else []
+    operands = [*source, held, *parts, *extra]
+    aliases = {} if out is None else {len(operands) - 1: 0}
+    out_shape = [jax.ShapeDtypeStruct(held.shape, held.dtype), jax.ShapeDtypeStruct((8, 128), jnp.float32)]
+    out_specs = [in_hbm, in_vmem]
+    if late:
+        aliases[1] = 2
+        out_shape.append(jax.ShapeDtypeStruct(held.shape, held.dtype))
+        out_specs.append(in_vmem)
     return pl.pallas_call(
-        functools.partial(merge_kernel, plan),
-        out_shape=(jax.ShapeDtypeStruct(base.shape, base.dtype), jax.ShapeDtypeStruct((8, 128), jnp.float32)),
-        in_specs=[in_vmem] * (1 + len(parts)) + [anywhere] * len(extra),
-        out_specs=(in_hbm, in_vmem),
+        functools.partial(merge_kernel, plan, late),
+        out_shape=out_shape,
+        in_specs=[in_hbm] * len(source) + [in_vmem] * (1 + len(parts)) + [anywhere] * len(extra),
+        out_specs=out_specs,
         scratch_shapes=[
-            pltpu.VMEM((projections, width, deep), base.dtype),
-            pltpu.VMEM((plan.span, deep), base.dtype),
-            pltpu.VMEM((projections, deep, plan.span), base.dtype),
-            pltpu.VMEM((out_slots, m_step, plan.span), base.dtype),
-            pltpu.SemaphoreType.DMA((out_slots,)),
+            pltpu.VMEM((projections, width, deep), held.dtype),
+            pltpu.VMEM((projections, plan.span, deep), held.dtype),
+            pltpu.VMEM((out_slots, width, plan.span), held.dtype),
+            pltpu.SemaphoreType.DMA((out_slots, 2)),
+            pltpu.SemaphoreType.DMA((max(late, 1),)),
         ],
-        input_output_aliases={} if out is None else {len(operands) - 1: 0},
+        input_output_aliases=aliases,
         compiler_params=pltpu.CompilerParams(vmem_limit_bytes=vmem_limit),
         cost_estimate=pl.CostEstimate(flops=2 * share * plan.rank, bytes_accessed=4 * share, transcendentals=0),
         name="merge",
@@ -226,14 +255,16 @@
             [(0, 0, rows * groups, whole)],
             [(1, 0, columns * shards * groups, whole)],
         )
-        return merge(plan, base, [n, w])[0]
+        return merge(plan, None, base, [n, w])[0]
 
     def swap(x, axis, bit):
         return lax.ppermute(x, axis, [(i, i ^ bit) for i in range(4)])
 
-    w3, w2, w1 = [swap(w, "shard", k) for k in (3, 2, 1)]
-    base = load(base, w1)
-    line = pack([w2, w3], (base,))
+    w2, w1 = [swap(w, "shard", k) for k in (2, 1)]
+    held = load(base, 0, after=(w1,))
+    w2 = pack([w2], (held,))
+    held = load(base, 1, held, (w2,))
+    line = pack([w2, swap(w2, "shard", 1)], (held,))
     own_a = pack([both, swap(both, "group", 2), w1, swap(w1, "group", 2)], (line,))
     other_a = swap(own_a, "group", 1)
     line_x = swap(line, "group", 2)
@@ -256,9 +287,9 @@
     near_plan = Plan(rank, span, 2, lambda s: s // 2, n_pieces, near)
     far_plan = Plan(rank, span, 2, lambda s: 1 - s // 2, n_pieces, far)
     parts = [own_a, other_a]
-    out, token = merge(near_plan, base, parts, after=(line,))
+    out, token, held = merge(near_plan, base, held, parts, 1, after=(line,))
     own_b = pack([line, line_x], (token,))
-    return merge(far_plan, base, parts + [own_b, swap(own_b, "group", 1)], out)[0]
+    return merge(far_plan, None, held, parts + [own_b, swap(own_b, "group", 1)], out=out)[0]
 
 
 def solution(mesh):

time: 32.1 us -> 34.9 us (1.087)
  waiting for transfers between devices: 2.03 us -> 4.63 us
    ppermute x8, waiting for transfers between devices: 2.03 us -> 4.63 us  [swap(): return lax.ppermute(x, axis, [(i, i ^ bit) for i in range(4)])]
    pallas_call x3 -> x4, Pallas kernels: 18.3 us -> 18.2 us  [the longest x2 12.6 us: merge(): pl.pallas_call(functools.partial(merge_kernel, plan, late), out_shape=out...]
  transfers between devices with their start and end apart: 8 -> 8, of which waited for: 3 -> 5; matrix products, arithmetic and copies ran while one was open for 0% -> 0% of each run, Pallas kernels for 38% -> 37%
where the time goes in v7:
time: 34.9 us; the launch traced here: 34.6 us
  Pallas kernels  20.1 us (58%)
  starting transfers between devices  9.77 us (28%)
  waiting for transfers between devices  4.63 us (13%)
    pallas_call x2, Pallas kernels, merge(): pl.pallas_call(functools.partial(merge_kernel, plan, late), out_shape=out...  12.6 us
    ppermute x8, starting transfers between devices, swap(): return lax.ppermute(x, axis, [(i, i ^ bit) for i in range(4)])  9.77 us
    pallas_call x2, Pallas kernels, load(): pl.pallas_call(functools.partial(load_kernel, p), out_shape=jax.ShapeDtyp...  5.58 us
    ppermute x8, waiting for transfers between devices, swap(): return lax.ppermute(x, axis, [(i, i ^ bit) for i in range(4)])  4.63 us
    pallas_call x1, Pallas kernels, select(): pl.pallas_call(select_kernel, out_shape=(jax.ShapeDtypeStruct((projection...  1.84 us
  transfers between devices with their start and end apart: 8, of which 5 were waited for; matrix products, arithmetic and copies ran while one was open for 0% of the time, Pallas kernels for 37%

profile of v7, /device:TPU:0, one launch (start us, length us, event | category | flops | bytes accessed | tf_op | source)
XLA Modules:
  0.0 34.6 jit_solution(11706868381253043084)
XLA Ops:
  0.0 1.8 %select.1 = (bf16[3,352,128]{2,1,0:T(8,128)(2,1)S(1)}, bf16[3,96,128]{2,1,0:T(8,128)(2,1)S(1)}) custom-call(s32[2]{0:T(128)} %index_ref.1, bf16[32,3,64,256]{3,2,1,0:T(8,128)(2,1)} %bitcast.1, bf16[32,3,64,96]{3,2,1,0:T(8,128)(2,1)} %wide_ref.1), custom_call_target="tpu_custom_call" | custom-call | tf_op jit(solution)/shard_map/select/pallas_call | solution.py:53
  1.9 3.0 %collective-permute-start.2 = (bf16[3,352,128]{2,1,0:T(8,128)(2,1)S(1)}, bf16[3,352,128]{2,1,0:T(8,128)(2,1)S(1)}, u32[]{:S(2)}, u32[]{:S(2)}) collective-permute-start(bf16[3,352,128]{2,1,0:T(8,128)(2,1)S(1)} %get-tuple-element.12.refs_0_), channel_id=1, source_target_pairs={{0,2},{1,3},{2,0},{3,1},{4,6},{5,7},{6,4},{7,5},{8,10},{9,11},{10,... | collective-permute-start | bytes 811016 | tf_op jit(solution)/shard_map/ppermute | solution.py:261
  4.9 1.6 %collective-permute-start.1 = (bf16[3,96,128]{2,1,0:T(8,128)(2,1)S(1)}, bf16[3,96,128]{2,1,0:T(8,128)(2,1)S(1)}, u32[]{:S(2)}, u32[]{:S(2)}) collective-permute-start(bf16[3,96,128]{2,1,0:T(8,128)(2,1)S(1)} %get-tuple-element.11), channel_id=1, source_target_pairs={{0,4},{4,0},{8,12},{12,8},{1,5},{5,1},{9,13},{13,9},{2,6},{6,2},{1... | collective-permute-start | bytes 221192 | tf_op jit(solution)/shard_map/ppermute | solution.py:261
  6.4 2.6 %collective-permute-start = (bf16[3,96,128]{2,1,0:T(8,128)(2,1)S(1)}, bf16[3,96,128]{2,1,0:T(8,128)(2,1)S(1)}, u32[]{:S(2)}, u32[]{:S(2)}) collective-permute-start(bf16[3,96,128]{2,1,0:T(8,128)(2,1)S(1)} %get-tuple-element.11), channel_id=1, source_target_pairs={{0,8},{4,12},{8,0},{12,4},{1,9},{5,13},{9,1},{13,5},{2,10},{6,14},... | collective-permute-start | bytes 221192 | tf_op jit(solution)/shard_map/ppermute | solution.py:261
  9.0 0.2 collective-permute-done.1.refs_0_.refs_2_
  9.2 2.8 %load.2.refs_1_ = bf16[2,3,1024,1536]{3,2,1,0:T(8,128)(2,1)S(1)} custom-call(bf16[2,3,1024,1536]{3,2,1,0:T(8,128)(2,1)} %refs_0_.1, bf16[3,96,128]{2,1,0:T(8,128)(2,1)S(1)} %collective-permute-done.1.refs_0_.refs_2_), custom_call_target="tpu_custom_call" | custom-call | bytes 6291456 | tf_op jit(solution)/shard_map/load/pallas_call | solution.py:83
  12.0 0.5 %collective-permute-done.refs_0_ = bf16[3,96,128]{2,1,0:T(8,128)(2,1)S(1)} collective-permute-done((bf16[3,96,128]{2,1,0:T(8,128)(2,1)S(1)}, bf16[3,96,128]{2,1,0:T(8,128)(2,1)S(1)}, u32[]{:S(2)}, u32[]{:S(2)}) %collective-permute-start) | collective-permute-done | bytes 73760 | tf_op jit(solution)/shard_map/ppermute | solution.py:261
  12.5 1.2 %collective-permute-start.4 = (bf16[3,96,128]{2,1,0:T(8,128)(2,1)S(1)}, bf16[3,96,128]{2,1,0:T(8,128)(2,1)S(1)}, u32[]{:S(2)}, u32[]{:S(2)}) collective-permute-start(bf16[3,96,128]{2,1,0:T(8,128)(2,1)S(1)} %pack.4.refs_0_), channel_id=1, source_target_pairs={{0,4},{4,0},{8,12},{12,8},{1,5},{5,1},{9,13},{13,9},{2,6},{6,2},{1... | collective-permute-start | bytes 221192 | tf_op jit(solution)/shard_map/ppermute | solution.py:261
  13.7 0.5 %collective-permute-start.3 = (bf16[3,96,128]{2,1,0:T(8,128)(2,1)S(1)}, bf16[3,96,128]{2,1,0:T(8,128)(2,1)S(1)}, u32[]{:S(2)}, u32[]{:S(2)}) collective-permute-start(bf16[3,96,128]{2,1,0:T(8,128)(2,1)S(1)} %collective-permute-done.1.refs_0_.refs_2_), channel_id=1, source_target_pairs={{0,2},{1,3},{2,0},{3,1},{4,6},{5,7},{6,4},{7,5},{8,10},{9,11},{10,... | collective-permute-start | bytes 221192 | tf_op jit(solution)/shard_map/ppermute | solution.py:261
  14.2 2.8 %load.3.refs_2_.refs_1_ = bf16[2,3,1024,1536]{3,2,1,0:T(8,128)(2,1)S(1)} custom-call(bf16[2,3,1024,1536]{3,2,1,0:T(8,128)(2,1)} %refs_0_.1, bf16[3,96,128]{2,1,0:T(8,128)(2,1)S(1)} %pack.4.refs_0_, bf16[2,3,1024,1536]{3,2,1,0:T(8,128)(2,1)S(1)} %load.2.refs_1_), custom_call_target="tpu_custom_call", output_to_operand_aliasing={{}: (2, {})} | custom-call | bytes 6291456 | tf_op jit(solution)/shard_map/load/pallas_call | solution.py:83
  17.0 0.0 collective-permute-done.4.refs_1_
  17.0 1.0 %collective-permute-done.3.refs_3_ = bf16[3,96,128]{2,1,0:T(8,128)(2,1)S(1)} collective-permute-done((bf16[3,96,128]{2,1,0:T(8,128)(2,1)S(1)}, bf16[3,96,128]{2,1,0:T(8,128)(2,1)S(1)}, u32[]{:S(2)}, u32[]{:S(2)}) %collective-permute-start.3) | collective-permute-done | bytes 73760 | tf_op jit(solution)/shard_map/ppermute | solution.py:261
  18.0 0.0 collective-permute-done.2.refs_1_
  18.1 0.1 collective-permute-start.5
  18.2 0.6 %collective-permute-start.6 = (bf16[3,192,128]{2,1,0:T(8,128)(2,1)S(1)}, bf16[3,192,128]{2,1,0:T(8,128)(2,1)S(1)}, u32[]{:S(2)}, u32[]{:S(2)}) collective-permute-start(bf16[3,192,128]{2,1,0:T(8,128)(2,1)S(1)} %pack.5.refs_4_.refs_0_), channel_id=1, source_target_pairs={{0,2},{1,3},{2,0},{3,1},{4,6},{5,7},{6,4},{7,5},{8,10},{9,11},{10,... | collective-permute-start | bytes 442376 | tf_op jit(solution)/shard_map/ppermute | solution.py:261
  18.8 1.5 %collective-permute-done.5.refs_3_.refs_2_ = bf16[3,896,128]{2,1,0:T(8,128)(2,1)S(1)} collective-permute-done((bf16[3,896,128]{2,1,0:T(8,128)(2,1)S(1)}, bf16[3,896,128]{2,1,0:T(8,128)(2,1)S(1)}, u32[]{:S(2)}, u32[]{:S(2)}) %collective-permute-start.5) | collective-permute-done | bytes 688160 | tf_op jit(solution)/shard_map/ppermute | solution.py:261
  20.3 7.3 %merge.2 = (bf16[2,3,1024,1536]{3,2,1,0:T(8,128)(2,1)}, f32[8,128]{1,0:T(8,128)S(1)}, bf16[2,3,1024,1536]{3,2,1,0:T(8,128)(2,1)S(1)}) custom-call(bf16[2,3,1024,1536]{3,2,1,0:T(8,128)(2,1)} %refs_0_.1, bf16[2,3,1024,1536]{3,2,1,0:T(8,128)(2,1)S(1)} %load.3.refs_2_.refs_1_, ...), custom_call_target="tpu_custom_call", output_to_operand_aliasing={{2}: (1, {})} | custom-call | flops 603979776 | bytes 18874368 | tf_op jit(solution)/shard_map/merge/pallas_call | solution.py:221
  27.6 0.0 collective-permute-done.6.refs_1_
  27.6 0.2 collective-permute-start.7
  27.8 1.5 %collective-permute-done.7.refs_4_ = bf16[3,384,128]{2,1,0:T(8,128)(2,1)S(1)} collective-permute-done((bf16[3,384,128]{2,1,0:T(8,128)(2,1)S(1)}, bf16[3,384,128]{2,1,0:T(8,128)(2,1)S(1)}, u32[]{:S(2)}, u32[]{:S(2)}) %collective-permute-start.7) | collective-permute-done | bytes 294944 | tf_op jit(solution)/shard_map/ppermute | solution.py:261
  29.3 5.3 %merge.3 = (bf16[2,3,1024,1536]{3,2,1,0:T(8,128)(2,1)}, f32[8,128]{1,0:T(8,128)}) custom-call(bf16[2,3,1024,1536]{3,2,1,0:T(8,128)(2,1)S(1)} %get-tuple-element.13.refs_0_, bf16[3,896,128]{2,1,0:T(8,128)(2,1)S(1)} %pack.6.refs_2_.refs_1_, bf16[3,896,128]{2,1,0:T(8,128)(2,1)S(1)} %collective-permute-done.5.refs_3_.refs_2_, ...), custom_call_target="tpu_custom_call", output_to_operand_aliasing={{0}: (5, {})} | custom-call | flops 603979776 | bytes 18874368 | tf_op jit(solution)/shard_map/merge/pallas_call | solution.py:221
  (4 shorter events, 0.1 us)
Async XLA Ops:
  1.9 16.2 %collective-permute-start.2 = (bf16[3,352,128]{2,1,0:T(8,128)(2,1)S(1)}, bf16[3,352,128]{2,1,0:T(8,128)(2,1)S(1)}, u32[]{:S(2)}, u32[]{:S(2)}) collective-permute-start(bf16[3,352,128]{2,1,0:T(8,128)(2,1)S(1)} %get-tuple-element.12.refs_0_), channel_id=1, source_target_pairs={{0,2},{1,3},{2,0},{3,1},{4,6},{5,7},{6,4},{7,5},{8,10},{9,11},{10,... | collective-permute-start | bytes 811016 | tf_op jit(solution)/shard_map/ppermute | solution.py:261
  4.9 4.4 %collective-permute-start.1 = (bf16[3,96,128]{2,1,0:T(8,128)(2,1)S(1)}, bf16[3,96,128]{2,1,0:T(8,128)(2,1)S(1)}, u32[]{:S(2)}, u32[]{:S(2)}) collective-permute-start(bf16[3,96,128]{2,1,0:T(8,128)(2,1)S(1)} %get-tuple-element.11), channel_id=1, source_target_pairs={{0,4},{4,0},{8,12},{12,8},{1,5},{5,1},{9,13},{13,9},{2,6},{6,2},{1... | collective-permute-start | bytes 221192 | tf_op jit(solution)/shard_map/ppermute | solution.py:261
  6.4 6.0 %collective-permute-start = (bf16[3,96,128]{2,1,0:T(8,128)(2,1)S(1)}, bf16[3,96,128]{2,1,0:T(8,128)(2,1)S(1)}, u32[]{:S(2)}, u32[]{:S(2)}) collective-permute-start(bf16[3,96,128]{2,1,0:T(8,128)(2,1)S(1)} %get-tuple-element.11), channel_id=1, source_target_pairs={{0,8},{4,12},{8,0},{12,4},{1,9},{5,13},{9,1},{13,5},{2,10},{6,14},... | collective-permute-start | bytes 221192 | tf_op jit(solution)/shard_map/ppermute | solution.py:261
  12.5 4.5 %collective-permute-start.4 = (bf16[3,96,128]{2,1,0:T(8,128)(2,1)S(1)}, bf16[3,96,128]{2,1,0:T(8,128)(2,1)S(1)}, u32[]{:S(2)}, u32[]{:S(2)}) collective-permute-start(bf16[3,96,128]{2,1,0:T(8,128)(2,1)S(1)} %pack.4.refs_0_), channel_id=1, source_target_pairs={{0,4},{4,0},{8,12},{12,8},{1,5},{5,1},{9,13},{13,9},{2,6},{6,2},{1... | collective-permute-start | bytes 221192 | tf_op jit(solution)/shard_map/ppermute | solution.py:261
  13.7 4.4 %collective-permute-start.3 = (bf16[3,96,128]{2,1,0:T(8,128)(2,1)S(1)}, bf16[3,96,128]{2,1,0:T(8,128)(2,1)S(1)}, u32[]{:S(2)}, u32[]{:S(2)}) collective-permute-start(bf16[3,96,128]{2,1,0:T(8,128)(2,1)S(1)} %collective-permute-done.1.refs_0_.refs_2_), channel_id=1, source_target_pairs={{0,2},{1,3},{2,0},{3,1},{4,6},{5,7},{6,4},{7,5},{8,10},{9,11},{10,... | collective-permute-start | bytes 221192 | tf_op jit(solution)/shard_map/ppermute | solution.py:261
  18.1 2.2 %collective-permute-start.5 = (bf16[3,896,128]{2,1,0:T(8,128)(2,1)S(1)}, bf16[3,896,128]{2,1,0:T(8,128)(2,1)S(1)}, u32[]{:S(2)}, u32[]{:S(2)}) collective-permute-start(bf16[3,896,128]{2,1,0:T(8,128)(2,1)S(1)} %pack.6.refs_2_.refs_1_), channel_id=1, source_target_pairs={{0,1},{1,0},{2,3},{3,2},{4,5},{5,4},{6,7},{7,6},{8,9},{9,8},{10,11... | collective-permute-start | bytes 2064392 | tf_op jit(solution)/shard_map/ppermute | solution.py:261
  18.2 9.4 %collective-permute-start.6 = (bf16[3,192,128]{2,1,0:T(8,128)(2,1)S(1)}, bf16[3,192,128]{2,1,0:T(8,128)(2,1)S(1)}, u32[]{:S(2)}, u32[]{:S(2)}) collective-permute-start(bf16[3,192,128]{2,1,0:T(8,128)(2,1)S(1)} %pack.5.refs_4_.refs_0_), channel_id=1, source_target_pairs={{0,2},{1,3},{2,0},{3,1},{4,6},{5,7},{6,4},{7,5},{8,10},{9,11},{10,... | collective-permute-start | bytes 442376 | tf_op jit(solution)/shard_map/ppermute | solution.py:261
  27.6 1.6 %collective-permute-start.7 = (bf16[3,384,128]{2,1,0:T(8,128)(2,1)S(1)}, bf16[3,384,128]{2,1,0:T(8,128)(2,1)S(1)}, u32[]{:S(2)}, u32[]{:S(2)}) collective-permute-start(bf16[3,384,128]{2,1,0:T(8,128)(2,1)S(1)} %pack.7.refs_3_), channel_id=1, source_target_pairs={{0,1},{1,0},{2,3},{3,2},{4,5},{5,4},{6,7},{7,6},{8,9},{9,8},{10,11... | collective-permute-start | bytes 884744 | tf_op jit(solution)/shard_map/ppermute | solution.py:261

commit v8 on v7

--- a/solution.py
+++ b/solution.py
@@ -17,7 +17,14 @@
 vmem_limit = 24 * 2**20
 
 
-def select_kernel(index_ref, narrow_ref, wide_ref, both_out, w_out, index, n_buf, w_buf, index_sem, sems):
+def held_copy(base_ref, held_ref, first, last, sem):
+    rows = pl.ds(first, last - first)
+    return pltpu.make_async_copy(base_ref.at[:, :, rows], held_ref.at[:, :, rows], sem)
+
+
+def select_kernel(early, index_ref, narrow_ref, wide_ref, *refs):
+    both_out, w_out = refs[:2]
+    index, n_buf, w_buf, index_sem, sems, early_sem = refs[-6:]
     experts = index_ref.shape[0]
     rank = narrow_ref.shape[2]
     rows = n_buf.shape[2]
@@ -32,6 +39,10 @@
         n_copies.append(pltpu.make_async_copy(narrow_ref.at[i], n_buf.at[:, ranks], sems.at[e, 0]))
     for copy in w_copies + n_copies:
         copy.start()
+    if early:
+        base_ref, held_ref = refs[2:4]
+        early_copy = held_copy(base_ref, held_ref, 0, early, early_sem)
+        early_copy.start()
     for copy in w_copies:
         copy.wait()
     for p in range(w_buf.shape[0]):
@@ -43,54 +54,61 @@
     for p in range(n_buf.shape[0]):
         n = n_buf[p].astype(jnp.float32) * adapter_scale
         both_out[p, :rows] = n.T.astype(both_out.dtype)
-
-
-def select(narrow, wide, index):
+    if early:
+        early_copy.wait()
+
+
+def select(narrow, wide, index, base=None, early=0):
     experts = index.shape[0]
     _, projections, rank, rows = narrow.shape
     columns = wide.shape[3]
     deep = experts * rank
-    return pl.pallas_call(
-        select_kernel,
-        out_shape=(
-            jax.ShapeDtypeStruct((projections, rows + columns, deep), narrow.dtype),
-            jax.ShapeDtypeStruct((projections, columns, deep), wide.dtype),
-        ),
-        in_specs=[in_hbm] * 3,
-        out_specs=[in_vmem] * 2,
+    operands = [index, narrow, wide] + ([base] if early else [])
+    out_shape = [
+        jax.ShapeDtypeStruct((projections, rows + columns, deep), narrow.dtype),
+        jax.ShapeDtypeStruct((projections, columns, deep), wide.dtype),
+    ] + ([jax.ShapeDtypeStruct(base.shape, base.dtype)] if early else [])
+
+    def kernel(*refs):
+        inputs, outputs, scratch = refs[:3], refs[len(operands) : -6], refs[-6:]
+        select_kernel(early, *inputs, *outputs[:2], *refs[3 : len(operands)], *outputs[2:], *scratch)
+
+    return pl.pallas_call(
+        kernel,
+        out_shape=out_shape,
+        in_specs=[in_hbm] * len(operands),
+        out_specs=[in_vmem] * len(out_shape),
         scratch_shapes=[
             pltpu.SMEM((experts,), index.dtype),
             pltpu.VMEM((projections, deep, rows), narrow.dtype),
             pltpu.VMEM((projections, deep, columns), wide.dtype),
             pltpu.SemaphoreType.DMA,
             pltpu.SemaphoreType.DMA((experts, 2)),
+            pltpu.SemaphoreType.DMA,
         ],
         compiler_params=pltpu.CompilerParams(vmem_limit_bytes=vmem_limit),
         name="select",
-    )(*[pltpu.with_memory_space_constraint(x, pltpu.HBM) for x in (index, narrow, wide)])
-
-
-def load_kernel(p, base_ref, *refs):
-    out_ref, sem = refs[-2:]
-    copy = pltpu.make_async_copy(base_ref.at[:, p], out_ref.at[:, p], sem)
+    )(*[pltpu.with_memory_space_constraint(x, pltpu.HBM) for x in operands])
+
+
+def load_kernel(early, base_ref, _, __, out_ref, sem):
+    copy = held_copy(base_ref, out_ref, early, out_ref.shape[2], sem)
     copy.start()
     copy.wait()
 
 
-def load(base, p, loaded=None, after=()):
-    extra = [*after] + ([] if loaded is None else [loaded])
-    specs = [anywhere] * len(after) + ([] if loaded is None else [in_vmem])
-    return pl.pallas_call(
-        functools.partial(load_kernel, p),
+def load(base, held, early, after):
+    return pl.pallas_call(
+        functools.partial(load_kernel, early),
         out_shape=jax.ShapeDtypeStruct(base.shape, base.dtype),
-        in_specs=[in_hbm] + specs,
+        in_specs=[in_hbm, in_vmem, anywhere],
         out_specs=in_vmem,
         scratch_shapes=[pltpu.SemaphoreType.DMA],
-        input_output_aliases={} if loaded is None else {len(extra): 0},
-        compiler_params=pltpu.CompilerParams(vmem_limit_bytes=vmem_limit),
-        cost_estimate=pl.CostEstimate(flops=0, bytes_accessed=2 * base.size // base.shape[1], transcendentals=0),
+        input_output_aliases={1: 0},
+        compiler_params=pltpu.CompilerParams(vmem_limit_bytes=vmem_limit),
+        cost_estimate=pl.CostEstimate(flops=0, bytes_accessed=2 * base.size, transcendentals=0),
         name="load",
-    )(pltpu.with_memory_space_constraint(base, pltpu.HBM), *extra)
+    )(pltpu.with_memory_space_constraint(base, pltpu.HBM), held, after)
 
 
 def pack_kernel(count, *refs):
@@ -115,10 +133,8 @@
     )(*blocks, *after)
 
 
-def merge_kernel(plan, late, *refs):
-    base_ref, held_ref, *refs = refs if late else (None, *refs)
-    n_all, w_all, out_buf, sems, late_sem = refs[-5:]
-    out_ref, token, held_ref = refs[-8:-5] if late else [*refs[-7:-5], held_ref]
+def merge_kernel(plan, held_ref, *refs):
+    out_ref, token, n_all, w_all, out_buf, sems = refs[-6:]
     experts, projections, width, _ = held_ref.shape
     _, span, deep = w_all.shape
     m_step = tile_rows if width % tile_rows == 0 else width
@@ -126,13 +142,6 @@
     steps = projections * experts
     s, g = lax.axis_index("shard"), lax.axis_index("group")
     lane_expert = lax.broadcasted_iota(jnp.int32, (m_step, deep), 1) // plan.rank
-    first_late = projections - late
-    late_copies = [
-        pltpu.make_async_copy(base_ref.at[:, p], held_ref.at[:, p], late_sem.at[p - first_late])
-        for p in range(first_late, projections)
-    ]
-    for copy in late_copies:
-        copy.start()
 
     def prepare(p, _):
         for i, first, rows, place in plan.n_pieces:
@@ -181,11 +190,7 @@
                 copy.start()
             return 0
 
-        lax.fori_loop(0, first_late * experts, tile, 0)
-        if late:
-            for copy in late_copies:
-                copy.wait()
-            lax.fori_loop(first_late * experts, steps, tile, 0)
+        lax.fori_loop(0, steps, tile, 0)
         for step in range(max(0, steps - out_slots), steps):
             for copy in out_copies(jnp.int32(step)):
                 copy.wait()
@@ -204,33 +209,24 @@
     w_pieces: list
 
 
-def merge(plan, base, held, parts, late=0, out=None, after=()):
+def merge(plan, held, parts, out=None, after=()):
     experts, projections, width, _ = held.shape
     deep = parts[0].shape[-1]
     share = projections * plan.span * experts * width
     extra = [*after] + ([] if out is None else [out])
-    source = [pltpu.with_memory_space_constraint(base, pltpu.HBM)] if late else []
-    operands = [*source, held, *parts, *extra]
-    aliases = {} if out is None else {len(operands) - 1: 0}
-    out_shape = [jax.ShapeDtypeStruct(held.shape, held.dtype), jax.ShapeDtypeStruct((8, 128), jnp.float32)]
-    out_specs = [in_hbm, in_vmem]
-    if late:
-        aliases[1] = 2
-        out_shape.append(jax.ShapeDtypeStruct(held.shape, held.dtype))
-        out_specs.append(in_vmem)
-    return pl.pallas_call(
-        functools.partial(merge_kernel, plan, late),
-        out_shape=out_shape,
-        in_specs=[in_hbm] * len(source) + [in_vmem] * (1 + len(parts)) + [anywhere] * len(extra),
-        out_specs=out_specs,
+    operands = [held, *parts, *extra]
+    return pl.pallas_call(
+        functools.partial(merge_kernel, plan),
+        out_shape=[jax.ShapeDtypeStruct(held.shape, held.dtype), jax.ShapeDtypeStruct((8, 128), jnp.float32)],
+        in_specs=[in_vmem] * (1 + len(parts)) + [anywhere] * len(extra),
+        out_specs=[in_hbm, in_vmem],
         scratch_shapes=[
             pltpu.VMEM((projections, width, deep), held.dtype),
             pltpu.VMEM((projections, plan.span, deep), held.dtype),
             pltpu.VMEM((out_slots, width, plan.span), held.dtype),
             pltpu.SemaphoreType.DMA((out_slots, 2)),
-            pltpu.SemaphoreType.DMA((max(late, 1),)),
         ],
-        input_output_aliases=aliases,
+        input_output_aliases={} if out is None else {len(operands) - 1: 0},
         compiler_params=pltpu.CompilerParams(vmem_limit_bytes=vmem_limit),
         cost_estimate=pl.CostEstimate(flops=2 * share * plan.rank, bytes_accessed=4 * share, transcendentals=0),
         name="merge",
@@ -240,31 +236,27 @@
 def on_device(shards, groups, base, narrow, wide, adapted_expert_index):
     rank = narrow.shape[3]
     rows, columns = narrow.shape[2], wide.shape[3]
-    both, w = select(jnp.swapaxes(narrow, 2, 3), wide, adapted_expert_index)
     axes = ("shard", "group")
+    narrow = jnp.swapaxes(narrow, 2, 3)
 
     if shards != 4 or groups != 4:
+        both, w = select(narrow, wide, adapted_expert_index)
         n = lax.all_gather(both[:, :rows], "group", axis=1, tiled=True)
         w = lax.all_gather(w, axes, axis=1, tiled=True)
         whole = lambda s, g: 0
-        plan = Plan(
-            rank,
-            columns * shards * groups,
-            1,
-            lambda s: 0,
-            [(0, 0, rows * groups, whole)],
-            [(1, 0, columns * shards * groups, whole)],
-        )
-        return merge(plan, None, base, [n, w])[0]
+        n_pieces = [(0, 0, rows * groups, whole)]
+        w_pieces = [(1, 0, columns * shards * groups, whole)]
+        plan = Plan(rank, columns * shards * groups, 1, lambda s: 0, n_pieces, w_pieces)
+        return merge(plan, base, [n, w])[0]
 
     def swap(x, axis, bit):
         return lax.ppermute(x, axis, [(i, i ^ bit) for i in range(4)])
 
-    w2, w1 = [swap(w, "shard", k) for k in (2, 1)]
-    held = load(base, 0, after=(w1,))
-    w2 = pack([w2], (held,))
-    held = load(base, 1, held, (w2,))
-    line = pack([w2, swap(w2, "shard", 1)], (held,))
+    early = rows
+    both, w, held = select(narrow, wide, adapted_expert_index, base, early)
+    w3, w2, w1 = [swap(w, "shard", k) for k in (3, 2, 1)]
+    held = load(base, held, early, w1)
+    line = pack([w2, w3], (held,))
     own_a = pack([both, swap(both, "group", 2), w1, swap(w1, "group", 2)], (line,))
     other_a = swap(own_a, "group", 1)
     line_x = swap(line, "group", 2)
@@ -287,9 +279,9 @@
     near_plan = Plan(rank, span, 2, lambda s: s // 2, n_pieces, near)
     far_plan = Plan(rank, span, 2, lambda s: 1 - s // 2, n_pieces, far)
     parts = [own_a, other_a]
-    out, token, held = merge(near_plan, base, held, parts, 1, after=(line,))
+    out, token = merge(near_plan, held, parts, after=(line,))
     own_b = pack([line, line_x], (token,))
-    return merge(far_plan, None, held, parts + [own_b, swap(own_b, "group", 1)], out=out)[0]
+    return merge(far_plan, held, parts + [own_b, swap(own_b, "group", 1)], out)[0]
 
 
 def solution(mesh):

time: 34.9 us -> 31.3 us (0.90)
  Pallas kernels: 20.1 us -> 18.4 us
  starting transfers between devices: 9.77 us -> 8.43 us
  waiting for transfers between devices: 4.63 us -> 4.26 us
    pallas_call x5 -> x4, Pallas kernels: 20 us -> 18.3 us  [the longest x2 10.1 us: merge(): pl.pallas_call(functools.partial(merge_kernel, plan), out_shape=[jax.Shap...]
    ppermute x8, starting transfers between devices: 9.77 us -> 8.43 us  [swap(): return lax.ppermute(x, axis, [(i, i ^ bit) for i in range(4)])]
    ppermute x8, waiting for transfers between devices: 4.63 us -> 4.26 us  [swap(): return lax.ppermute(x, axis, [(i, i ^ bit) for i in range(4)])]
  transfers between devices with their start and end apart: 8 -> 8, of which waited for: 5 -> 4; matrix products, arithmetic and copies ran while one was open for 0% -> 0% of each run, Pallas kernels for 37% -> 31%
where the time goes in v8:
time: 31.3 us; the launch traced here: 31.2 us
  Pallas kernels  18.4 us (59%)
  starting transfers between devices  8.43 us (27%)
  waiting for transfers between devices  4.26 us (14%)
    pallas_call x2, Pallas kernels, merge(): pl.pallas_call(functools.partial(merge_kernel, plan), out_shape=[jax.Shap...  10.1 us
    ppermute x8, starting transfers between devices, swap(): return lax.ppermute(x, axis, [(i, i ^ bit) for i in range(4)])  8.43 us
    pallas_call x1, Pallas kernels, load(): pl.pallas_call(functools.partial(load_kernel, early), out_shape=jax.Shape...  5.03 us
    ppermute x8, waiting for transfers between devices, swap(): return lax.ppermute(x, axis, [(i, i ^ bit) for i in range(4)])  4.26 us
    pallas_call x1, Pallas kernels, select(): pl.pallas_call(kernel, out_shape=out_shape, in_specs=[in_hbm] * len(opera...  3.21 us
  transfers between devices with their start and end apart: 8, of which 4 were waited for; matrix products, arithmetic and copies ran while one was open for 0% of the time, Pallas kernels for 31%

profile of v8, /device:TPU:0, one launch (start us, length us, event | category | flops | bytes accessed | tf_op | source)
XLA Modules:
  0.0 31.2 jit_solution(5761176941741321397)
XLA Ops:
  0.0 3.2 %select.1 = (bf16[3,352,128]{2,1,0:T(8,128)(2,1)S(1)}, bf16[3,96,128]{2,1,0:T(8,128)(2,1)S(1)}, bf16[2,3,1024,1536]{3,2,1,0:T(8,128)(2,1)S(1)}) custom-call(s32[2]{0:T(128)} %refs_0_.1, bf16[32,3,64,256]{3,2,1,0:T(8,128)(2,1)} %bitcast.1, bf16[32,3,64,96]{3,2,1,0:T(8,128)(2,1)} %refs_2_.1, bf16[2,3,1024,1536]{3,2,1,0:T(8,128)(2,1)} %base_ref.1), custom_call_target="tpu_custom_call" | custom-call | tf_op jit(solution)/shard_map/select/pallas_call | solution.py:76
  3.2 3.0 %collective-permute-start.1 = (bf16[3,352,128]{2,1,0:T(8,128)(2,1)S(1)}, bf16[3,352,128]{2,1,0:T(8,128)(2,1)S(1)}, u32[]{:S(2)}, u32[]{:S(2)}) collective-permute-start(bf16[3,352,128]{2,1,0:T(8,128)(2,1)S(1)} %get-tuple-element.13.refs_0_), channel_id=1, source_target_pairs={{0,2},{1,3},{2,0},{3,1},{4,6},{5,7},{6,4},{7,5},{8,10},{9,11},{10,... | collective-permute-start | bytes 811016 | tf_op jit(solution)/shard_map/ppermute | solution.py:253
  6.2 1.6 %collective-permute-start = (bf16[3,96,128]{2,1,0:T(8,128)(2,1)S(1)}, bf16[3,96,128]{2,1,0:T(8,128)(2,1)S(1)}, u32[]{:S(2)}, u32[]{:S(2)}) collective-permute-start(bf16[3,96,128]{2,1,0:T(8,128)(2,1)S(1)} %get-tuple-element.12), channel_id=1, source_target_pairs={{0,4},{4,0},{8,12},{12,8},{1,5},{5,1},{9,13},{13,9},{2,6},{6,2},{1... | collective-permute-start | bytes 221192 | tf_op jit(solution)/shard_map/ppermute | solution.py:253
  7.8 2.5 %collective-permute-start.4 = (bf16[3,96,128]{2,1,0:T(8,128)(2,1)S(1)}, bf16[3,96,128]{2,1,0:T(8,128)(2,1)S(1)}, u32[]{:S(2)}, u32[]{:S(2)}) collective-permute-start(bf16[3,96,128]{2,1,0:T(8,128)(2,1)S(1)} %get-tuple-element.12), channel_id=1, source_target_pairs={{0,12},{4,8},{8,4},{12,0},{1,13},{5,9},{9,5},{13,1},{2,14},{6,10},... | collective-permute-start | bytes 221192 | tf_op jit(solution)/shard_map/ppermute | solution.py:253
  10.3 0.1 collective-permute-start.3
  10.4 0.2 collective-permute-done.__.refs_2_
  10.6 0.4 %collective-permute-start.2 = (bf16[3,96,128]{2,1,0:T(8,128)(2,1)S(1)}, bf16[3,96,128]{2,1,0:T(8,128)(2,1)S(1)}, u32[]{:S(2)}, u32[]{:S(2)}) collective-permute-start(bf16[3,96,128]{2,1,0:T(8,128)(2,1)S(1)} %collective-permute-done.__.refs_2_), channel_id=1, source_target_pairs={{0,2},{1,3},{2,0},{3,1},{4,6},{5,7},{6,4},{7,5},{8,10},{9,11},{10,... | collective-permute-start | bytes 221192 | tf_op jit(solution)/shard_map/ppermute | solution.py:253
  10.9 5.0 %load.1.refs_2_.held_ref = bf16[2,3,1024,1536]{3,2,1,0:T(8,128)(2,1)S(1)} custom-call(bf16[2,3,1024,1536]{3,2,1,0:T(8,128)(2,1)} %base_ref.1, bf16[2,3,1024,1536]{3,2,1,0:T(8,128)(2,1)S(1)} %get-tuple-element.11._, bf16[3,96,128]{2,1,0:T(8,128)(2,1)S(1)} %collective-permute-done.__.refs_2_), custom_call_target="tpu_custom_call", output_to_operand_aliasing={{}: (1, {})} | custom-call | bytes 18874368 | tf_op jit(solution)/shard_map/load/pallas_call | solution.py:101
  16.0 0.0 collective-permute-done.4.refs_1_
  16.0 1.1 %collective-permute-done.3.refs_0_ = bf16[3,96,128]{2,1,0:T(8,128)(2,1)S(1)} collective-permute-done((bf16[3,96,128]{2,1,0:T(8,128)(2,1)S(1)}, bf16[3,96,128]{2,1,0:T(8,128)(2,1)S(1)}, u32[]{:S(2)}, u32[]{:S(2)}) %collective-permute-start.3) | collective-permute-done | bytes 73760 | tf_op jit(solution)/shard_map/ppermute | solution.py:253
  17.1 0.0 collective-permute-done.2.refs_3_
  17.1 0.0 collective-permute-done.1.refs_1_
  17.2 0.1 collective-permute-start.5
  17.3 0.6 %collective-permute-start.6 = (bf16[3,192,128]{2,1,0:T(8,128)(2,1)S(1)}, bf16[3,192,128]{2,1,0:T(8,128)(2,1)S(1)}, u32[]{:S(2)}, u32[]{:S(2)}) collective-permute-start(bf16[3,192,128]{2,1,0:T(8,128)(2,1)S(1)} %pack.3.refs_4_.refs_2_.refs_0_), channel_id=1, source_target_pairs={{0,2},{1,3},{2,0},{3,1},{4,6},{5,7},{6,4},{7,5},{8,10},{9,11},{10,... | collective-permute-start | bytes 442376 | tf_op jit(solution)/shard_map/ppermute | solution.py:253
  17.9 1.5 %collective-permute-done.5.refs_1_ = bf16[3,896,128]{2,1,0:T(8,128)(2,1)S(1)} collective-permute-done((bf16[3,896,128]{2,1,0:T(8,128)(2,1)S(1)}, bf16[3,896,128]{2,1,0:T(8,128)(2,1)S(1)}, u32[]{:S(2)}, u32[]{:S(2)}) %collective-permute-start.5) | collective-permute-done | bytes 688160 | tf_op jit(solution)/shard_map/ppermute | solution.py:253
  19.4 4.7 %merge.2 = (bf16[2,3,1024,1536]{3,2,1,0:T(8,128)(2,1)}, f32[8,128]{1,0:T(8,128)S(1)}) custom-call(bf16[2,3,1024,1536]{3,2,1,0:T(8,128)(2,1)S(1)} %load.1.refs_2_.held_ref, bf16[3,896,128]{2,1,0:T(8,128)(2,1)S(1)} %pack.4.refs_0_, bf16[3,896,128]{2,1,0:T(8,128)(2,1)S(1)} %collective-permute-done.5.refs_1_, bf16[3,192,128]{2,1,0:T(8,128)(2,1)S(1)} %pack.3.refs_4_.refs_2_.refs_0_), custom_call_target="tpu_custom_call" | custom-call | flops 603979776 | bytes 18874368 | tf_op jit(solution)/shard_map/merge/pallas_call | solution.py:218
  24.2 0.0 collective-permute-done.6.refs_1_
  24.2 0.2 collective-permute-start.7
  24.4 1.4 %collective-permute-done.7.refs_3_ = bf16[3,384,128]{2,1,0:T(8,128)(2,1)S(1)} collective-permute-done((bf16[3,384,128]{2,1,0:T(8,128)(2,1)S(1)}, bf16[3,384,128]{2,1,0:T(8,128)(2,1)S(1)}, u32[]{:S(2)}, u32[]{:S(2)}) %collective-permute-start.7) | collective-permute-done | bytes 294944 | tf_op jit(solution)/shard_map/ppermute | solution.py:253
  25.8 5.3 %merge.3 = (bf16[2,3,1024,1536]{3,2,1,0:T(8,128)(2,1)}, f32[8,128]{1,0:T(8,128)}) custom-call(bf16[2,3,1024,1536]{3,2,1,0:T(8,128)(2,1)S(1)} %load.1.refs_2_.held_ref, bf16[3,896,128]{2,1,0:T(8,128)(2,1)S(1)} %pack.4.refs_0_, bf16[3,896,128]{2,1,0:T(8,128)(2,1)S(1)} %collective-permute-done.5.refs_1_, ...), custom_call_target="tpu_custom_call", output_to_operand_aliasing={{0}: (5, {})} | custom-call | flops 603979776 | bytes 18874368 | tf_op jit(solution)/shard_map/merge/pallas_call | solution.py:218
  (3 shorter events, 0.1 us)
Async XLA Ops:
  3.2 13.9 %collective-permute-start.1 = (bf16[3,352,128]{2,1,0:T(8,128)(2,1)S(1)}, bf16[3,352,128]{2,1,0:T(8,128)(2,1)S(1)}, u32[]{:S(2)}, u32[]{:S(2)}) collective-permute-start(bf16[3,352,128]{2,1,0:T(8,128)(2,1)S(1)} %get-tuple-element.13.refs_0_), channel_id=1, source_target_pairs={{0,2},{1,3},{2,0},{3,1},{4,6},{5,7},{6,4},{7,5},{8,10},{9,11},{10,... | collective-permute-start | bytes 811016 | tf_op jit(solution)/shard_map/ppermute | solution.py:253
  6.2 4.4 %collective-permute-start = (bf16[3,96,128]{2,1,0:T(8,128)(2,1)S(1)}, bf16[3,96,128]{2,1,0:T(8,128)(2,1)S(1)}, u32[]{:S(2)}, u32[]{:S(2)}) collective-permute-start(bf16[3,96,128]{2,1,0:T(8,128)(2,1)S(1)} %get-tuple-element.12), channel_id=1, source_target_pairs={{0,4},{4,0},{8,12},{12,8},{1,5},{5,1},{9,13},{13,9},{2,6},{6,2},{1... | collective-permute-start | bytes 221192 | tf_op jit(solution)/shard_map/ppermute | solution.py:253
  7.8 8.2 %collective-permute-start.4 = (bf16[3,96,128]{2,1,0:T(8,128)(2,1)S(1)}, bf16[3,96,128]{2,1,0:T(8,128)(2,1)S(1)}, u32[]{:S(2)}, u32[]{:S(2)}) collective-permute-start(bf16[3,96,128]{2,1,0:T(8,128)(2,1)S(1)} %get-tuple-element.12), channel_id=1, source_target_pairs={{0,12},{4,8},{8,4},{12,0},{1,13},{5,9},{9,5},{13,1},{2,14},{6,10},... | collective-permute-start | bytes 221192 | tf_op jit(solution)/shard_map/ppermute | solution.py:253
  10.3 6.8 %collective-permute-start.3 = (bf16[3,96,128]{2,1,0:T(8,128)(2,1)S(1)}, bf16[3,96,128]{2,1,0:T(8,128)(2,1)S(1)}, u32[]{:S(2)}, u32[]{:S(2)}) collective-permute-start(bf16[3,96,128]{2,1,0:T(8,128)(2,1)S(1)} %get-tuple-element.12), channel_id=1, source_target_pairs={{0,8},{4,12},{8,0},{12,4},{1,9},{5,13},{9,1},{13,5},{2,10},{6,14},... | collective-permute-start | bytes 221192 | tf_op jit(solution)/shard_map/ppermute | solution.py:253
  10.6 6.5 %collective-permute-start.2 = (bf16[3,96,128]{2,1,0:T(8,128)(2,1)S(1)}, bf16[3,96,128]{2,1,0:T(8,128)(2,1)S(1)}, u32[]{:S(2)}, u32[]{:S(2)}) collective-permute-start(bf16[3,96,128]{2,1,0:T(8,128)(2,1)S(1)} %collective-permute-done.__.refs_2_), channel_id=1, source_target_pairs={{0,2},{1,3},{2,0},{3,1},{4,6},{5,7},{6,4},{7,5},{8,10},{9,11},{10,... | collective-permute-start | bytes 221192 | tf_op jit(solution)/shard_map/ppermute | solution.py:253
  17.2 2.2 %collective-permute-start.5 = (bf16[3,896,128]{2,1,0:T(8,128)(2,1)S(1)}, bf16[3,896,128]{2,1,0:T(8,128)(2,1)S(1)}, u32[]{:S(2)}, u32[]{:S(2)}) collective-permute-start(bf16[3,896,128]{2,1,0:T(8,128)(2,1)S(1)} %pack.4.refs_0_), channel_id=1, source_target_pairs={{0,1},{1,0},{2,3},{3,2},{4,5},{5,4},{6,7},{7,6},{8,9},{9,8},{10,11... | collective-permute-start | bytes 2064392 | tf_op jit(solution)/shard_map/ppermute | solution.py:253
  17.3 6.9 %collective-permute-start.6 = (bf16[3,192,128]{2,1,0:T(8,128)(2,1)S(1)}, bf16[3,192,128]{2,1,0:T(8,128)(2,1)S(1)}, u32[]{:S(2)}, u32[]{:S(2)}) collective-permute-start(bf16[3,192,128]{2,1,0:T(8,128)(2,1)S(1)} %pack.3.refs_4_.refs_2_.refs_0_), channel_id=1, source_target_pairs={{0,2},{1,3},{2,0},{3,1},{4,6},{5,7},{6,4},{7,5},{8,10},{9,11},{10,... | collective-permute-start | bytes 442376 | tf_op jit(solution)/shard_map/ppermute | solution.py:253
  24.2 1.6 %collective-permute-start.7 = (bf16[3,384,128]{2,1,0:T(8,128)(2,1)S(1)}, bf16[3,384,128]{2,1,0:T(8,128)(2,1)S(1)}, u32[]{:S(2)}, u32[]{:S(2)}) collective-permute-start(bf16[3,384,128]{2,1,0:T(8,128)(2,1)S(1)} %pack.5.refs_2_), channel_id=1, source_target_pairs={{0,1},{1,0},{2,3},{3,2},{4,5},{5,4},{6,7},{7,6},{8,9},{9,8},{10,11... | collective-permute-start | bytes 884744 | tf_op jit(solution)/shard_map/ppermute | solution.py:253

commit v9 on v6

v9 whole, which is shorter than its diff:
```python
import functools
import typing

import jax
import jax.numpy as jnp
from jax import lax
from jax.experimental import pallas as pl
from jax.experimental.pallas import tpu as pltpu
from jax.sharding import PartitionSpec as P

adapter_scale = 0.5
out_slots = 4
tile_rows = 512
in_vmem = pl.BlockSpec(memory_space=pltpu.VMEM)
in_hbm = pl.BlockSpec(memory_space=pltpu.HBM)
anywhere = pl.BlockSpec(memory_space=pl.ANY)
vmem_limit = 24 * 2**20


def select_kernel(index_ref, narrow_ref, wide_ref, both_out, w_out, index, n_buf, w_buf, index_sem, sems):
    experts = index_ref.shape[0]
    rank = narrow_ref.shape[2]
    rows = n_buf.shape[2]
    index_copy = pltpu.make_async_copy(index_ref, index, index_sem)
    index_copy.start()
    index_copy.wait()
    n_copies, w_copies = [], []
    for e in range(experts):
        i = index[e]
        ranks = pl.ds(e * rank, rank)
        w_copies.append(pltpu.make_async_copy(wide_ref.at[i], w_buf.at[:, ranks], sems.at[e, 1]))
        n_copies.append(pltpu.make_async_copy(narrow_ref.at[i], n_buf.at[:, ranks], sems.at[e, 0]))
    for copy in w_copies + n_copies:
        copy.start()
    for copy in w_copies:
        copy.wait()
    for p in range(w_buf.shape[0]):
        w = w_buf[p].astype(jnp.float32).T.astype(w_out.dtype)
        w_out[p] = w
        both_out[p, rows:] = w
    for copy in n_copies:
        copy.wait()
    for p in range(n_buf.shape[0]):
        n = n_buf[p].astype(jnp.float32) * adapter_scale
        both_out[p, :rows] = n.T.astype(both_out.dtype)


def select(narrow, wide, index):
    experts = index.shape[0]
    _, projections, rank, rows = narrow.shape
    columns = wide.shape[3]
    deep = experts * rank
    return pl.pallas_call(
        select_kernel,
        out_shape=(
            jax.ShapeDtypeStruct((projections, rows + columns, deep), narrow.dtype),
            jax.ShapeDtypeStruct((projections, columns, deep), wide.dtype),
        ),
        in_specs=[in_hbm] * 3,
        out_specs=[in_vmem] * 2,
        scratch_shapes=[
            pltpu.SMEM((experts,), index.dtype),
            pltpu.VMEM((projections, deep, rows), narrow.dtype),
            pltpu.VMEM((projections, deep, columns), wide.dtype),
            pltpu.SemaphoreType.DMA,
            pltpu.SemaphoreType.DMA((experts, 2)),
        ],
        compiler_params=pltpu.CompilerParams(vmem_limit_bytes=vmem_limit),
        name="select",
    )(*[pltpu.with_memory_space_constraint(x, pltpu.HBM) for x in (index, narrow, wide)])


def load_kernel(first, last, base_ref, *refs):
    out_ref, sem = refs[-2:]
    rows = pl.ds(first, last - first)
    copy = pltpu.make_async_copy(base_ref.at[:, :, rows], out_ref.at[:, :, rows], sem)
    copy.start()
    copy.wait()


def load(base, first, last, after, held=None):
    operands = [pltpu.with_memory_space_constraint(base, pltpu.HBM), after] + ([] if held is None else [held])
    return pl.pallas_call(
        functools.partial(load_kernel, first, last),
        out_shape=jax.ShapeDtypeStruct(base.shape, base.dtype),
        in_specs=[in_hbm, anywhere, in_vmem][: len(operands)],
        out_specs=in_vmem,
        scratch_shapes=[pltpu.SemaphoreType.DMA],
        input_output_aliases={} if held is None else {2: 0},
        compiler_params=pltpu.CompilerParams(vmem_limit_bytes=vmem_limit),
        cost_estimate=pl.CostEstimate(flops=0, bytes_accessed=2 * base.size, transcendentals=0),
        name="load",
    )(*operands)


def pack_kernel(count, *refs):
    out_ref = refs[-1]
    at = 0
    for ref in refs[:count]:
        rows = ref.shape[1]
        out_ref[:, at : at + rows] = ref[...]
        at += rows


def pack(blocks, after=()):
    projections, _, deep = blocks[0].shape
    rows = sum(x.shape[1] for x in blocks)
    return pl.pallas_call(
        functools.partial(pack_kernel, len(blocks)),
        out_shape=jax.ShapeDtypeStruct((projections, rows, deep), blocks[0].dtype),
        in_specs=[in_vmem] * len(blocks) + [anywhere] * len(after),
        out_specs=in_vmem,
        compiler_params=pltpu.CompilerParams(vmem_limit_bytes=vmem_limit),
        name="pack",
    )(*blocks, *after)


def merge_kernel(plan, held_ref, *refs):
    out_ref, n_all, w_all, out_buf, sems = refs[-5:]
    experts, projections, width, wide_columns = held_ref.shape
    deep = n_all.shape[2]
    m_step = out_buf.shape[1]
    f_step = 256 if wide_columns % 256 == 0 else wide_columns
    strips = width // m_step
    tiles = experts * strips
    steps = projections * tiles
    s, g = lax.axis_index("shard"), lax.axis_index("group")
    lane_expert = lax.broadcasted_iota(jnp.int32, (m_step, deep), 1) // plan.rank

    def prepare(p, _):
        for pieces, whole in ((plan.n_pieces, n_all), (plan.w_pieces, w_all)):
            for i, first, rows, place in pieces:
                at = pl.multiple_of(place(s, g) * rows, rows)
                whole[p, pl.ds(at, rows), :] = refs[i][p, pl.ds(first, rows)]
        return 0

    def where(step):
        p, t = step // tiles, lax.rem(step, tiles)
        rows = pl.ds(pl.multiple_of(lax.rem(t, strips) * m_step, m_step), m_step)
        return t // strips, p, rows, lax.rem(step, out_slots)

    def out_copy(step):
        e, p, rows, slot = where(step)
        return pltpu.make_async_copy(out_buf.at[slot], out_ref.at[e, p, rows], sems.at[slot])

    def tile(step, _):
        e, p, rows, slot = where(step)

        @pl.when(step >= out_slots)
        def _():
            out_copy(step - out_slots).wait()

        n = n_all[p, rows, :]
        n = jnp.where(lane_expert == e, n, jnp.zeros_like(n))
        for f in range(0, wide_columns, f_step):
            delta = lax.dot_general(
                n, w_all[p, f : f + f_step], (((1,), (1,)), ((), ())), preferred_element_type=jnp.float32
            )
            b = held_ref[e, p, rows, f : f + f_step].astype(jnp.float32)
            out_buf[slot, :, f : f + f_step] = (b + delta).astype(out_buf.dtype)
        out_copy(step).start()
        return 0

    lax.fori_loop(0, projections, prepare, 0)
    lax.fori_loop(0, steps, tile, 0)
    for step in range(max(0, steps - out_slots), steps):
        out_copy(jnp.int32(step)).wait()


class Plan(typing.NamedTuple):
    rank: int
    n_pieces: list
    w_pieces: list


def merge(plan, held, parts):
    experts, projections, width, wide_columns = held.shape
    deep = parts[0].shape[-1]
    m_step = tile_rows if width % tile_rows == 0 else width
    return pl.pallas_call(
        functools.partial(merge_kernel, plan),
        out_shape=jax.ShapeDtypeStruct(held.shape, held.dtype),
        in_specs=[in_vmem] * (1 + len(parts)),
        out_specs=in_hbm,
        scratch_shapes=[
            pltpu.VMEM((projections, width, deep), held.dtype),
            pltpu.VMEM((projections, wide_columns, deep), held.dtype),
            pltpu.VMEM((out_slots, m_step, wide_columns), held.dtype),
            pltpu.SemaphoreType.DMA((out_slots,)),
        ],
        compiler_params=pltpu.CompilerParams(vmem_limit_bytes=vmem_limit),
        cost_estimate=pl.CostEstimate(
            flops=2 * held.size * plan.rank, bytes_accessed=4 * held.size, transcendentals=0
        ),
        name="merge",
    )(held, *parts)


def on_device(shards, groups, base, narrow, wide, adapted_expert_index):
    rank = narrow.shape[3]
    rows, columns = narrow.shape[2], wide.shape[3]
    axes = ("shard", "group")
    narrow = jnp.swapaxes(narrow, 2, 3)

    if shards != 4 or groups != 4:
        both, w = select(narrow, wide, adapted_expert_index)
        n = lax.all_gather(both[:, :rows], "group", axis=1, tiled=True)
        w = lax.all_gather(w, axes, axis=1, tiled=True)
        whole = lambda s, g: 0
        n_pieces = [(0, 0, rows * groups, whole)]
        w_pieces = [(1, 0, columns * shards * groups, whole)]
        return merge(Plan(rank, n_pieces, w_pieces), base, [n, w])

    def swap(x, axis, bit):
        return lax.ppermute(x, axis, [(i, i ^ bit) for i in range(4)])

    both, w = select(narrow, wide, adapted_expert_index)
    w3, w2, w1 = [swap(w, "shard", k) for k in (3, 2, 1)]
    both_x = swap(pack([both], (w1,)), "group", 2)
    split = base.shape[2] * 3 // 8
    held = load(base, 0, split, w1)
    line = pack([w1, w2, w3], (held,))
    own = pack([both, line])
    held = load(base, split, base.shape[2], line, held)
    both_x = pack([both_x], (held,))
    parts = [own, both_x, swap(line, "group", 2)]
    parts += [swap(x, "group", 1) for x in parts]
    n_pieces, w_pieces = [], []
    for i, m in ((0, 0), (3, 1)):
        n_pieces += [(i, 0, rows, lambda s, g, m=m: g ^ m), (i + 1, 0, rows, lambda s, g, m=m: g ^ m ^ 2)]
        for k in range(4):
            place = lambda s, g, m=m, k=k: (s ^ k) * groups + (g ^ m)
            place_x = lambda s, g, m=m, k=k: (s ^ k) * groups + (g ^ m ^ 2)
            w_pieces.append((i, rows + k * columns, columns, place))
            w_pieces.append((i + 1, rows, columns, place_x) if k == 0 else (i + 2, (k - 1) * columns, columns, place_x))
    return merge(Plan(rank, n_pieces, w_pieces), held, parts)


def solution(mesh):
    return jax.shard_map(
        functools.partial(on_device, mesh.shape["shard"], mesh.shape["group"]),
        mesh=mesh,
        in_specs=(
            P("parts", None, "shard", None),
            P("parts", None, ("shard", "group"), None),
            P("parts", None, None, ("shard", "group")),
            P("parts"),
        ),
        out_specs=P("parts", None, "shard", None),
        check_vma=False,
    )
```

time: 32.1 us -> 32.6 us (1.016)
  waiting for transfers between devices: 2.03 us -> 5.28 us
  Pallas kernels: 20.3 us -> 17.7 us
    ppermute x8, waiting for transfers between devices: 2.03 us -> 5.28 us  [swap(): return lax.ppermute(x, axis, [(i, i ^ bit) for i in range(4)])]
    pallas_call x3, Pallas kernels: 18.3 us -> 15.8 us  [the longest x1 8.38 us: merge(): pl.pallas_call(functools.partial(merge_kernel, plan), out_shape=jax.Shape...]
  transfers between devices with their start and end apart: 8 -> 8, of which waited for: 3 -> 3; matrix products, arithmetic and copies ran while one was open for 0% -> 0% of each run, Pallas kernels for 38% -> 23%
where the time goes in v9:
time: 32.6 us; the launch traced here: 32.3 us
  Pallas kernels  17.7 us (54%)
  starting transfers between devices  9.28 us (28%)
  waiting for transfers between devices  5.28 us (16%)
    ppermute x8, starting transfers between devices, swap(): return lax.ppermute(x, axis, [(i, i ^ bit) for i in range(4)])  9.28 us
    pallas_call x1, Pallas kernels, merge(): pl.pallas_call(functools.partial(merge_kernel, plan), out_shape=jax.Shape...  8.38 us
    pallas_call x2, Pallas kernels, load(): pl.pallas_call(functools.partial(load_kernel, first, last), out_shape=jax...  7.37 us
    ppermute x8, waiting for transfers between devices, swap(): return lax.ppermute(x, axis, [(i, i ^ bit) for i in range(4)])  5.28 us
    pallas_call x1, Pallas kernels, select(): pl.pallas_call(select_kernel, out_shape=(jax.ShapeDtypeStruct((projection...  1.84 us
  transfers between devices with their start and end apart: 8, of which 3 were waited for; matrix products, arithmetic and copies ran while one was open for 0% of the time, Pallas kernels for 23%

profile of v9, /device:TPU:0, one launch (start us, length us, event | category | flops | bytes accessed | tf_op | source)
XLA Modules:
  0.0 32.3 jit_solution(15566820502876400549)
XLA Ops:
  0.0 1.8 %select.1 = (bf16[3,352,128]{2,1,0:T(8,128)(2,1)S(1)}, bf16[3,96,128]{2,1,0:T(8,128)(2,1)S(1)}) custom-call(s32[2]{0:T(128)} %index_ref.1, bf16[32,3,64,256]{3,2,1,0:T(8,128)(2,1)} %bitcast.1, bf16[32,3,64,96]{3,2,1,0:T(8,128)(2,1)} %wide_ref.1), custom_call_target="tpu_custom_call" | custom-call | tf_op jit(solution)/shard_map/select/pallas_call | solution.py:53
  1.9 3.1 %collective-permute-start = (bf16[3,96,128]{2,1,0:T(8,128)(2,1)S(1)}, bf16[3,96,128]{2,1,0:T(8,128)(2,1)S(1)}, u32[]{:S(2)}, u32[]{:S(2)}) collective-permute-start(bf16[3,96,128]{2,1,0:T(8,128)(2,1)S(1)} %get-tuple-element.7), channel_id=1, source_target_pairs={{0,4},{4,0},{8,12},{12,8},{1,5},{5,1},{9,13},{13,9},{2,6},{6,2},{1... | collective-permute-start | bytes 221192 | tf_op jit(solution)/shard_map/ppermute | solution.py:215
  4.9 2.5 %collective-permute-start.2 = (bf16[3,96,128]{2,1,0:T(8,128)(2,1)S(1)}, bf16[3,96,128]{2,1,0:T(8,128)(2,1)S(1)}, u32[]{:S(2)}, u32[]{:S(2)}) collective-permute-start(bf16[3,96,128]{2,1,0:T(8,128)(2,1)S(1)} %get-tuple-element.7), channel_id=1, source_target_pairs={{0,12},{4,8},{8,4},{12,0},{1,13},{5,9},{9,5},{13,1},{2,14},{6,10},... | collective-permute-start | bytes 221192 | tf_op jit(solution)/shard_map/ppermute | solution.py:215
  7.4 0.1 collective-permute-start.1
  7.5 0.0 collective-permute-done.refs_0_.refs_1_
  7.6 1.7 %collective-permute-start.3 = (bf16[3,352,128]{2,1,0:T(8,128)(2,1)S(1)}, bf16[3,352,128]{2,1,0:T(8,128)(2,1)S(1)}, u32[]{:S(2)}, u32[]{:S(2)}) collective-permute-start(bf16[3,352,128]{2,1,0:T(8,128)(2,1)S(1)} %pack.6), channel_id=1, source_target_pairs={{0,2},{1,3},{2,0},{3,1},{4,6},{5,7},{6,4},{7,5},{8,10},{9,11},{10,... | collective-permute-start | bytes 811016 | tf_op jit(solution)/shard_map/ppermute | solution.py:215
  9.3 3.0 %load.2.refs_3_.refs_1_ = bf16[2,3,1024,1536]{3,2,1,0:T(8,128)(2,1)S(1)} custom-call(bf16[2,3,1024,1536]{3,2,1,0:T(8,128)(2,1)} %base_ref.3, bf16[3,96,128]{2,1,0:T(8,128)(2,1)S(1)} %collective-permute-done.refs_0_.refs_1_), custom_call_target="tpu_custom_call" | custom-call | bytes 18874368 | tf_op jit(solution)/shard_map/load/pallas_call | solution.py:83
  12.3 0.0 collective-permute-done.2.refs_2_
  12.3 2.1 %collective-permute-done.1.refs_1_ = bf16[3,96,128]{2,1,0:T(8,128)(2,1)S(1)} collective-permute-done((bf16[3,96,128]{2,1,0:T(8,128)(2,1)S(1)}, bf16[3,96,128]{2,1,0:T(8,128)(2,1)S(1)}, u32[]{:S(2)}, u32[]{:S(2)}) %collective-permute-start.1) | collective-permute-done | bytes 73760 | tf_op jit(solution)/shard_map/ppermute | solution.py:215
  14.5 0.1 collective-permute-start.5
  14.6 1.6 %collective-permute-start.4 = (bf16[3,288,128]{2,1,0:T(8,128)(2,1)S(1)}, bf16[3,288,128]{2,1,0:T(8,128)(2,1)S(1)}, u32[]{:S(2)}, u32[]{:S(2)}) collective-permute-start(bf16[3,288,128]{2,1,0:T(8,128)(2,1)S(1)} %pack.4.refs_0_.refs_1_), channel_id=1, source_target_pairs={{0,2},{1,3},{2,0},{3,1},{4,6},{5,7},{6,4},{7,5},{8,10},{9,11},{10,... | collective-permute-start | bytes 663560 | tf_op jit(solution)/shard_map/ppermute | solution.py:215
  16.2 4.4 %load.3.refs_1_.held_ref = bf16[2,3,1024,1536]{3,2,1,0:T(8,128)(2,1)S(1)} custom-call(bf16[2,3,1024,1536]{3,2,1,0:T(8,128)(2,1)} %base_ref.3, bf16[3,288,128]{2,1,0:T(8,128)(2,1)S(1)} %pack.4.refs_0_.refs_1_, bf16[2,3,1024,1536]{3,2,1,0:T(8,128)(2,1)S(1)} %load.2.refs_3_.refs_1_), custom_call_target="tpu_custom_call", output_to_operand_aliasing={{}: (2, {})} | custom-call | bytes 18874368 | tf_op jit(solution)/shard_map/load/pallas_call | solution.py:83
  20.5 0.0 collective-permute-done.3.refs_0_
  20.6 0.2 collective-permute-start.6
  20.8 1.7 %collective-permute-done.4.refs_2_ = bf16[3,288,128]{2,1,0:T(8,128)(2,1)S(1)} collective-permute-done((bf16[3,288,128]{2,1,0:T(8,128)(2,1)S(1)}, bf16[3,288,128]{2,1,0:T(8,128)(2,1)S(1)}, u32[]{:S(2)}, u32[]{:S(2)}) %collective-permute-start.4) | collective-permute-done | bytes 221216 | tf_op jit(solution)/shard_map/ppermute | solution.py:215
  22.5 0.0 collective-permute-start.7
  22.5 1.5 %collective-permute-done.7.refs_5_ = bf16[3,288,128]{2,1,0:T(8,128)(2,1)S(1)} collective-permute-done((bf16[3,288,128]{2,1,0:T(8,128)(2,1)S(1)}, bf16[3,288,128]{2,1,0:T(8,128)(2,1)S(1)}, u32[]{:S(2)}, u32[]{:S(2)}) %collective-permute-start.7) | collective-permute-done | bytes 221216 | tf_op jit(solution)/shard_map/ppermute | solution.py:215
  23.9 0.0 collective-permute-done.5.refs_3_
  23.9 0.0 collective-permute-done.6.refs_4_
  23.9 8.4 %merge.1 = bf16[2,3,1024,1536]{3,2,1,0:T(8,128)(2,1)} custom-call(bf16[2,3,1024,1536]{3,2,1,0:T(8,128)(2,1)S(1)} %load.3.refs_1_.held_ref, bf16[3,640,128]{2,1,0:T(8,128)(2,1)S(1)} %pack.5.refs_0_, bf16[3,352,128]{2,1,0:T(8,128)(2,1)S(1)} %pack.7.refs_1_, bf16[3,288,128]{2,1,0:T(8,128)(2,1)S(1)} %collective-permute-done.4.refs_2_, ...), custom_call_target="tpu_custom_call" | custom-call | flops 1207959552 | bytes 37748736 | tf_op jit(solution)/shard_map/merge/pallas_call | solution.py:180
  (4 shorter events, 0.1 us)
Async XLA Ops:
  1.9 5.7 %collective-permute-start = (bf16[3,96,128]{2,1,0:T(8,128)(2,1)S(1)}, bf16[3,96,128]{2,1,0:T(8,128)(2,1)S(1)}, u32[]{:S(2)}, u32[]{:S(2)}) collective-permute-start(bf16[3,96,128]{2,1,0:T(8,128)(2,1)S(1)} %get-tuple-element.7), channel_id=1, source_target_pairs={{0,4},{4,0},{8,12},{12,8},{1,5},{5,1},{9,13},{13,9},{2,6},{6,2},{1... | collective-permute-start | bytes 221192 | tf_op jit(solution)/shard_map/ppermute | solution.py:215
  4.9 7.4 %collective-permute-start.2 = (bf16[3,96,128]{2,1,0:T(8,128)(2,1)S(1)}, bf16[3,96,128]{2,1,0:T(8,128)(2,1)S(1)}, u32[]{:S(2)}, u32[]{:S(2)}) collective-permute-start(bf16[3,96,128]{2,1,0:T(8,128)(2,1)S(1)} %get-tuple-element.7), channel_id=1, source_target_pairs={{0,12},{4,8},{8,4},{12,0},{1,13},{5,9},{9,5},{13,1},{2,14},{6,10},... | collective-permute-start | bytes 221192 | tf_op jit(solution)/shard_map/ppermute | solution.py:215
  7.4 7.1 %collective-permute-start.1 = (bf16[3,96,128]{2,1,0:T(8,128)(2,1)S(1)}, bf16[3,96,128]{2,1,0:T(8,128)(2,1)S(1)}, u32[]{:S(2)}, u32[]{:S(2)}) collective-permute-start(bf16[3,96,128]{2,1,0:T(8,128)(2,1)S(1)} %get-tuple-element.7), channel_id=1, source_target_pairs={{0,8},{4,12},{8,0},{12,4},{1,9},{5,13},{9,1},{13,5},{2,10},{6,14},... | collective-permute-start | bytes 221192 | tf_op jit(solution)/shard_map/ppermute | solution.py:215
  7.6 13.0 %collective-permute-start.3 = (bf16[3,352,128]{2,1,0:T(8,128)(2,1)S(1)}, bf16[3,352,128]{2,1,0:T(8,128)(2,1)S(1)}, u32[]{:S(2)}, u32[]{:S(2)}) collective-permute-start(bf16[3,352,128]{2,1,0:T(8,128)(2,1)S(1)} %pack.6), channel_id=1, source_target_pairs={{0,2},{1,3},{2,0},{3,1},{4,6},{5,7},{6,4},{7,5},{8,10},{9,11},{10,... | collective-permute-start | bytes 811016 | tf_op jit(solution)/shard_map/ppermute | solution.py:215
  14.5 9.4 %collective-permute-start.5 = (bf16[3,640,128]{2,1,0:T(8,128)(2,1)S(1)}, bf16[3,640,128]{2,1,0:T(8,128)(2,1)S(1)}, u32[]{:S(2)}, u32[]{:S(2)}) collective-permute-start(bf16[3,640,128]{2,1,0:T(8,128)(2,1)S(1)} %pack.5.refs_0_), channel_id=1, source_target_pairs={{0,1},{1,0},{2,3},{3,2},{4,5},{5,4},{6,7},{7,6},{8,9},{9,8},{10,11... | collective-permute-start | bytes 1474568 | tf_op jit(solution)/shard_map/ppermute | solution.py:215
  14.6 7.8 %collective-permute-start.4 = (bf16[3,288,128]{2,1,0:T(8,128)(2,1)S(1)}, bf16[3,288,128]{2,1,0:T(8,128)(2,1)S(1)}, u32[]{:S(2)}, u32[]{:S(2)}) collective-permute-start(bf16[3,288,128]{2,1,0:T(8,128)(2,1)S(1)} %pack.4.refs_0_.refs_1_), channel_id=1, source_target_pairs={{0,2},{1,3},{2,0},{3,1},{4,6},{5,7},{6,4},{7,5},{8,10},{9,11},{10,... | collective-permute-start | bytes 663560 | tf_op jit(solution)/shard_map/ppermute | solution.py:215
  20.6 3.4 %collective-permute-start.6 = (bf16[3,352,128]{2,1,0:T(8,128)(2,1)S(1)}, bf16[3,352,128]{2,1,0:T(8,128)(2,1)S(1)}, u32[]{:S(2)}, u32[]{:S(2)}) collective-permute-start(bf16[3,352,128]{2,1,0:T(8,128)(2,1)S(1)} %pack.7.refs_1_), channel_id=1, source_target_pairs={{0,1},{1,0},{2,3},{3,2},{4,5},{5,4},{6,7},{7,6},{8,9},{9,8},{10,11... | collective-permute-start | bytes 811016 | tf_op jit(solution)/shard_map/ppermute | solution.py:215
  22.5 1.5 %collective-permute-start.7 = (bf16[3,288,128]{2,1,0:T(8,128)(2,1)S(1)}, bf16[3,288,128]{2,1,0:T(8,128)(2,1)S(1)}, u32[]{:S(2)}, u32[]{:S(2)}) collective-permute-start(bf16[3,288,128]{2,1,0:T(8,128)(2,1)S(1)} %collective-permute-done.4.refs_2_), channel_id=1, source_target_pairs={{0,1},{1,0},{2,3},{3,2},{4,5},{5,4},{6,7},{7,6},{8,9},{9,8},{10,11... | collective-permute-start | bytes 663560 | tf_op jit(solution)/shard_map/ppermute | solution.py:215

commit v10 on v8

--- a/solution.py
+++ b/solution.py
@@ -17,14 +17,7 @@
 vmem_limit = 24 * 2**20
 
 
-def held_copy(base_ref, held_ref, first, last, sem):
-    rows = pl.ds(first, last - first)
-    return pltpu.make_async_copy(base_ref.at[:, :, rows], held_ref.at[:, :, rows], sem)
-
-
-def select_kernel(early, index_ref, narrow_ref, wide_ref, *refs):
-    both_out, w_out = refs[:2]
-    index, n_buf, w_buf, index_sem, sems, early_sem = refs[-6:]
+def select_kernel(index_ref, narrow_ref, wide_ref, both_out, w_out, index, n_buf, w_buf, index_sem, sems):
     experts = index_ref.shape[0]
     rank = narrow_ref.shape[2]
     rows = n_buf.shape[2]
@@ -39,10 +32,6 @@
         n_copies.append(pltpu.make_async_copy(narrow_ref.at[i], n_buf.at[:, ranks], sems.at[e, 0]))
     for copy in w_copies + n_copies:
         copy.start()
-    if early:
-        base_ref, held_ref = refs[2:4]
-        early_copy = held_copy(base_ref, held_ref, 0, early, early_sem)
-        early_copy.start()
     for copy in w_copies:
         copy.wait()
     for p in range(w_buf.shape[0]):
@@ -54,61 +43,62 @@
     for p in range(n_buf.shape[0]):
         n = n_buf[p].astype(jnp.float32) * adapter_scale
         both_out[p, :rows] = n.T.astype(both_out.dtype)
-    if early:
-        early_copy.wait()
-
-
-def select(narrow, wide, index, base=None, early=0):
+
+
+def select(narrow, wide, index):
     experts = index.shape[0]
     _, projections, rank, rows = narrow.shape
     columns = wide.shape[3]
     deep = experts * rank
-    operands = [index, narrow, wide] + ([base] if early else [])
-    out_shape = [
-        jax.ShapeDtypeStruct((projections, rows + columns, deep), narrow.dtype),
-        jax.ShapeDtypeStruct((projections, columns, deep), wide.dtype),
-    ] + ([jax.ShapeDtypeStruct(base.shape, base.dtype)] if early else [])
-
-    def kernel(*refs):
-        inputs, outputs, scratch = refs[:3], refs[len(operands) : -6], refs[-6:]
-        select_kernel(early, *inputs, *outputs[:2], *refs[3 : len(operands)], *outputs[2:], *scratch)
-
-    return pl.pallas_call(
-        kernel,
-        out_shape=out_shape,
-        in_specs=[in_hbm] * len(operands),
-        out_specs=[in_vmem] * len(out_shape),
+    return pl.pallas_call(
+        select_kernel,
+        out_shape=(
+            jax.ShapeDtypeStruct((projections, rows + columns, deep), narrow.dtype),
+            jax.ShapeDtypeStruct((projections, columns, deep), wide.dtype),
+        ),
+        in_specs=[in_hbm] * 3,
+        out_specs=[in_vmem] * 2,
         scratch_shapes=[
             pltpu.SMEM((experts,), index.dtype),
             pltpu.VMEM((projections, deep, rows), narrow.dtype),
             pltpu.VMEM((projections, deep, columns), wide.dtype),
             pltpu.SemaphoreType.DMA,
             pltpu.SemaphoreType.DMA((experts, 2)),
-            pltpu.SemaphoreType.DMA,
         ],
         compiler_params=pltpu.CompilerParams(vmem_limit_bytes=vmem_limit),
         name="select",
-    )(*[pltpu.with_memory_space_constraint(x, pltpu.HBM) for x in operands])
-
-
-def load_kernel(early, base_ref, _, __, out_ref, sem):
-    copy = held_copy(base_ref, out_ref, early, out_ref.shape[2], sem)
-    copy.start()
-    copy.wait()
-
-
-def load(base, held, early, after):
-    return pl.pallas_call(
-        functools.partial(load_kernel, early),
+    )(*[pltpu.with_memory_space_constraint(x, pltpu.HBM) for x in (index, narrow, wide)])
+
+
+def load_kernel(blocks, base_ref, *refs):
+    out_ref, sems = refs[-2:]
+    s = lax.axis_index("shard")
+    copies = []
+    for n, (chunk, span, first, last) in enumerate(blocks):
+        columns = pl.ds(pl.multiple_of(chunk(s) * span, span), span)
+        rows = pl.ds(first, last - first)
+        copies.append(
+            pltpu.make_async_copy(base_ref.at[:, :, rows, columns], out_ref.at[:, :, rows, columns], sems.at[n])
+        )
+    for copy in copies:
+        copy.start()
+    for copy in copies:
+        copy.wait()
+
+
+def load(base, blocks, after, held=None):
+    operands = [pltpu.with_memory_space_constraint(base, pltpu.HBM), after] + ([] if held is None else [held])
+    return pl.pallas_call(
+        functools.partial(load_kernel, blocks),
         out_shape=jax.ShapeDtypeStruct(base.shape, base.dtype),
-        in_specs=[in_hbm, in_vmem, anywhere],
+        in_specs=[in_hbm, anywhere, in_vmem][: len(operands)],
         out_specs=in_vmem,
-        scratch_shapes=[pltpu.SemaphoreType.DMA],
-        input_output_aliases={1: 0},
+        scratch_shapes=[pltpu.SemaphoreType.DMA((len(blocks),))],
+        input_output_aliases={} if held is None else {2: 0},
         compiler_params=pltpu.CompilerParams(vmem_limit_bytes=vmem_limit),
         cost_estimate=pl.CostEstimate(flops=0, bytes_accessed=2 * base.size, transcendentals=0),
         name="load",
-    )(pltpu.with_memory_space_constraint(base, pltpu.HBM), held, after)
+    )(*operands)
 
 
 def pack_kernel(count, *refs):
@@ -252,10 +242,13 @@
     def swap(x, axis, bit):
         return lax.ppermute(x, axis, [(i, i ^ bit) for i in range(4)])
 
-    early = rows
-    both, w, held = select(narrow, wide, adapted_expert_index, base, early)
+    both, w = select(narrow, wide, adapted_expert_index)
     w3, w2, w1 = [swap(w, "shard", k) for k in (3, 2, 1)]
-    held = load(base, held, early, w1)
+    width = base.shape[2]
+    split = width * 11 // 16
+    span = 2 * columns * groups
+    near_half, far_half = lambda s: s // 2, lambda s: 1 - s // 2
+    held = load(base, [(near_half, span, 0, width), (far_half, span, 0, split)], w1)
     line = pack([w2, w3], (held,))
     own_a = pack([both, swap(both, "group", 2), w1, swap(w1, "group", 2)], (line,))
     other_a = swap(own_a, "group", 1)
@@ -275,12 +268,12 @@
         near += [w_piece(i, 2 * half, 1, m), w_piece(i, 2 * half + columns, 1, m ^ 2)]
         for at, k in ((0, 2), (1, 3)):
             far += [w_piece(i + 2, at * columns, k, m), w_piece(i + 2, (at + 2) * columns, k, m ^ 2)]
-    span = 2 * columns * groups
-    near_plan = Plan(rank, span, 2, lambda s: s // 2, n_pieces, near)
-    far_plan = Plan(rank, span, 2, lambda s: 1 - s // 2, n_pieces, far)
+    near_plan = Plan(rank, span, 2, near_half, n_pieces, near)
+    far_plan = Plan(rank, span, 2, far_half, n_pieces, far)
     parts = [own_a, other_a]
     out, token = merge(near_plan, held, parts, after=(line,))
     own_b = pack([line, line_x], (token,))
+    held = load(base, [(far_half, span, split, width)], own_b, held)
     return merge(far_plan, held, parts + [own_b, swap(own_b, "group", 1)], out)[0]
 
 

time: 31.3 us -> 30.5 us (0.974)
  waiting for transfers between devices: 4.26 us -> 1.72 us
  Pallas kernels: 18.4 us -> 19.5 us
  starting transfers between devices: 8.43 us -> 8.98 us
    ppermute x8, waiting for transfers between devices: 4.26 us -> 1.72 us  [swap(): return lax.ppermute(x, axis, [(i, i ^ bit) for i in range(4)])]
    pallas_call x2 -> x3, Pallas kernels: 8.24 us -> 9.3 us  [the longest x2 7.45 us: load(): pl.pallas_call(functools.partial(load_kernel, blocks), out_shape=jax.Shap...]
    ppermute x8, starting transfers between devices: 8.43 us -> 8.98 us  [swap(): return lax.ppermute(x, axis, [(i, i ^ bit) for i in range(4)])]
  transfers between devices with their start and end apart: 8 -> 8, of which waited for: 4 -> 3; matrix products, arithmetic and copies ran while one was open for 0% -> 0% of each run, Pallas kernels for 31% -> 40%
where the time goes in v10:
time: 30.5 us; the launch traced here: 30.3 us
  Pallas kernels  19.5 us (64%)
  starting transfers between devices  8.98 us (29%)
  waiting for transfers between devices  1.72 us (6%)
    pallas_call x2, Pallas kernels, merge(): pl.pallas_call(functools.partial(merge_kernel, plan), out_shape=[jax.Shap...  10.1 us
    ppermute x8, starting transfers between devices, swap(): return lax.ppermute(x, axis, [(i, i ^ bit) for i in range(4)])  8.98 us
    pallas_call x2, Pallas kernels, load(): pl.pallas_call(functools.partial(load_kernel, blocks), out_shape=jax.Shap...  7.45 us
    pallas_call x1, Pallas kernels, select(): pl.pallas_call(select_kernel, out_shape=(jax.ShapeDtypeStruct((projection...  1.84 us
    ppermute x8, waiting for transfers between devices, swap(): return lax.ppermute(x, axis, [(i, i ^ bit) for i in range(4)])  1.72 us
  transfers between devices with their start and end apart: 8, of which 3 were waited for; matrix products, arithmetic and copies ran while one was open for 0% of the time, Pallas kernels for 40%

profile of v10, /device:TPU:0, one launch (start us, length us, event | category | flops | bytes accessed | tf_op | source)
XLA Modules:
  0.0 30.3 jit_solution(6528018934466731529)
XLA Ops:
  0.0 1.8 %select.1 = (bf16[3,352,128]{2,1,0:T(8,128)(2,1)S(1)}, bf16[3,96,128]{2,1,0:T(8,128)(2,1)S(1)}) custom-call(s32[2]{0:T(128)} %index_ref.1, bf16[32,3,64,256]{3,2,1,0:T(8,128)(2,1)} %bitcast.1, bf16[32,3,64,96]{3,2,1,0:T(8,128)(2,1)} %wide_ref.1), custom_call_target="tpu_custom_call" | custom-call | tf_op jit(solution)/shard_map/select/pallas_call | solution.py:53
  1.9 3.0 %collective-permute-start.4 = (bf16[3,352,128]{2,1,0:T(8,128)(2,1)S(1)}, bf16[3,352,128]{2,1,0:T(8,128)(2,1)S(1)}, u32[]{:S(2)}, u32[]{:S(2)}) collective-permute-start(bf16[3,352,128]{2,1,0:T(8,128)(2,1)S(1)} %get-tuple-element.11.refs_0_), channel_id=1, source_target_pairs={{0,2},{1,3},{2,0},{3,1},{4,6},{5,7},{6,4},{7,5},{8,10},{9,11},{10,... | collective-permute-start | bytes 811016 | tf_op jit(solution)/shard_map/ppermute | solution.py:243
  4.9 1.6 %collective-permute-start.2 = (bf16[3,96,128]{2,1,0:T(8,128)(2,1)S(1)}, bf16[3,96,128]{2,1,0:T(8,128)(2,1)S(1)}, u32[]{:S(2)}, u32[]{:S(2)}) collective-permute-start(bf16[3,96,128]{2,1,0:T(8,128)(2,1)S(1)} %get-tuple-element.10), channel_id=1, source_target_pairs={{0,4},{4,0},{8,12},{12,8},{1,5},{5,1},{9,13},{13,9},{2,6},{6,2},{1... | collective-permute-start | bytes 221192 | tf_op jit(solution)/shard_map/ppermute | solution.py:243
  6.4 2.5 %collective-permute-start.1 = (bf16[3,96,128]{2,1,0:T(8,128)(2,1)S(1)}, bf16[3,96,128]{2,1,0:T(8,128)(2,1)S(1)}, u32[]{:S(2)}, u32[]{:S(2)}) collective-permute-start(bf16[3,96,128]{2,1,0:T(8,128)(2,1)S(1)} %get-tuple-element.10), channel_id=1, source_target_pairs={{0,12},{4,8},{8,4},{12,0},{1,13},{5,9},{9,5},{13,1},{2,14},{6,10},... | collective-permute-start | bytes 221192 | tf_op jit(solution)/shard_map/ppermute | solution.py:243
  8.9 0.1 collective-permute-start
  9.0 0.2 collective-permute-done.2.refs_0_.refs_2_
  9.2 0.4 %collective-permute-start.5 = (bf16[3,96,128]{2,1,0:T(8,128)(2,1)S(1)}, bf16[3,96,128]{2,1,0:T(8,128)(2,1)S(1)}, u32[]{:S(2)}, u32[]{:S(2)}) collective-permute-start(bf16[3,96,128]{2,1,0:T(8,128)(2,1)S(1)} %collective-permute-done.2.refs_0_.refs_2_), channel_id=1, source_target_pairs={{0,2},{1,3},{2,0},{3,1},{4,6},{5,7},{6,4},{7,5},{8,10},{9,11},{10,... | collective-permute-start | bytes 221192 | tf_op jit(solution)/shard_map/ppermute | solution.py:243
  9.6 5.6 %load.2.refs_2_.held_ref.refs_1_ = bf16[2,3,1024,1536]{3,2,1,0:T(8,128)(2,1)S(1)} custom-call(bf16[2,3,1024,1536]{3,2,1,0:T(8,128)(2,1)} %base_ref.3, bf16[3,96,128]{2,1,0:T(8,128)(2,1)S(1)} %collective-permute-done.2.refs_0_.refs_2_), custom_call_target="tpu_custom_call" | custom-call | bytes 18874368 | tf_op jit(solution)/shard_map/load/pallas_call | solution.py:91
  15.2 0.0 collective-permute-done.1.refs_1_
  15.2 0.6 %collective-permute-done.refs_0_ = bf16[3,96,128]{2,1,0:T(8,128)(2,1)S(1)} collective-permute-done((bf16[3,96,128]{2,1,0:T(8,128)(2,1)S(1)}, bf16[3,96,128]{2,1,0:T(8,128)(2,1)S(1)}, u32[]{:S(2)}, u32[]{:S(2)}) %collective-permute-start) | collective-permute-done | bytes 73760 | tf_op jit(solution)/shard_map/ppermute | solution.py:243
  15.7 0.0 collective-permute-done.5.refs_3_
  15.8 0.0 collective-permute-done.4.refs_1_
  15.8 0.1 collective-permute-start.6
  15.9 1.2 %collective-permute-start.3 = (bf16[3,192,128]{2,1,0:T(8,128)(2,1)S(1)}, bf16[3,192,128]{2,1,0:T(8,128)(2,1)S(1)}, u32[]{:S(2)}, u32[]{:S(2)}) collective-permute-start(bf16[3,192,128]{2,1,0:T(8,128)(2,1)S(1)} %pack.3.refs_4_.refs_2_.refs_0_), channel_id=1, source_target_pairs={{0,2},{1,3},{2,0},{3,1},{4,6},{5,7},{6,4},{7,5},{8,10},{9,11},{10,... | collective-permute-start | bytes 442376 | tf_op jit(solution)/shard_map/ppermute | solution.py:243
  17.1 0.9 %collective-permute-done.6.refs_1_ = bf16[3,896,128]{2,1,0:T(8,128)(2,1)S(1)} collective-permute-done((bf16[3,896,128]{2,1,0:T(8,128)(2,1)S(1)}, bf16[3,896,128]{2,1,0:T(8,128)(2,1)S(1)}, u32[]{:S(2)}, u32[]{:S(2)}) %collective-permute-start.6) | collective-permute-done | bytes 688160 | tf_op jit(solution)/shard_map/ppermute | solution.py:243
  18.0 4.7 %merge.2 = (bf16[2,3,1024,1536]{3,2,1,0:T(8,128)(2,1)}, f32[8,128]{1,0:T(8,128)S(1)}) custom-call(bf16[2,3,1024,1536]{3,2,1,0:T(8,128)(2,1)S(1)} %load.2.refs_2_.held_ref.refs_1_, bf16[3,896,128]{2,1,0:T(8,128)(2,1)S(1)} %pack.4.refs_0_, bf16[3,896,128]{2,1,0:T(8,128)(2,1)S(1)} %collective-permute-done.6.refs_1_, ...), custom_call_target="tpu_custom_call" | custom-call | flops 603979776 | bytes 18874368 | tf_op jit(solution)/shard_map/merge/pallas_call | solution.py:208
  22.8 0.0 collective-permute-done.3.refs_1_
  22.8 0.2 collective-permute-start.7
  23.0 1.9 %load.3.held_ref = bf16[2,3,1024,1536]{3,2,1,0:T(8,128)(2,1)S(1)} custom-call(bf16[2,3,1024,1536]{3,2,1,0:T(8,128)(2,1)} %base_ref.3, bf16[3,384,128]{2,1,0:T(8,128)(2,1)S(1)} %pack.5.refs_0_.refs_2_, bf16[2,3,1024,1536]{3,2,1,0:T(8,128)(2,1)S(1)} %load.2.refs_2_.held_ref.refs_1_), custom_call_target="tpu_custom_call", output_to_operand_aliasing={{}: (2, {})} | custom-call | bytes 18874368 | tf_op jit(solution)/shard_map/load/pallas_call | solution.py:91
  24.9 0.0 collective-permute-done.7.refs_3_
  24.9 5.4 %merge.3 = (bf16[2,3,1024,1536]{3,2,1,0:T(8,128)(2,1)}, f32[8,128]{1,0:T(8,128)}) custom-call(bf16[2,3,1024,1536]{3,2,1,0:T(8,128)(2,1)S(1)} %load.3.held_ref, bf16[3,896,128]{2,1,0:T(8,128)(2,1)S(1)} %pack.4.refs_0_, bf16[3,896,128]{2,1,0:T(8,128)(2,1)S(1)} %collective-permute-done.6.refs_1_, ...), custom_call_target="tpu_custom_call", output_to_operand_aliasing={{0}: (5, {})} | custom-call | flops 603979776 | bytes 18874368 | tf_op jit(solution)/shard_map/merge/pallas_call | solution.py:208
  (3 shorter events, 0.1 us)
Async XLA Ops:
  1.9 13.9 %collective-permute-start.4 = (bf16[3,352,128]{2,1,0:T(8,128)(2,1)S(1)}, bf16[3,352,128]{2,1,0:T(8,128)(2,1)S(1)}, u32[]{:S(2)}, u32[]{:S(2)}) collective-permute-start(bf16[3,352,128]{2,1,0:T(8,128)(2,1)S(1)} %get-tuple-element.11.refs_0_), channel_id=1, source_target_pairs={{0,2},{1,3},{2,0},{3,1},{4,6},{5,7},{6,4},{7,5},{8,10},{9,11},{10,... | collective-permute-start | bytes 811016 | tf_op jit(solution)/shard_map/ppermute | solution.py:243
  4.9 4.4 %collective-permute-start.2 = (bf16[3,96,128]{2,1,0:T(8,128)(2,1)S(1)}, bf16[3,96,128]{2,1,0:T(8,128)(2,1)S(1)}, u32[]{:S(2)}, u32[]{:S(2)}) collective-permute-start(bf16[3,96,128]{2,1,0:T(8,128)(2,1)S(1)} %get-tuple-element.10), channel_id=1, source_target_pairs={{0,4},{4,0},{8,12},{12,8},{1,5},{5,1},{9,13},{13,9},{2,6},{6,2},{1... | collective-permute-start | bytes 221192 | tf_op jit(solution)/shard_map/ppermute | solution.py:243
  6.4 8.7 %collective-permute-start.1 = (bf16[3,96,128]{2,1,0:T(8,128)(2,1)S(1)}, bf16[3,96,128]{2,1,0:T(8,128)(2,1)S(1)}, u32[]{:S(2)}, u32[]{:S(2)}) collective-permute-start(bf16[3,96,128]{2,1,0:T(8,128)(2,1)S(1)} %get-tuple-element.10), channel_id=1, source_target_pairs={{0,12},{4,8},{8,4},{12,0},{1,13},{5,9},{9,5},{13,1},{2,14},{6,10},... | collective-permute-start | bytes 221192 | tf_op jit(solution)/shard_map/ppermute | solution.py:243
  8.9 6.8 %collective-permute-start = (bf16[3,96,128]{2,1,0:T(8,128)(2,1)S(1)}, bf16[3,96,128]{2,1,0:T(8,128)(2,1)S(1)}, u32[]{:S(2)}, u32[]{:S(2)}) collective-permute-start(bf16[3,96,128]{2,1,0:T(8,128)(2,1)S(1)} %get-tuple-element.10), channel_id=1, source_target_pairs={{0,8},{4,12},{8,0},{12,4},{1,9},{5,13},{9,1},{13,5},{2,10},{6,14},... | collective-permute-start | bytes 221192 | tf_op jit(solution)/shard_map/ppermute | solution.py:243
  9.2 6.5 %collective-permute-start.5 = (bf16[3,96,128]{2,1,0:T(8,128)(2,1)S(1)}, bf16[3,96,128]{2,1,0:T(8,128)(2,1)S(1)}, u32[]{:S(2)}, u32[]{:S(2)}) collective-permute-start(bf16[3,96,128]{2,1,0:T(8,128)(2,1)S(1)} %collective-permute-done.2.refs_0_.refs_2_), channel_id=1, source_target_pairs={{0,2},{1,3},{2,0},{3,1},{4,6},{5,7},{6,4},{7,5},{8,10},{9,11},{10,... | collective-permute-start | bytes 221192 | tf_op jit(solution)/shard_map/ppermute | solution.py:243
  15.8 2.2 %collective-permute-start.6 = (bf16[3,896,128]{2,1,0:T(8,128)(2,1)S(1)}, bf16[3,896,128]{2,1,0:T(8,128)(2,1)S(1)}, u32[]{:S(2)}, u32[]{:S(2)}) collective-permute-start(bf16[3,896,128]{2,1,0:T(8,128)(2,1)S(1)} %pack.4.refs_0_), channel_id=1, source_target_pairs={{0,1},{1,0},{2,3},{3,2},{4,5},{5,4},{6,7},{7,6},{8,9},{9,8},{10,11... | collective-permute-start | bytes 2064392 | tf_op jit(solution)/shard_map/ppermute | solution.py:243
  15.9 6.9 %collective-permute-start.3 = (bf16[3,192,128]{2,1,0:T(8,128)(2,1)S(1)}, bf16[3,192,128]{2,1,0:T(8,128)(2,1)S(1)}, u32[]{:S(2)}, u32[]{:S(2)}) collective-permute-start(bf16[3,192,128]{2,1,0:T(8,128)(2,1)S(1)} %pack.3.refs_4_.refs_2_.refs_0_), channel_id=1, source_target_pairs={{0,2},{1,3},{2,0},{3,1},{4,6},{5,7},{6,4},{7,5},{8,10},{9,11},{10,... | collective-permute-start | bytes 442376 | tf_op jit(solution)/shard_map/ppermute | solution.py:243
  22.8 2.1 %collective-permute-start.7 = (bf16[3,384,128]{2,1,0:T(8,128)(2,1)S(1)}, bf16[3,384,128]{2,1,0:T(8,128)(2,1)S(1)}, u32[]{:S(2)}, u32[]{:S(2)}) collective-permute-start(bf16[3,384,128]{2,1,0:T(8,128)(2,1)S(1)} %pack.5.refs_0_.refs_2_), channel_id=1, source_target_pairs={{0,1},{1,0},{2,3},{3,2},{4,5},{5,4},{6,7},{7,6},{8,9},{9,8},{10,11... | collective-permute-start | bytes 884744 | tf_op jit(solution)/shard_map/ppermute | solution.py:243

commit v11 on v10

--- a/solution.py
+++ b/solution.py
@@ -35,14 +35,13 @@
     for copy in w_copies:
         copy.wait()
     for p in range(w_buf.shape[0]):
-        w = w_buf[p].astype(jnp.float32).T.astype(w_out.dtype)
+        w = w_buf[p].T
         w_out[p] = w
         both_out[p, rows:] = w
     for copy in n_copies:
         copy.wait()
     for p in range(n_buf.shape[0]):
-        n = n_buf[p].astype(jnp.float32) * adapter_scale
-        both_out[p, :rows] = n.T.astype(both_out.dtype)
+        both_out[p, :rows] = (n_buf[p] * adapter_scale).T
 
 
 def select(narrow, wide, index):
@@ -133,16 +132,13 @@
     s, g = lax.axis_index("shard"), lax.axis_index("group")
     lane_expert = lax.broadcasted_iota(jnp.int32, (m_step, deep), 1) // plan.rank
 
-    def prepare(p, _):
+    def prepare(p):
         for i, first, rows, place in plan.n_pieces:
             at = pl.multiple_of(place(s, g) * rows, rows)
             n_all[p, pl.ds(at, rows), :] = refs[i][p, pl.ds(first, rows)]
         for i, first, rows, place in plan.w_pieces:
             at = pl.multiple_of(place(s, g) * rows, rows)
             w_all[p, pl.ds(at, rows), :] = refs[i][p, pl.ds(first, rows)]
-        return 0
-
-    lax.fori_loop(0, projections, prepare, 0)
 
     def merge_chunk(first_column):
         columns = pl.ds(first_column, span)
@@ -162,6 +158,7 @@
         def tile(step, _):
             p, e = step // experts, lax.rem(step, experts)
             slot = lax.rem(step, out_slots)
+            pl.when(e == 0)(lambda: prepare(p))
 
             @pl.when(step >= out_slots)
             def _():

time: 30.5 us -> 30.5 us (level)
  no operation moved by 1% of the time
where the time goes in v11:
time: 30.5 us; the launch traced here: 30.3 us
  Pallas kernels  19.5 us (64%)
  starting transfers between devices  8.98 us (29%)
  waiting for transfers between devices  1.72 us (6%)
    pallas_call x2, Pallas kernels, merge(): pl.pallas_call(functools.partial(merge_kernel, plan), out_shape=[jax.Shap...  10.2 us
    ppermute x8, starting transfers between devices, swap(): return lax.ppermute(x, axis, [(i, i ^ bit) for i in range(4)])  8.98 us
    pallas_call x2, Pallas kernels, load(): pl.pallas_call(functools.partial(load_kernel, blocks), out_shape=jax.Shap...  7.45 us
    pallas_call x1, Pallas kernels, select(): pl.pallas_call(select_kernel, out_shape=(jax.ShapeDtypeStruct((projection...  1.81 us
    ppermute x8, waiting for transfers between devices, swap(): return lax.ppermute(x, axis, [(i, i ^ bit) for i in range(4)])  1.72 us
  transfers between devices with their start and end apart: 8, of which 3 were waited for; matrix products, arithmetic and copies ran while one was open for 0% of the time, Pallas kernels for 40%

profile of v11, /device:TPU:0, one launch (start us, length us, event | category | flops | bytes accessed | tf_op | source)
XLA Modules:
  0.0 30.3 jit_solution(8472904748258865536)
XLA Ops:
  0.0 1.8 %select.1 = (bf16[3,352,128]{2,1,0:T(8,128)(2,1)S(1)}, bf16[3,96,128]{2,1,0:T(8,128)(2,1)S(1)}) custom-call(s32[2]{0:T(128)} %index_ref.1, bf16[32,3,64,256]{3,2,1,0:T(8,128)(2,1)} %bitcast.1, bf16[32,3,64,96]{3,2,1,0:T(8,128)(2,1)} %wide_ref.1), custom_call_target="tpu_custom_call" | custom-call | tf_op jit(solution)/shard_map/select/pallas_call | solution.py:52
  1.8 3.0 %collective-permute-start.4 = (bf16[3,352,128]{2,1,0:T(8,128)(2,1)S(1)}, bf16[3,352,128]{2,1,0:T(8,128)(2,1)S(1)}, u32[]{:S(2)}, u32[]{:S(2)}) collective-permute-start(bf16[3,352,128]{2,1,0:T(8,128)(2,1)S(1)} %get-tuple-element.11.refs_0_), channel_id=1, source_target_pairs={{0,2},{1,3},{2,0},{3,1},{4,6},{5,7},{6,4},{7,5},{8,10},{9,11},{10,... | collective-permute-start | bytes 811016 | tf_op jit(solution)/shard_map/ppermute | solution.py:240
  4.8 1.6 %collective-permute-start.2 = (bf16[3,96,128]{2,1,0:T(8,128)(2,1)S(1)}, bf16[3,96,128]{2,1,0:T(8,128)(2,1)S(1)}, u32[]{:S(2)}, u32[]{:S(2)}) collective-permute-start(bf16[3,96,128]{2,1,0:T(8,128)(2,1)S(1)} %get-tuple-element.10), channel_id=1, source_target_pairs={{0,4},{4,0},{8,12},{12,8},{1,5},{5,1},{9,13},{13,9},{2,6},{6,2},{1... | collective-permute-start | bytes 221192 | tf_op jit(solution)/shard_map/ppermute | solution.py:240
  6.4 2.5 %collective-permute-start.1 = (bf16[3,96,128]{2,1,0:T(8,128)(2,1)S(1)}, bf16[3,96,128]{2,1,0:T(8,128)(2,1)S(1)}, u32[]{:S(2)}, u32[]{:S(2)}) collective-permute-start(bf16[3,96,128]{2,1,0:T(8,128)(2,1)S(1)} %get-tuple-element.10), channel_id=1, source_target_pairs={{0,12},{4,8},{8,4},{12,0},{1,13},{5,9},{9,5},{13,1},{2,14},{6,10},... | collective-permute-start | bytes 221192 | tf_op jit(solution)/shard_map/ppermute | solution.py:240
  8.9 0.1 collective-permute-start
  9.0 0.2 collective-permute-done.2.refs_0_.refs_2_
  9.2 0.4 %collective-permute-start.5 = (bf16[3,96,128]{2,1,0:T(8,128)(2,1)S(1)}, bf16[3,96,128]{2,1,0:T(8,128)(2,1)S(1)}, u32[]{:S(2)}, u32[]{:S(2)}) collective-permute-start(bf16[3,96,128]{2,1,0:T(8,128)(2,1)S(1)} %collective-permute-done.2.refs_0_.refs_2_), channel_id=1, source_target_pairs={{0,2},{1,3},{2,0},{3,1},{4,6},{5,7},{6,4},{7,5},{8,10},{9,11},{10,... | collective-permute-start | bytes 221192 | tf_op jit(solution)/shard_map/ppermute | solution.py:240
  9.5 5.6 %load.2.refs_2_.held_ref.refs_1_ = bf16[2,3,1024,1536]{3,2,1,0:T(8,128)(2,1)S(1)} custom-call(bf16[2,3,1024,1536]{3,2,1,0:T(8,128)(2,1)} %base_ref.3, bf16[3,96,128]{2,1,0:T(8,128)(2,1)S(1)} %collective-permute-done.2.refs_0_.refs_2_), custom_call_target="tpu_custom_call" | custom-call | bytes 18874368 | tf_op jit(solution)/shard_map/load/pallas_call | solution.py:90
  15.1 0.0 collective-permute-done.1.refs_1_
  15.1 0.6 %collective-permute-done.refs_0_ = bf16[3,96,128]{2,1,0:T(8,128)(2,1)S(1)} collective-permute-done((bf16[3,96,128]{2,1,0:T(8,128)(2,1)S(1)}, bf16[3,96,128]{2,1,0:T(8,128)(2,1)S(1)}, u32[]{:S(2)}, u32[]{:S(2)}) %collective-permute-start) | collective-permute-done | bytes 73760 | tf_op jit(solution)/shard_map/ppermute | solution.py:240
  15.7 0.0 collective-permute-done.5.refs_3_
  15.7 0.0 collective-permute-done.4.refs_1_
  15.8 0.1 collective-permute-start.6
  15.9 1.2 %collective-permute-start.3 = (bf16[3,192,128]{2,1,0:T(8,128)(2,1)S(1)}, bf16[3,192,128]{2,1,0:T(8,128)(2,1)S(1)}, u32[]{:S(2)}, u32[]{:S(2)}) collective-permute-start(bf16[3,192,128]{2,1,0:T(8,128)(2,1)S(1)} %pack.3.refs_4_.refs_2_.refs_0_), channel_id=1, source_target_pairs={{0,2},{1,3},{2,0},{3,1},{4,6},{5,7},{6,4},{7,5},{8,10},{9,11},{10,... | collective-permute-start | bytes 442376 | tf_op jit(solution)/shard_map/ppermute | solution.py:240
  17.1 0.9 %collective-permute-done.6.refs_1_ = bf16[3,896,128]{2,1,0:T(8,128)(2,1)S(1)} collective-permute-done((bf16[3,896,128]{2,1,0:T(8,128)(2,1)S(1)}, bf16[3,896,128]{2,1,0:T(8,128)(2,1)S(1)}, u32[]{:S(2)}, u32[]{:S(2)}) %collective-permute-start.6) | collective-permute-done | bytes 688160 | tf_op jit(solution)/shard_map/ppermute | solution.py:240
  18.0 4.8 %merge.2 = (bf16[2,3,1024,1536]{3,2,1,0:T(8,128)(2,1)}, f32[8,128]{1,0:T(8,128)S(1)}) custom-call(bf16[2,3,1024,1536]{3,2,1,0:T(8,128)(2,1)S(1)} %load.2.refs_2_.held_ref.refs_1_, bf16[3,896,128]{2,1,0:T(8,128)(2,1)S(1)} %pack.4.refs_0_, bf16[3,896,128]{2,1,0:T(8,128)(2,1)S(1)} %collective-permute-done.6.refs_1_, ...), custom_call_target="tpu_custom_call" | custom-call | flops 603979776 | bytes 18874368 | tf_op jit(solution)/shard_map/merge/pallas_call | solution.py:205
  22.8 0.0 collective-permute-done.3.refs_1_
  22.8 0.2 collective-permute-start.7
  23.0 1.9 %load.3.held_ref = bf16[2,3,1024,1536]{3,2,1,0:T(8,128)(2,1)S(1)} custom-call(bf16[2,3,1024,1536]{3,2,1,0:T(8,128)(2,1)} %base_ref.3, bf16[3,384,128]{2,1,0:T(8,128)(2,1)S(1)} %pack.5.refs_0_.refs_2_, bf16[2,3,1024,1536]{3,2,1,0:T(8,128)(2,1)S(1)} %load.2.refs_2_.held_ref.refs_1_), custom_call_target="tpu_custom_call", output_to_operand_aliasing={{}: (2, {})} | custom-call | bytes 18874368 | tf_op jit(solution)/shard_map/load/pallas_call | solution.py:90
  24.9 0.0 collective-permute-done.7.refs_3_
  24.9 5.4 %merge.3 = (bf16[2,3,1024,1536]{3,2,1,0:T(8,128)(2,1)}, f32[8,128]{1,0:T(8,128)}) custom-call(bf16[2,3,1024,1536]{3,2,1,0:T(8,128)(2,1)S(1)} %load.3.held_ref, bf16[3,896,128]{2,1,0:T(8,128)(2,1)S(1)} %pack.4.refs_0_, bf16[3,896,128]{2,1,0:T(8,128)(2,1)S(1)} %collective-permute-done.6.refs_1_, ...), custom_call_target="tpu_custom_call", output_to_operand_aliasing={{0}: (5, {})} | custom-call | flops 603979776 | bytes 18874368 | tf_op jit(solution)/shard_map/merge/pallas_call | solution.py:205
  (3 shorter events, 0.1 us)
Async XLA Ops:
  1.8 13.9 %collective-permute-start.4 = (bf16[3,352,128]{2,1,0:T(8,128)(2,1)S(1)}, bf16[3,352,128]{2,1,0:T(8,128)(2,1)S(1)}, u32[]{:S(2)}, u32[]{:S(2)}) collective-permute-start(bf16[3,352,128]{2,1,0:T(8,128)(2,1)S(1)} %get-tuple-element.11.refs_0_), channel_id=1, source_target_pairs={{0,2},{1,3},{2,0},{3,1},{4,6},{5,7},{6,4},{7,5},{8,10},{9,11},{10,... | collective-permute-start | bytes 811016 | tf_op jit(solution)/shard_map/ppermute | solution.py:240
  4.8 4.4 %collective-permute-start.2 = (bf16[3,96,128]{2,1,0:T(8,128)(2,1)S(1)}, bf16[3,96,128]{2,1,0:T(8,128)(2,1)S(1)}, u32[]{:S(2)}, u32[]{:S(2)}) collective-permute-start(bf16[3,96,128]{2,1,0:T(8,128)(2,1)S(1)} %get-tuple-element.10), channel_id=1, source_target_pairs={{0,4},{4,0},{8,12},{12,8},{1,5},{5,1},{9,13},{13,9},{2,6},{6,2},{1... | collective-permute-start | bytes 221192 | tf_op jit(solution)/shard_map/ppermute | solution.py:240
  6.4 8.7 %collective-permute-start.1 = (bf16[3,96,128]{2,1,0:T(8,128)(2,1)S(1)}, bf16[3,96,128]{2,1,0:T(8,128)(2,1)S(1)}, u32[]{:S(2)}, u32[]{:S(2)}) collective-permute-start(bf16[3,96,128]{2,1,0:T(8,128)(2,1)S(1)} %get-tuple-element.10), channel_id=1, source_target_pairs={{0,12},{4,8},{8,4},{12,0},{1,13},{5,9},{9,5},{13,1},{2,14},{6,10},... | collective-permute-start | bytes 221192 | tf_op jit(solution)/shard_map/ppermute | solution.py:240
  8.9 6.8 %collective-permute-start = (bf16[3,96,128]{2,1,0:T(8,128)(2,1)S(1)}, bf16[3,96,128]{2,1,0:T(8,128)(2,1)S(1)}, u32[]{:S(2)}, u32[]{:S(2)}) collective-permute-start(bf16[3,96,128]{2,1,0:T(8,128)(2,1)S(1)} %get-tuple-element.10), channel_id=1, source_target_pairs={{0,8},{4,12},{8,0},{12,4},{1,9},{5,13},{9,1},{13,5},{2,10},{6,14},... | collective-permute-start | bytes 221192 | tf_op jit(solution)/shard_map/ppermute | solution.py:240
  9.2 6.5 %collective-permute-start.5 = (bf16[3,96,128]{2,1,0:T(8,128)(2,1)S(1)}, bf16[3,96,128]{2,1,0:T(8,128)(2,1)S(1)}, u32[]{:S(2)}, u32[]{:S(2)}) collective-permute-start(bf16[3,96,128]{2,1,0:T(8,128)(2,1)S(1)} %collective-permute-done.2.refs_0_.refs_2_), channel_id=1, source_target_pairs={{0,2},{1,3},{2,0},{3,1},{4,6},{5,7},{6,4},{7,5},{8,10},{9,11},{10,... | collective-permute-start | bytes 221192 | tf_op jit(solution)/shard_map/ppermute | solution.py:240
  15.8 2.2 %collective-permute-start.6 = (bf16[3,896,128]{2,1,0:T(8,128)(2,1)S(1)}, bf16[3,896,128]{2,1,0:T(8,128)(2,1)S(1)}, u32[]{:S(2)}, u32[]{:S(2)}) collective-permute-start(bf16[3,896,128]{2,1,0:T(8,128)(2,1)S(1)} %pack.4.refs_0_), channel_id=1, source_target_pairs={{0,1},{1,0},{2,3},{3,2},{4,5},{5,4},{6,7},{7,6},{8,9},{9,8},{10,11... | collective-permute-start | bytes 2064392 | tf_op jit(solution)/shard_map/ppermute | solution.py:240
  15.9 6.9 %collective-permute-start.3 = (bf16[3,192,128]{2,1,0:T(8,128)(2,1)S(1)}, bf16[3,192,128]{2,1,0:T(8,128)(2,1)S(1)}, u32[]{:S(2)}, u32[]{:S(2)}) collective-permute-start(bf16[3,192,128]{2,1,0:T(8,128)(2,1)S(1)} %pack.3.refs_4_.refs_2_.refs_0_), channel_id=1, source_target_pairs={{0,2},{1,3},{2,0},{3,1},{4,6},{5,7},{6,4},{7,5},{8,10},{9,11},{10,... | collective-permute-start | bytes 442376 | tf_op jit(solution)/shard_map/ppermute | solution.py:240
  22.8 2.1 %collective-permute-start.7 = (bf16[3,384,128]{2,1,0:T(8,128)(2,1)S(1)}, bf16[3,384,128]{2,1,0:T(8,128)(2,1)S(1)}, u32[]{:S(2)}, u32[]{:S(2)}) collective-permute-start(bf16[3,384,128]{2,1,0:T(8,128)(2,1)S(1)} %pack.5.refs_0_.refs_2_), channel_id=1, source_target_pairs={{0,1},{1,0},{2,3},{3,2},{4,5},{5,4},{6,7},{7,6},{8,9},{9,8},{10,11... | collective-permute-start | bytes 884744 | tf_op jit(solution)/shard_map/ppermute | solution.py:240

commit v12 on v11

--- a/solution.py
+++ b/solution.py
@@ -123,22 +123,24 @@
 
 
 def merge_kernel(plan, held_ref, *refs):
-    out_ref, token, n_all, w_all, out_buf, sems = refs[-6:]
+    out_ref, token, n_all, w_rows, w_all, out_buf, sems = refs[-7:]
     experts, projections, width, _ = held_ref.shape
-    _, span, deep = w_all.shape
+    deep, span = w_all.shape
     m_step = tile_rows if width % tile_rows == 0 else width
     f_step = 256 if span % 256 == 0 else span
     steps = projections * experts
     s, g = lax.axis_index("shard"), lax.axis_index("group")
-    lane_expert = lax.broadcasted_iota(jnp.int32, (m_step, deep), 1) // plan.rank
+    lane_expert = lax.broadcasted_iota(jnp.int32, (width, deep), 1) // plan.rank
 
     def prepare(p):
         for i, first, rows, place in plan.n_pieces:
             at = pl.multiple_of(place(s, g) * rows, rows)
-            n_all[p, pl.ds(at, rows), :] = refs[i][p, pl.ds(first, rows)]
+            n_all[pl.ds(at, rows), :] = refs[i][p, pl.ds(first, rows)]
         for i, first, rows, place in plan.w_pieces:
             at = pl.multiple_of(place(s, g) * rows, rows)
-            w_all[p, pl.ds(at, rows), :] = refs[i][p, pl.ds(first, rows)]
+            w_rows[pl.ds(at, rows), :] = refs[i][p, pl.ds(first, rows)]
+        for f in range(0, span, f_step):
+            w_all[:, f : f + f_step] = w_rows[f : f + f_step].T
 
     def merge_chunk(first_column):
         columns = pl.ds(first_column, span)
@@ -165,15 +167,13 @@
                 for copy in out_copies(step - out_slots):
                     copy.wait()
 
-            for copy, m in zip(out_copies(step), range(0, width, m_step)):
-                n = n_all[p, m : m + m_step, :]
-                n = jnp.where(lane_expert == e, n, jnp.zeros_like(n))
-                for f in range(0, span, f_step):
-                    delta = lax.dot_general(
-                        n, w_all[p, f : f + f_step], (((1,), (1,)), ((), ())), preferred_element_type=jnp.float32
-                    )
-                    b = held_ref[e, p, m : m + m_step, first_column + f : first_column + f + f_step]
-                    out_buf[slot, m : m + m_step, f : f + f_step] = (b.astype(jnp.float32) + delta).astype(out_buf.dtype)
+            n = n_all[...]
+            n = jnp.where(lane_expert == e, n, jnp.zeros_like(n))
+            for f in range(0, span, f_step):
+                delta = jnp.dot(n, w_all[:, f : f + f_step], preferred_element_type=jnp.float32)
+                b = held_ref[e, p, :, first_column + f : first_column + f + f_step].astype(jnp.float32)
+                out_buf[slot, :, f : f + f_step] = (b + delta).astype(out_buf.dtype)
+            for copy in out_copies(step):
                 copy.start()
             return 0
 
@@ -208,8 +208,9 @@
         in_specs=[in_vmem] * (1 + len(parts)) + [anywhere] * len(extra),
         out_specs=[in_hbm, in_vmem],
         scratch_shapes=[
-            pltpu.VMEM((projections, width, deep), held.dtype),
-            pltpu.VMEM((projections, plan.span, deep), held.dtype),
+            pltpu.VMEM((width, deep), held.dtype),
+            pltpu.VMEM((plan.span, deep), held.dtype),
+            pltpu.VMEM((deep, plan.span), held.dtype),
             pltpu.VMEM((out_slots, width, plan.span), held.dtype),
             pltpu.SemaphoreType.DMA((out_slots, 2)),
         ],

time: 30.5 us -> 30.9 us (1.013)
  Pallas kernels: 19.5 us -> 20 us
    pallas_call x2, Pallas kernels: 10.2 us -> 10.6 us  [merge(): pl.pallas_call(functools.partial(merge_kernel, plan), out_shape=[jax.Shap...]
where the time goes in v12:
time: 30.9 us; the launch traced here: 30.8 us
  Pallas kernels  20 us (65%)
  starting transfers between devices  8.98 us (29%)
  waiting for transfers between devices  1.72 us (6%)
    pallas_call x2, Pallas kernels, merge(): pl.pallas_call(functools.partial(merge_kernel, plan), out_shape=[jax.Shap...  10.6 us
    ppermute x8, starting transfers between devices, swap(): return lax.ppermute(x, axis, [(i, i ^ bit) for i in range(4)])  8.98 us
    pallas_call x2, Pallas kernels, load(): pl.pallas_call(functools.partial(load_kernel, blocks), out_shape=jax.Shap...  7.45 us
    pallas_call x1, Pallas kernels, select(): pl.pallas_call(select_kernel, out_shape=(jax.ShapeDtypeStruct((projection...  1.81 us
    ppermute x8, waiting for transfers between devices, swap(): return lax.ppermute(x, axis, [(i, i ^ bit) for i in range(4)])  1.72 us
  transfers between devices with their start and end apart: 8, of which 3 were waited for; matrix products, arithmetic and copies ran while one was open for 0% of the time, Pallas kernels for 40%

profile of v12, /device:TPU:0, one launch (start us, length us, event | category | flops | bytes accessed | tf_op | source)
XLA Modules:
  0.0 30.8 jit_solution(15102672737368738538)
XLA Ops:
  0.0 1.8 %select.1 = (bf16[3,352,128]{2,1,0:T(8,128)(2,1)S(1)}, bf16[3,96,128]{2,1,0:T(8,128)(2,1)S(1)}) custom-call(s32[2]{0:T(128)} %index_ref.1, bf16[32,3,64,256]{3,2,1,0:T(8,128)(2,1)} %bitcast.1, bf16[32,3,64,96]{3,2,1,0:T(8,128)(2,1)} %wide_ref.1), custom_call_target="tpu_custom_call" | custom-call | tf_op jit(solution)/shard_map/select/pallas_call | solution.py:52
  1.8 3.0 %collective-permute-start.4 = (bf16[3,352,128]{2,1,0:T(8,128)(2,1)S(1)}, bf16[3,352,128]{2,1,0:T(8,128)(2,1)S(1)}, u32[]{:S(2)}, u32[]{:S(2)}) collective-permute-start(bf16[3,352,128]{2,1,0:T(8,128)(2,1)S(1)} %get-tuple-element.11.refs_0_), channel_id=1, source_target_pairs={{0,2},{1,3},{2,0},{3,1},{4,6},{5,7},{6,4},{7,5},{8,10},{9,11},{10,... | collective-permute-start | bytes 811016 | tf_op jit(solution)/shard_map/ppermute | solution.py:241
  4.8 1.6 %collective-permute-start.2 = (bf16[3,96,128]{2,1,0:T(8,128)(2,1)S(1)}, bf16[3,96,128]{2,1,0:T(8,128)(2,1)S(1)}, u32[]{:S(2)}, u32[]{:S(2)}) collective-permute-start(bf16[3,96,128]{2,1,0:T(8,128)(2,1)S(1)} %get-tuple-element.10), channel_id=1, source_target_pairs={{0,4},{4,0},{8,12},{12,8},{1,5},{5,1},{9,13},{13,9},{2,6},{6,2},{1... | collective-permute-start | bytes 221192 | tf_op jit(solution)/shard_map/ppermute | solution.py:241
  6.4 2.5 %collective-permute-start.1 = (bf16[3,96,128]{2,1,0:T(8,128)(2,1)S(1)}, bf16[3,96,128]{2,1,0:T(8,128)(2,1)S(1)}, u32[]{:S(2)}, u32[]{:S(2)}) collective-permute-start(bf16[3,96,128]{2,1,0:T(8,128)(2,1)S(1)} %get-tuple-element.10), channel_id=1, source_target_pairs={{0,12},{4,8},{8,4},{12,0},{1,13},{5,9},{9,5},{13,1},{2,14},{6,10},... | collective-permute-start | bytes 221192 | tf_op jit(solution)/shard_map/ppermute | solution.py:241
  8.9 0.1 collective-permute-start
  9.0 0.2 collective-permute-done.2.refs_0_.refs_2_
  9.2 0.4 %collective-permute-start.5 = (bf16[3,96,128]{2,1,0:T(8,128)(2,1)S(1)}, bf16[3,96,128]{2,1,0:T(8,128)(2,1)S(1)}, u32[]{:S(2)}, u32[]{:S(2)}) collective-permute-start(bf16[3,96,128]{2,1,0:T(8,128)(2,1)S(1)} %collective-permute-done.2.refs_0_.refs_2_), channel_id=1, source_target_pairs={{0,2},{1,3},{2,0},{3,1},{4,6},{5,7},{6,4},{7,5},{8,10},{9,11},{10,... | collective-permute-start | bytes 221192 | tf_op jit(solution)/shard_map/ppermute | solution.py:241
  9.5 5.6 %load.2.refs_2_.held_ref.refs_1_ = bf16[2,3,1024,1536]{3,2,1,0:T(8,128)(2,1)S(1)} custom-call(bf16[2,3,1024,1536]{3,2,1,0:T(8,128)(2,1)} %base_ref.3, bf16[3,96,128]{2,1,0:T(8,128)(2,1)S(1)} %collective-permute-done.2.refs_0_.refs_2_), custom_call_target="tpu_custom_call" | custom-call | bytes 18874368 | tf_op jit(solution)/shard_map/load/pallas_call | solution.py:90
  15.1 0.0 collective-permute-done.1.refs_1_
  15.1 0.6 %collective-permute-done.refs_0_ = bf16[3,96,128]{2,1,0:T(8,128)(2,1)S(1)} collective-permute-done((bf16[3,96,128]{2,1,0:T(8,128)(2,1)S(1)}, bf16[3,96,128]{2,1,0:T(8,128)(2,1)S(1)}, u32[]{:S(2)}, u32[]{:S(2)}) %collective-permute-start) | collective-permute-done | bytes 73760 | tf_op jit(solution)/shard_map/ppermute | solution.py:241
  15.7 0.0 collective-permute-done.5.refs_3_
  15.7 0.0 collective-permute-done.4.refs_1_
  15.8 0.1 collective-permute-start.6
  15.9 1.2 %collective-permute-start.3 = (bf16[3,192,128]{2,1,0:T(8,128)(2,1)S(1)}, bf16[3,192,128]{2,1,0:T(8,128)(2,1)S(1)}, u32[]{:S(2)}, u32[]{:S(2)}) collective-permute-start(bf16[3,192,128]{2,1,0:T(8,128)(2,1)S(1)} %pack.3.refs_4_.refs_2_.refs_0_), channel_id=1, source_target_pairs={{0,2},{1,3},{2,0},{3,1},{4,6},{5,7},{6,4},{7,5},{8,10},{9,11},{10,... | collective-permute-start | bytes 442376 | tf_op jit(solution)/shard_map/ppermute | solution.py:241
  17.1 0.9 %collective-permute-done.6.refs_1_ = bf16[3,896,128]{2,1,0:T(8,128)(2,1)S(1)} collective-permute-done((bf16[3,896,128]{2,1,0:T(8,128)(2,1)S(1)}, bf16[3,896,128]{2,1,0:T(8,128)(2,1)S(1)}, u32[]{:S(2)}, u32[]{:S(2)}) %collective-permute-start.6) | collective-permute-done | bytes 688160 | tf_op jit(solution)/shard_map/ppermute | solution.py:241
  18.0 5.0 %merge.2 = (bf16[2,3,1024,1536]{3,2,1,0:T(8,128)(2,1)}, f32[8,128]{1,0:T(8,128)S(1)}) custom-call(bf16[2,3,1024,1536]{3,2,1,0:T(8,128)(2,1)S(1)} %load.2.refs_2_.held_ref.refs_1_, bf16[3,896,128]{2,1,0:T(8,128)(2,1)S(1)} %pack.4.refs_0_, bf16[3,896,128]{2,1,0:T(8,128)(2,1)S(1)} %collective-permute-done.6.refs_1_, ...), custom_call_target="tpu_custom_call" | custom-call | flops 603979776 | bytes 18874368 | tf_op jit(solution)/shard_map/merge/pallas_call | solution.py:205
  23.0 0.0 collective-permute-done.3.refs_1_
  23.0 0.2 collective-permute-start.7
  23.3 1.9 %load.3.held_ref = bf16[2,3,1024,1536]{3,2,1,0:T(8,128)(2,1)S(1)} custom-call(bf16[2,3,1024,1536]{3,2,1,0:T(8,128)(2,1)} %base_ref.3, bf16[3,384,128]{2,1,0:T(8,128)(2,1)S(1)} %pack.5.refs_0_.refs_2_, bf16[2,3,1024,1536]{3,2,1,0:T(8,128)(2,1)S(1)} %load.2.refs_2_.held_ref.refs_1_), custom_call_target="tpu_custom_call", output_to_operand_aliasing={{}: (2, {})} | custom-call | bytes 18874368 | tf_op jit(solution)/shard_map/load/pallas_call | solution.py:90
  25.1 0.0 collective-permute-done.7.refs_3_
  25.1 5.6 %merge.3 = (bf16[2,3,1024,1536]{3,2,1,0:T(8,128)(2,1)}, f32[8,128]{1,0:T(8,128)}) custom-call(bf16[2,3,1024,1536]{3,2,1,0:T(8,128)(2,1)S(1)} %load.3.held_ref, bf16[3,896,128]{2,1,0:T(8,128)(2,1)S(1)} %pack.4.refs_0_, bf16[3,896,128]{2,1,0:T(8,128)(2,1)S(1)} %collective-permute-done.6.refs_1_, ...), custom_call_target="tpu_custom_call", output_to_operand_aliasing={{0}: (5, {})} | custom-call | flops 603979776 | bytes 18874368 | tf_op jit(solution)/shard_map/merge/pallas_call | solution.py:205
  (3 shorter events, 0.1 us)
Async XLA Ops:
  1.8 13.9 %collective-permute-start.4 = (bf16[3,352,128]{2,1,0:T(8,128)(2,1)S(1)}, bf16[3,352,128]{2,1,0:T(8,128)(2,1)S(1)}, u32[]{:S(2)}, u32[]{:S(2)}) collective-permute-start(bf16[3,352,128]{2,1,0:T(8,128)(2,1)S(1)} %get-tuple-element.11.refs_0_), channel_id=1, source_target_pairs={{0,2},{1,3},{2,0},{3,1},{4,6},{5,7},{6,4},{7,5},{8,10},{9,11},{10,... | collective-permute-start | bytes 811016 | tf_op jit(solution)/shard_map/ppermute | solution.py:241
  4.8 4.4 %collective-permute-start.2 = (bf16[3,96,128]{2,1,0:T(8,128)(2,1)S(1)}, bf16[3,96,128]{2,1,0:T(8,128)(2,1)S(1)}, u32[]{:S(2)}, u32[]{:S(2)}) collective-permute-start(bf16[3,96,128]{2,1,0:T(8,128)(2,1)S(1)} %get-tuple-element.10), channel_id=1, source_target_pairs={{0,4},{4,0},{8,12},{12,8},{1,5},{5,1},{9,13},{13,9},{2,6},{6,2},{1... | collective-permute-start | bytes 221192 | tf_op jit(solution)/shard_map/ppermute | solution.py:241
  6.4 8.7 %collective-permute-start.1 = (bf16[3,96,128]{2,1,0:T(8,128)(2,1)S(1)}, bf16[3,96,128]{2,1,0:T(8,128)(2,1)S(1)}, u32[]{:S(2)}, u32[]{:S(2)}) collective-permute-start(bf16[3,96,128]{2,1,0:T(8,128)(2,1)S(1)} %get-tuple-element.10), channel_id=1, source_target_pairs={{0,12},{4,8},{8,4},{12,0},{1,13},{5,9},{9,5},{13,1},{2,14},{6,10},... | collective-permute-start | bytes 221192 | tf_op jit(solution)/shard_map/ppermute | solution.py:241
  8.9 6.8 %collective-permute-start = (bf16[3,96,128]{2,1,0:T(8,128)(2,1)S(1)}, bf16[3,96,128]{2,1,0:T(8,128)(2,1)S(1)}, u32[]{:S(2)}, u32[]{:S(2)}) collective-permute-start(bf16[3,96,128]{2,1,0:T(8,128)(2,1)S(1)} %get-tuple-element.10), channel_id=1, source_target_pairs={{0,8},{4,12},{8,0},{12,4},{1,9},{5,13},{9,1},{13,5},{2,10},{6,14},... | collective-permute-start | bytes 221192 | tf_op jit(solution)/shard_map/ppermute | solution.py:241
  9.2 6.5 %collective-permute-start.5 = (bf16[3,96,128]{2,1,0:T(8,128)(2,1)S(1)}, bf16[3,96,128]{2,1,0:T(8,128)(2,1)S(1)}, u32[]{:S(2)}, u32[]{:S(2)}) collective-permute-start(bf16[3,96,128]{2,1,0:T(8,128)(2,1)S(1)} %collective-permute-done.2.refs_0_.refs_2_), channel_id=1, source_target_pairs={{0,2},{1,3},{2,0},{3,1},{4,6},{5,7},{6,4},{7,5},{8,10},{9,11},{10,... | collective-permute-start | bytes 221192 | tf_op jit(solution)/shard_map/ppermute | solution.py:241
  15.8 2.2 %collective-permute-start.6 = (bf16[3,896,128]{2,1,0:T(8,128)(2,1)S(1)}, bf16[3,896,128]{2,1,0:T(8,128)(2,1)S(1)}, u32[]{:S(2)}, u32[]{:S(2)}) collective-permute-start(bf16[3,896,128]{2,1,0:T(8,128)(2,1)S(1)} %pack.4.refs_0_), channel_id=1, source_target_pairs={{0,1},{1,0},{2,3},{3,2},{4,5},{5,4},{6,7},{7,6},{8,9},{9,8},{10,11... | collective-permute-start | bytes 2064392 | tf_op jit(solution)/shard_map/ppermute | solution.py:241
  15.9 7.1 %collective-permute-start.3 = (bf16[3,192,128]{2,1,0:T(8,128)(2,1)S(1)}, bf16[3,192,128]{2,1,0:T(8,128)(2,1)S(1)}, u32[]{:S(2)}, u32[]{:S(2)}) collective-permute-start(bf16[3,192,128]{2,1,0:T(8,128)(2,1)S(1)} %pack.3.refs_4_.refs_2_.refs_0_), channel_id=1, source_target_pairs={{0,2},{1,3},{2,0},{3,1},{4,6},{5,7},{6,4},{7,5},{8,10},{9,11},{10,... | collective-permute-start | bytes 442376 | tf_op jit(solution)/shard_map/ppermute | solution.py:241
  23.0 2.1 %collective-permute-start.7 = (bf16[3,384,128]{2,1,0:T(8,128)(2,1)S(1)}, bf16[3,384,128]{2,1,0:T(8,128)(2,1)S(1)}, u32[]{:S(2)}, u32[]{:S(2)}) collective-permute-start(bf16[3,384,128]{2,1,0:T(8,128)(2,1)S(1)} %pack.5.refs_0_.refs_2_), channel_id=1, source_target_pairs={{0,1},{1,0},{2,3},{3,2},{4,5},{5,4},{6,7},{7,6},{8,9},{9,8},{10,11... | collective-permute-start | bytes 884744 | tf_op jit(solution)/shard_map/ppermute | solution.py:241

commit v13 on v11

--- a/solution.py
+++ b/solution.py
@@ -10,7 +10,7 @@
 
 adapter_scale = 0.5
 out_slots = 3
-tile_rows = 512
+tile_rows = 256
 in_vmem = pl.BlockSpec(memory_space=pltpu.VMEM)
 in_hbm = pl.BlockSpec(memory_space=pltpu.HBM)
 anywhere = pl.BlockSpec(memory_space=pl.ANY)
@@ -199,6 +199,7 @@
 def merge(plan, held, parts, out=None, after=()):
     experts, projections, width, _ = held.shape
     deep = parts[0].shape[-1]
+    m_step = tile_rows if width % tile_rows == 0 else width
     share = projections * plan.span * experts * width
     extra = [*after] + ([] if out is None else [out])
     operands = [held, *parts, *extra]
@@ -211,7 +212,7 @@
             pltpu.VMEM((projections, width, deep), held.dtype),
             pltpu.VMEM((projections, plan.span, deep), held.dtype),
             pltpu.VMEM((out_slots, width, plan.span), held.dtype),
-            pltpu.SemaphoreType.DMA((out_slots, 2)),
+            pltpu.SemaphoreType.DMA((out_slots, width // m_step)),
         ],
         input_output_aliases={} if out is None else {len(operands) - 1: 0},
         compiler_params=pltpu.CompilerParams(vmem_limit_bytes=vmem_limit),

time: 30.5 us -> 30.2 us (level)
  no operation moved by 1% of the time
where the time goes in v13:
time: 30.2 us; the launch traced here: 30.1 us
  Pallas kernels  19.3 us (64%)
  starting transfers between devices  8.98 us (30%)
  waiting for transfers between devices  1.72 us (6%)
    pallas_call x2, Pallas kernels, merge(): pl.pallas_call(functools.partial(merge_kernel, plan), out_shape=[jax.Shap...  9.91 us
    ppermute x8, starting transfers between devices, swap(): return lax.ppermute(x, axis, [(i, i ^ bit) for i in range(4)])  8.98 us
    pallas_call x2, Pallas kernels, load(): pl.pallas_call(functools.partial(load_kernel, blocks), out_shape=jax.Shap...  7.45 us
    pallas_call x1, Pallas kernels, select(): pl.pallas_call(select_kernel, out_shape=(jax.ShapeDtypeStruct((projection...  1.81 us
    ppermute x8, waiting for transfers between devices, swap(): return lax.ppermute(x, axis, [(i, i ^ bit) for i in range(4)])  1.72 us
  transfers between devices with their start and end apart: 8, of which 3 were waited for; matrix products, arithmetic and copies ran while one was open for 0% of the time, Pallas kernels for 40%

profile of v13, /device:TPU:0, one launch (start us, length us, event | category | flops | bytes accessed | tf_op | source)
XLA Modules:
  0.0 30.1 jit_solution(9570857116364271174)
XLA Ops:
  0.0 1.8 %select.1 = (bf16[3,352,128]{2,1,0:T(8,128)(2,1)S(1)}, bf16[3,96,128]{2,1,0:T(8,128)(2,1)S(1)}) custom-call(s32[2]{0:T(128)} %index_ref.1, bf16[32,3,64,256]{3,2,1,0:T(8,128)(2,1)} %bitcast.1, bf16[32,3,64,96]{3,2,1,0:T(8,128)(2,1)} %wide_ref.1), custom_call_target="tpu_custom_call" | custom-call | tf_op jit(solution)/shard_map/select/pallas_call | solution.py:52
  1.8 3.0 %collective-permute-start.4 = (bf16[3,352,128]{2,1,0:T(8,128)(2,1)S(1)}, bf16[3,352,128]{2,1,0:T(8,128)(2,1)S(1)}, u32[]{:S(2)}, u32[]{:S(2)}) collective-permute-start(bf16[3,352,128]{2,1,0:T(8,128)(2,1)S(1)} %get-tuple-element.11.refs_0_), channel_id=1, source_target_pairs={{0,2},{1,3},{2,0},{3,1},{4,6},{5,7},{6,4},{7,5},{8,10},{9,11},{10,... | collective-permute-start | bytes 811016 | tf_op jit(solution)/shard_map/ppermute | solution.py:241
  4.8 1.6 %collective-permute-start.2 = (bf16[3,96,128]{2,1,0:T(8,128)(2,1)S(1)}, bf16[3,96,128]{2,1,0:T(8,128)(2,1)S(1)}, u32[]{:S(2)}, u32[]{:S(2)}) collective-permute-start(bf16[3,96,128]{2,1,0:T(8,128)(2,1)S(1)} %get-tuple-element.10), channel_id=1, source_target_pairs={{0,4},{4,0},{8,12},{12,8},{1,5},{5,1},{9,13},{13,9},{2,6},{6,2},{1... | collective-permute-start | bytes 221192 | tf_op jit(solution)/shard_map/ppermute | solution.py:241
  6.4 2.5 %collective-permute-start.1 = (bf16[3,96,128]{2,1,0:T(8,128)(2,1)S(1)}, bf16[3,96,128]{2,1,0:T(8,128)(2,1)S(1)}, u32[]{:S(2)}, u32[]{:S(2)}) collective-permute-start(bf16[3,96,128]{2,1,0:T(8,128)(2,1)S(1)} %get-tuple-element.10), channel_id=1, source_target_pairs={{0,12},{4,8},{8,4},{12,0},{1,13},{5,9},{9,5},{13,1},{2,14},{6,10},... | collective-permute-start | bytes 221192 | tf_op jit(solution)/shard_map/ppermute | solution.py:241
  8.9 0.1 collective-permute-start
  9.0 0.2 collective-permute-done.2.refs_0_.refs_2_
  9.2 0.4 %collective-permute-start.5 = (bf16[3,96,128]{2,1,0:T(8,128)(2,1)S(1)}, bf16[3,96,128]{2,1,0:T(8,128)(2,1)S(1)}, u32[]{:S(2)}, u32[]{:S(2)}) collective-permute-start(bf16[3,96,128]{2,1,0:T(8,128)(2,1)S(1)} %collective-permute-done.2.refs_0_.refs_2_), channel_id=1, source_target_pairs={{0,2},{1,3},{2,0},{3,1},{4,6},{5,7},{6,4},{7,5},{8,10},{9,11},{10,... | collective-permute-start | bytes 221192 | tf_op jit(solution)/shard_map/ppermute | solution.py:241
  9.5 5.6 %load.2.refs_2_.held_ref.refs_1_ = bf16[2,3,1024,1536]{3,2,1,0:T(8,128)(2,1)S(1)} custom-call(bf16[2,3,1024,1536]{3,2,1,0:T(8,128)(2,1)} %base_ref.3, bf16[3,96,128]{2,1,0:T(8,128)(2,1)S(1)} %collective-permute-done.2.refs_0_.refs_2_), custom_call_target="tpu_custom_call" | custom-call | bytes 18874368 | tf_op jit(solution)/shard_map/load/pallas_call | solution.py:90
  15.1 0.0 collective-permute-done.1.refs_1_
  15.1 0.6 %collective-permute-done.refs_0_ = bf16[3,96,128]{2,1,0:T(8,128)(2,1)S(1)} collective-permute-done((bf16[3,96,128]{2,1,0:T(8,128)(2,1)S(1)}, bf16[3,96,128]{2,1,0:T(8,128)(2,1)S(1)}, u32[]{:S(2)}, u32[]{:S(2)}) %collective-permute-start) | collective-permute-done | bytes 73760 | tf_op jit(solution)/shard_map/ppermute | solution.py:241
  15.7 0.0 collective-permute-done.5.refs_3_
  15.7 0.0 collective-permute-done.4.refs_1_
  15.8 0.1 collective-permute-start.6
  15.9 1.2 %collective-permute-start.3 = (bf16[3,192,128]{2,1,0:T(8,128)(2,1)S(1)}, bf16[3,192,128]{2,1,0:T(8,128)(2,1)S(1)}, u32[]{:S(2)}, u32[]{:S(2)}) collective-permute-start(bf16[3,192,128]{2,1,0:T(8,128)(2,1)S(1)} %pack.3.refs_4_.refs_2_.refs_0_), channel_id=1, source_target_pairs={{0,2},{1,3},{2,0},{3,1},{4,6},{5,7},{6,4},{7,5},{8,10},{9,11},{10,... | collective-permute-start | bytes 442376 | tf_op jit(solution)/shard_map/ppermute | solution.py:241
  17.1 0.9 %collective-permute-done.6.refs_1_ = bf16[3,896,128]{2,1,0:T(8,128)(2,1)S(1)} collective-permute-done((bf16[3,896,128]{2,1,0:T(8,128)(2,1)S(1)}, bf16[3,896,128]{2,1,0:T(8,128)(2,1)S(1)}, u32[]{:S(2)}, u32[]{:S(2)}) %collective-permute-start.6) | collective-permute-done | bytes 688160 | tf_op jit(solution)/shard_map/ppermute | solution.py:241
  18.0 4.6 %merge.2 = (bf16[2,3,1024,1536]{3,2,1,0:T(8,128)(2,1)}, f32[8,128]{1,0:T(8,128)S(1)}) custom-call(bf16[2,3,1024,1536]{3,2,1,0:T(8,128)(2,1)S(1)} %load.2.refs_2_.held_ref.refs_1_, bf16[3,896,128]{2,1,0:T(8,128)(2,1)S(1)} %pack.4.refs_0_, bf16[3,896,128]{2,1,0:T(8,128)(2,1)S(1)} %collective-permute-done.6.refs_1_, ...), custom_call_target="tpu_custom_call" | custom-call | flops 603979776 | bytes 18874368 | tf_op jit(solution)/shard_map/merge/pallas_call | solution.py:206
  22.6 0.0 collective-permute-done.3.refs_1_
  22.7 0.2 collective-permute-start.7
  22.9 1.9 %load.3.held_ref = bf16[2,3,1024,1536]{3,2,1,0:T(8,128)(2,1)S(1)} custom-call(bf16[2,3,1024,1536]{3,2,1,0:T(8,128)(2,1)} %base_ref.3, bf16[3,384,128]{2,1,0:T(8,128)(2,1)S(1)} %pack.5.refs_0_.refs_2_, bf16[2,3,1024,1536]{3,2,1,0:T(8,128)(2,1)S(1)} %load.2.refs_2_.held_ref.refs_1_), custom_call_target="tpu_custom_call", output_to_operand_aliasing={{}: (2, {})} | custom-call | bytes 18874368 | tf_op jit(solution)/shard_map/load/pallas_call | solution.py:90
  24.7 0.0 collective-permute-done.7.refs_3_
  24.8 5.3 %merge.3 = (bf16[2,3,1024,1536]{3,2,1,0:T(8,128)(2,1)}, f32[8,128]{1,0:T(8,128)}) custom-call(bf16[2,3,1024,1536]{3,2,1,0:T(8,128)(2,1)S(1)} %load.3.held_ref, bf16[3,896,128]{2,1,0:T(8,128)(2,1)S(1)} %pack.4.refs_0_, bf16[3,896,128]{2,1,0:T(8,128)(2,1)S(1)} %collective-permute-done.6.refs_1_, ...), custom_call_target="tpu_custom_call", output_to_operand_aliasing={{0}: (5, {})} | custom-call | flops 603979776 | bytes 18874368 | tf_op jit(solution)/shard_map/merge/pallas_call | solution.py:206
  (3 shorter events, 0.1 us)
Async XLA Ops:
  1.8 13.9 %collective-permute-start.4 = (bf16[3,352,128]{2,1,0:T(8,128)(2,1)S(1)}, bf16[3,352,128]{2,1,0:T(8,128)(2,1)S(1)}, u32[]{:S(2)}, u32[]{:S(2)}) collective-permute-start(bf16[3,352,128]{2,1,0:T(8,128)(2,1)S(1)} %get-tuple-element.11.refs_0_), channel_id=1, source_target_pairs={{0,2},{1,3},{2,0},{3,1},{4,6},{5,7},{6,4},{7,5},{8,10},{9,11},{10,... | collective-permute-start | bytes 811016 | tf_op jit(solution)/shard_map/ppermute | solution.py:241
  4.8 4.4 %collective-permute-start.2 = (bf16[3,96,128]{2,1,0:T(8,128)(2,1)S(1)}, bf16[3,96,128]{2,1,0:T(8,128)(2,1)S(1)}, u32[]{:S(2)}, u32[]{:S(2)}) collective-permute-start(bf16[3,96,128]{2,1,0:T(8,128)(2,1)S(1)} %get-tuple-element.10), channel_id=1, source_target_pairs={{0,4},{4,0},{8,12},{12,8},{1,5},{5,1},{9,13},{13,9},{2,6},{6,2},{1... | collective-permute-start | bytes 221192 | tf_op jit(solution)/shard_map/ppermute | solution.py:241
  6.4 8.7 %collective-permute-start.1 = (bf16[3,96,128]{2,1,0:T(8,128)(2,1)S(1)}, bf16[3,96,128]{2,1,0:T(8,128)(2,1)S(1)}, u32[]{:S(2)}, u32[]{:S(2)}) collective-permute-start(bf16[3,96,128]{2,1,0:T(8,128)(2,1)S(1)} %get-tuple-element.10), channel_id=1, source_target_pairs={{0,12},{4,8},{8,4},{12,0},{1,13},{5,9},{9,5},{13,1},{2,14},{6,10},... | collective-permute-start | bytes 221192 | tf_op jit(solution)/shard_map/ppermute | solution.py:241
  8.9 6.8 %collective-permute-start = (bf16[3,96,128]{2,1,0:T(8,128)(2,1)S(1)}, bf16[3,96,128]{2,1,0:T(8,128)(2,1)S(1)}, u32[]{:S(2)}, u32[]{:S(2)}) collective-permute-start(bf16[3,96,128]{2,1,0:T(8,128)(2,1)S(1)} %get-tuple-element.10), channel_id=1, source_target_pairs={{0,8},{4,12},{8,0},{12,4},{1,9},{5,13},{9,1},{13,5},{2,10},{6,14},... | collective-permute-start | bytes 221192 | tf_op jit(solution)/shard_map/ppermute | solution.py:241
  9.2 6.5 %collective-permute-start.5 = (bf16[3,96,128]{2,1,0:T(8,128)(2,1)S(1)}, bf16[3,96,128]{2,1,0:T(8,128)(2,1)S(1)}, u32[]{:S(2)}, u32[]{:S(2)}) collective-permute-start(bf16[3,96,128]{2,1,0:T(8,128)(2,1)S(1)} %collective-permute-done.2.refs_0_.refs_2_), channel_id=1, source_target_pairs={{0,2},{1,3},{2,0},{3,1},{4,6},{5,7},{6,4},{7,5},{8,10},{9,11},{10,... | collective-permute-start | bytes 221192 | tf_op jit(solution)/shard_map/ppermute | solution.py:241
  15.8 2.2 %collective-permute-start.6 = (bf16[3,896,128]{2,1,0:T(8,128)(2,1)S(1)}, bf16[3,896,128]{2,1,0:T(8,128)(2,1)S(1)}, u32[]{:S(2)}, u32[]{:S(2)}) collective-permute-start(bf16[3,896,128]{2,1,0:T(8,128)(2,1)S(1)} %pack.4.refs_0_), channel_id=1, source_target_pairs={{0,1},{1,0},{2,3},{3,2},{4,5},{5,4},{6,7},{7,6},{8,9},{9,8},{10,11... | collective-permute-start | bytes 2064392 | tf_op jit(solution)/shard_map/ppermute | solution.py:241
  15.9 6.8 %collective-permute-start.3 = (bf16[3,192,128]{2,1,0:T(8,128)(2,1)S(1)}, bf16[3,192,128]{2,1,0:T(8,128)(2,1)S(1)}, u32[]{:S(2)}, u32[]{:S(2)}) collective-permute-start(bf16[3,192,128]{2,1,0:T(8,128)(2,1)S(1)} %pack.3.refs_4_.refs_2_.refs_0_), channel_id=1, source_target_pairs={{0,2},{1,3},{2,0},{3,1},{4,6},{5,7},{6,4},{7,5},{8,10},{9,11},{10,... | collective-permute-start | bytes 442376 | tf_op jit(solution)/shard_map/ppermute | solution.py:241
  22.7 2.1 %collective-permute-start.7 = (bf16[3,384,128]{2,1,0:T(8,128)(2,1)S(1)}, bf16[3,384,128]{2,1,0:T(8,128)(2,1)S(1)}, u32[]{:S(2)}, u32[]{:S(2)}) collective-permute-start(bf16[3,384,128]{2,1,0:T(8,128)(2,1)S(1)} %pack.5.refs_0_.refs_2_), channel_id=1, source_target_pairs={{0,1},{1,0},{2,3},{3,2},{4,5},{5,4},{6,7},{7,6},{8,9},{9,8},{10,11... | collective-permute-start | bytes 884744 | tf_op jit(solution)/shard_map/ppermute | solution.py:241

commit v14 on v13

--- a/solution.py
+++ b/solution.py
@@ -10,7 +10,7 @@
 
 adapter_scale = 0.5
 out_slots = 3
-tile_rows = 256
+tile_rows = 128
 in_vmem = pl.BlockSpec(memory_space=pltpu.VMEM)
 in_hbm = pl.BlockSpec(memory_space=pltpu.HBM)
 anywhere = pl.BlockSpec(memory_space=pl.ANY)
@@ -243,7 +243,7 @@
     both, w = select(narrow, wide, adapted_expert_index)
     w3, w2, w1 = [swap(w, "shard", k) for k in (3, 2, 1)]
     width = base.shape[2]
-    split = width * 11 // 16
+    split = width * 13 // 16
     span = 2 * columns * groups
     near_half, far_half = lambda s: s // 2, lambda s: 1 - s // 2
     held = load(base, [(near_half, span, 0, width), (far_half, span, 0, split)], w1)

time: 30.2 us -> 30.1 us (level)
  waiting for transfers between devices: 1.72 us -> 1.04 us
  starting transfers between devices: 8.98 us -> 9.32 us
    ppermute x8, waiting for transfers between devices: 1.72 us -> 1.04 us  [swap(): return lax.ppermute(x, axis, [(i, i ^ bit) for i in range(4)])]
    ppermute x8, starting transfers between devices: 8.98 us -> 9.32 us  [swap(): return lax.ppermute(x, axis, [(i, i ^ bit) for i in range(4)])]
  transfers between devices with their start and end apart: 8 -> 8, of which waited for: 3 -> 3; matrix products, arithmetic and copies ran while one was open for 0% -> 0% of each run, Pallas kernels for 40% -> 41%
where the time goes in v14:
time: 30.1 us; the launch traced here: 29.9 us
  Pallas kernels  19.4 us (64%)
  starting transfers between devices  9.32 us (31%)
  waiting for transfers between devices  1.04 us (3%)
    pallas_call x2, Pallas kernels, merge(): pl.pallas_call(functools.partial(merge_kernel, plan), out_shape=[jax.Shap...  10.1 us
    ppermute x8, starting transfers between devices, swap(): return lax.ppermute(x, axis, [(i, i ^ bit) for i in range(4)])  9.32 us
    pallas_call x2, Pallas kernels, load(): pl.pallas_call(functools.partial(load_kernel, blocks), out_shape=jax.Shap...  7.42 us
    pallas_call x1, Pallas kernels, select(): pl.pallas_call(select_kernel, out_shape=(jax.ShapeDtypeStruct((projection...  1.81 us
    ppermute x8, waiting for transfers between devices, swap(): return lax.ppermute(x, axis, [(i, i ^ bit) for i in range(4)])  1.04 us
  transfers between devices with their start and end apart: 8, of which 3 were waited for; matrix products, arithmetic and copies ran while one was open for 0% of the time, Pallas kernels for 41%

profile of v14, /device:TPU:0, one launch (start us, length us, event | category | flops | bytes accessed | tf_op | source)
XLA Modules:
  0.0 29.9 jit_solution(9022085631716203699)
XLA Ops:
  0.0 1.8 %select.1 = (bf16[3,352,128]{2,1,0:T(8,128)(2,1)S(1)}, bf16[3,96,128]{2,1,0:T(8,128)(2,1)S(1)}) custom-call(s32[2]{0:T(128)} %index_ref.1, bf16[32,3,64,256]{3,2,1,0:T(8,128)(2,1)} %bitcast.1, bf16[32,3,64,96]{3,2,1,0:T(8,128)(2,1)} %wide_ref.1), custom_call_target="tpu_custom_call" | custom-call | tf_op jit(solution)/shard_map/select/pallas_call | solution.py:52
  1.8 3.0 %collective-permute-start.4 = (bf16[3,352,128]{2,1,0:T(8,128)(2,1)S(1)}, bf16[3,352,128]{2,1,0:T(8,128)(2,1)S(1)}, u32[]{:S(2)}, u32[]{:S(2)}) collective-permute-start(bf16[3,352,128]{2,1,0:T(8,128)(2,1)S(1)} %get-tuple-element.11.refs_0_), channel_id=1, source_target_pairs={{0,2},{1,3},{2,0},{3,1},{4,6},{5,7},{6,4},{7,5},{8,10},{9,11},{10,... | collective-permute-start | bytes 811016 | tf_op jit(solution)/shard_map/ppermute | solution.py:241
  4.8 1.6 %collective-permute-start.2 = (bf16[3,96,128]{2,1,0:T(8,128)(2,1)S(1)}, bf16[3,96,128]{2,1,0:T(8,128)(2,1)S(1)}, u32[]{:S(2)}, u32[]{:S(2)}) collective-permute-start(bf16[3,96,128]{2,1,0:T(8,128)(2,1)S(1)} %get-tuple-element.10), channel_id=1, source_target_pairs={{0,4},{4,0},{8,12},{12,8},{1,5},{5,1},{9,13},{13,9},{2,6},{6,2},{1... | collective-permute-start | bytes 221192 | tf_op jit(solution)/shard_map/ppermute | solution.py:241
  6.4 2.5 %collective-permute-start.1 = (bf16[3,96,128]{2,1,0:T(8,128)(2,1)S(1)}, bf16[3,96,128]{2,1,0:T(8,128)(2,1)S(1)}, u32[]{:S(2)}, u32[]{:S(2)}) collective-permute-start(bf16[3,96,128]{2,1,0:T(8,128)(2,1)S(1)} %get-tuple-element.10), channel_id=1, source_target_pairs={{0,12},{4,8},{8,4},{12,0},{1,13},{5,9},{9,5},{13,1},{2,14},{6,10},... | collective-permute-start | bytes 221192 | tf_op jit(solution)/shard_map/ppermute | solution.py:241
  8.9 0.1 collective-permute-start
  9.0 0.2 collective-permute-done.2.refs_0_.refs_2_
  9.2 0.4 %collective-permute-start.5 = (bf16[3,96,128]{2,1,0:T(8,128)(2,1)S(1)}, bf16[3,96,128]{2,1,0:T(8,128)(2,1)S(1)}, u32[]{:S(2)}, u32[]{:S(2)}) collective-permute-start(bf16[3,96,128]{2,1,0:T(8,128)(2,1)S(1)} %collective-permute-done.2.refs_0_.refs_2_), channel_id=1, source_target_pairs={{0,2},{1,3},{2,0},{3,1},{4,6},{5,7},{6,4},{7,5},{8,10},{9,11},{10,... | collective-permute-start | bytes 221192 | tf_op jit(solution)/shard_map/ppermute | solution.py:241
  9.5 5.9 %load.2.refs_2_.held_ref.refs_1_ = bf16[2,3,1024,1536]{3,2,1,0:T(8,128)(2,1)S(1)} custom-call(bf16[2,3,1024,1536]{3,2,1,0:T(8,128)(2,1)} %base_ref.3, bf16[3,96,128]{2,1,0:T(8,128)(2,1)S(1)} %collective-permute-done.2.refs_0_.refs_2_), custom_call_target="tpu_custom_call" | custom-call | bytes 18874368 | tf_op jit(solution)/shard_map/load/pallas_call | solution.py:90
  15.5 0.0 collective-permute-done.1.refs_1_
  15.5 0.2 collective-permute-done.refs_0_
  15.7 0.0 collective-permute-done.5.refs_3_
  15.7 0.0 collective-permute-done.4.refs_1_
  15.8 0.1 collective-permute-start.6
  15.9 1.5 %collective-permute-start.3 = (bf16[3,192,128]{2,1,0:T(8,128)(2,1)S(1)}, bf16[3,192,128]{2,1,0:T(8,128)(2,1)S(1)}, u32[]{:S(2)}, u32[]{:S(2)}) collective-permute-start(bf16[3,192,128]{2,1,0:T(8,128)(2,1)S(1)} %pack.3.refs_4_.refs_2_.refs_0_), channel_id=1, source_target_pairs={{0,2},{1,3},{2,0},{3,1},{4,6},{5,7},{6,4},{7,5},{8,10},{9,11},{10,... | collective-permute-start | bytes 442376 | tf_op jit(solution)/shard_map/ppermute | solution.py:241
  17.4 0.6 %collective-permute-done.6.refs_1_ = bf16[3,896,128]{2,1,0:T(8,128)(2,1)S(1)} collective-permute-done((bf16[3,896,128]{2,1,0:T(8,128)(2,1)S(1)}, bf16[3,896,128]{2,1,0:T(8,128)(2,1)S(1)}, u32[]{:S(2)}, u32[]{:S(2)}) %collective-permute-start.6) | collective-permute-done | bytes 688160 | tf_op jit(solution)/shard_map/ppermute | solution.py:241
  18.0 4.7 %merge.2 = (bf16[2,3,1024,1536]{3,2,1,0:T(8,128)(2,1)}, f32[8,128]{1,0:T(8,128)S(1)}) custom-call(bf16[2,3,1024,1536]{3,2,1,0:T(8,128)(2,1)S(1)} %load.2.refs_2_.held_ref.refs_1_, bf16[3,896,128]{2,1,0:T(8,128)(2,1)S(1)} %pack.4.refs_0_, bf16[3,896,128]{2,1,0:T(8,128)(2,1)S(1)} %collective-permute-done.6.refs_1_, ...), custom_call_target="tpu_custom_call" | custom-call | flops 603979776 | bytes 18874368 | tf_op jit(solution)/shard_map/merge/pallas_call | solution.py:206
  22.7 0.0 collective-permute-done.3.refs_1_
  22.8 0.2 collective-permute-start.7
  23.0 1.5 %load.3.held_ref = bf16[2,3,1024,1536]{3,2,1,0:T(8,128)(2,1)S(1)} custom-call(bf16[2,3,1024,1536]{3,2,1,0:T(8,128)(2,1)} %base_ref.3, bf16[3,384,128]{2,1,0:T(8,128)(2,1)S(1)} %pack.5.refs_0_.refs_2_, bf16[2,3,1024,1536]{3,2,1,0:T(8,128)(2,1)S(1)} %load.2.refs_2_.held_ref.refs_1_), custom_call_target="tpu_custom_call", output_to_operand_aliasing={{}: (2, {})} | custom-call | bytes 18874368 | tf_op jit(solution)/shard_map/load/pallas_call | solution.py:90
  24.5 0.0 collective-permute-done.7.refs_3_
  24.5 5.4 %merge.3 = (bf16[2,3,1024,1536]{3,2,1,0:T(8,128)(2,1)}, f32[8,128]{1,0:T(8,128)}) custom-call(bf16[2,3,1024,1536]{3,2,1,0:T(8,128)(2,1)S(1)} %load.3.held_ref, bf16[3,896,128]{2,1,0:T(8,128)(2,1)S(1)} %pack.4.refs_0_, bf16[3,896,128]{2,1,0:T(8,128)(2,1)S(1)} %collective-permute-done.6.refs_1_, ...), custom_call_target="tpu_custom_call", output_to_operand_aliasing={{0}: (5, {})} | custom-call | flops 603979776 | bytes 18874368 | tf_op jit(solution)/shard_map/merge/pallas_call | solution.py:206
  (3 shorter events, 0.1 us)
Async XLA Ops:
  1.8 13.9 %collective-permute-start.4 = (bf16[3,352,128]{2,1,0:T(8,128)(2,1)S(1)}, bf16[3,352,128]{2,1,0:T(8,128)(2,1)S(1)}, u32[]{:S(2)}, u32[]{:S(2)}) collective-permute-start(bf16[3,352,128]{2,1,0:T(8,128)(2,1)S(1)} %get-tuple-element.11.refs_0_), channel_id=1, source_target_pairs={{0,2},{1,3},{2,0},{3,1},{4,6},{5,7},{6,4},{7,5},{8,10},{9,11},{10,... | collective-permute-start | bytes 811016 | tf_op jit(solution)/shard_map/ppermute | solution.py:241
  4.8 4.4 %collective-permute-start.2 = (bf16[3,96,128]{2,1,0:T(8,128)(2,1)S(1)}, bf16[3,96,128]{2,1,0:T(8,128)(2,1)S(1)}, u32[]{:S(2)}, u32[]{:S(2)}) collective-permute-start(bf16[3,96,128]{2,1,0:T(8,128)(2,1)S(1)} %get-tuple-element.10), channel_id=1, source_target_pairs={{0,4},{4,0},{8,12},{12,8},{1,5},{5,1},{9,13},{13,9},{2,6},{6,2},{1... | collective-permute-start | bytes 221192 | tf_op jit(solution)/shard_map/ppermute | solution.py:241
  6.4 9.1 %collective-permute-start.1 = (bf16[3,96,128]{2,1,0:T(8,128)(2,1)S(1)}, bf16[3,96,128]{2,1,0:T(8,128)(2,1)S(1)}, u32[]{:S(2)}, u32[]{:S(2)}) collective-permute-start(bf16[3,96,128]{2,1,0:T(8,128)(2,1)S(1)} %get-tuple-element.10), channel_id=1, source_target_pairs={{0,12},{4,8},{8,4},{12,0},{1,13},{5,9},{9,5},{13,1},{2,14},{6,10},... | collective-permute-start | bytes 221192 | tf_op jit(solution)/shard_map/ppermute | solution.py:241
  8.9 6.8 %collective-permute-start = (bf16[3,96,128]{2,1,0:T(8,128)(2,1)S(1)}, bf16[3,96,128]{2,1,0:T(8,128)(2,1)S(1)}, u32[]{:S(2)}, u32[]{:S(2)}) collective-permute-start(bf16[3,96,128]{2,1,0:T(8,128)(2,1)S(1)} %get-tuple-element.10), channel_id=1, source_target_pairs={{0,8},{4,12},{8,0},{12,4},{1,9},{5,13},{9,1},{13,5},{2,10},{6,14},... | collective-permute-start | bytes 221192 | tf_op jit(solution)/shard_map/ppermute | solution.py:241
  9.2 6.5 %collective-permute-start.5 = (bf16[3,96,128]{2,1,0:T(8,128)(2,1)S(1)}, bf16[3,96,128]{2,1,0:T(8,128)(2,1)S(1)}, u32[]{:S(2)}, u32[]{:S(2)}) collective-permute-start(bf16[3,96,128]{2,1,0:T(8,128)(2,1)S(1)} %collective-permute-done.2.refs_0_.refs_2_), channel_id=1, source_target_pairs={{0,2},{1,3},{2,0},{3,1},{4,6},{5,7},{6,4},{7,5},{8,10},{9,11},{10,... | collective-permute-start | bytes 221192 | tf_op jit(solution)/shard_map/ppermute | solution.py:241
  15.8 2.2 %collective-permute-start.6 = (bf16[3,896,128]{2,1,0:T(8,128)(2,1)S(1)}, bf16[3,896,128]{2,1,0:T(8,128)(2,1)S(1)}, u32[]{:S(2)}, u32[]{:S(2)}) collective-permute-start(bf16[3,896,128]{2,1,0:T(8,128)(2,1)S(1)} %pack.4.refs_0_), channel_id=1, source_target_pairs={{0,1},{1,0},{2,3},{3,2},{4,5},{5,4},{6,7},{7,6},{8,9},{9,8},{10,11... | collective-permute-start | bytes 2064392 | tf_op jit(solution)/shard_map/ppermute | solution.py:241
  15.9 6.9 %collective-permute-start.3 = (bf16[3,192,128]{2,1,0:T(8,128)(2,1)S(1)}, bf16[3,192,128]{2,1,0:T(8,128)(2,1)S(1)}, u32[]{:S(2)}, u32[]{:S(2)}) collective-permute-start(bf16[3,192,128]{2,1,0:T(8,128)(2,1)S(1)} %pack.3.refs_4_.refs_2_.refs_0_), channel_id=1, source_target_pairs={{0,2},{1,3},{2,0},{3,1},{4,6},{5,7},{6,4},{7,5},{8,10},{9,11},{10,... | collective-permute-start | bytes 442376 | tf_op jit(solution)/shard_map/ppermute | solution.py:241
  22.8 1.7 %collective-permute-start.7 = (bf16[3,384,128]{2,1,0:T(8,128)(2,1)S(1)}, bf16[3,384,128]{2,1,0:T(8,128)(2,1)S(1)}, u32[]{:S(2)}, u32[]{:S(2)}) collective-permute-start(bf16[3,384,128]{2,1,0:T(8,128)(2,1)S(1)} %pack.5.refs_0_.refs_2_), channel_id=1, source_target_pairs={{0,1},{1,0},{2,3},{3,2},{4,5},{5,4},{6,7},{7,6},{8,9},{9,8},{10,11... | collective-permute-start | bytes 884744 | tf_op jit(solution)/shard_map/ppermute | solution.py:241

commit v15 on v14

--- a/solution.py
+++ b/solution.py
@@ -9,8 +9,8 @@
 from jax.sharding import PartitionSpec as P
 
 adapter_scale = 0.5
-out_slots = 3
-tile_rows = 128
+out_slots = 6
+tile_rows = 256
 in_vmem = pl.BlockSpec(memory_space=pltpu.VMEM)
 in_hbm = pl.BlockSpec(memory_space=pltpu.HBM)
 anywhere = pl.BlockSpec(memory_space=pl.ANY)

time: 30.1 us -> 30.1 us (level)
  no operation moved by 1% of the time
where the time goes in v15:
time: 30.1 us; the launch traced here: 29.9 us
  Pallas kernels  19.4 us (64%)
  starting transfers between devices  9.31 us (31%)
  waiting for transfers between devices  1.04 us (3%)
    pallas_call x2, Pallas kernels, merge(): pl.pallas_call(functools.partial(merge_kernel, plan), out_shape=[jax.Shap...  10.1 us
    ppermute x8, starting transfers between devices, swap(): return lax.ppermute(x, axis, [(i, i ^ bit) for i in range(4)])  9.31 us
    pallas_call x2, Pallas kernels, load(): pl.pallas_call(functools.partial(load_kernel, blocks), out_shape=jax.Shap...  7.42 us
    pallas_call x1, Pallas kernels, select(): pl.pallas_call(select_kernel, out_shape=(jax.ShapeDtypeStruct((projection...  1.81 us
    ppermute x8, waiting for transfers between devices, swap(): return lax.ppermute(x, axis, [(i, i ^ bit) for i in range(4)])  1.04 us
  transfers between devices with their start and end apart: 8, of which 3 were waited for; matrix products, arithmetic and copies ran while one was open for 0% of the time, Pallas kernels for 41%

profile of v15, /device:TPU:0, one launch (start us, length us, event | category | flops | bytes accessed | tf_op | source)
XLA Modules:
  0.0 29.9 jit_solution(2983568326208966274)
XLA Ops:
  0.0 1.8 %select.1 = (bf16[3,352,128]{2,1,0:T(8,128)(2,1)S(1)}, bf16[3,96,128]{2,1,0:T(8,128)(2,1)S(1)}) custom-call(s32[2]{0:T(128)} %index_ref.1, bf16[32,3,64,256]{3,2,1,0:T(8,128)(2,1)} %bitcast.1, bf16[32,3,64,96]{3,2,1,0:T(8,128)(2,1)} %wide_ref.1), custom_call_target="tpu_custom_call" | custom-call | tf_op jit(solution)/shard_map/select/pallas_call | solution.py:52
  1.8 3.0 %collective-permute-start.4 = (bf16[3,352,128]{2,1,0:T(8,128)(2,1)S(1)}, bf16[3,352,128]{2,1,0:T(8,128)(2,1)S(1)}, u32[]{:S(2)}, u32[]{:S(2)}) collective-permute-start(bf16[3,352,128]{2,1,0:T(8,128)(2,1)S(1)} %get-tuple-element.11.refs_0_), channel_id=1, source_target_pairs={{0,2},{1,3},{2,0},{3,1},{4,6},{5,7},{6,4},{7,5},{8,10},{9,11},{10,... | collective-permute-start | bytes 811016 | tf_op jit(solution)/shard_map/ppermute | solution.py:241
  4.8 1.6 %collective-permute-start.2 = (bf16[3,96,128]{2,1,0:T(8,128)(2,1)S(1)}, bf16[3,96,128]{2,1,0:T(8,128)(2,1)S(1)}, u32[]{:S(2)}, u32[]{:S(2)}) collective-permute-start(bf16[3,96,128]{2,1,0:T(8,128)(2,1)S(1)} %get-tuple-element.10), channel_id=1, source_target_pairs={{0,4},{4,0},{8,12},{12,8},{1,5},{5,1},{9,13},{13,9},{2,6},{6,2},{1... | collective-permute-start | bytes 221192 | tf_op jit(solution)/shard_map/ppermute | solution.py:241
  6.4 2.5 %collective-permute-start.1 = (bf16[3,96,128]{2,1,0:T(8,128)(2,1)S(1)}, bf16[3,96,128]{2,1,0:T(8,128)(2,1)S(1)}, u32[]{:S(2)}, u32[]{:S(2)}) collective-permute-start(bf16[3,96,128]{2,1,0:T(8,128)(2,1)S(1)} %get-tuple-element.10), channel_id=1, source_target_pairs={{0,12},{4,8},{8,4},{12,0},{1,13},{5,9},{9,5},{13,1},{2,14},{6,10},... | collective-permute-start | bytes 221192 | tf_op jit(solution)/shard_map/ppermute | solution.py:241
  8.9 0.1 collective-permute-start
  9.0 0.2 collective-permute-done.2.refs_0_.refs_2_
  9.2 0.4 %collective-permute-start.5 = (bf16[3,96,128]{2,1,0:T(8,128)(2,1)S(1)}, bf16[3,96,128]{2,1,0:T(8,128)(2,1)S(1)}, u32[]{:S(2)}, u32[]{:S(2)}) collective-permute-start(bf16[3,96,128]{2,1,0:T(8,128)(2,1)S(1)} %collective-permute-done.2.refs_0_.refs_2_), channel_id=1, source_target_pairs={{0,2},{1,3},{2,0},{3,1},{4,6},{5,7},{6,4},{7,5},{8,10},{9,11},{10,... | collective-permute-start | bytes 221192 | tf_op jit(solution)/shard_map/ppermute | solution.py:241
  9.5 5.9 %load.2.refs_2_.held_ref.refs_1_ = bf16[2,3,1024,1536]{3,2,1,0:T(8,128)(2,1)S(1)} custom-call(bf16[2,3,1024,1536]{3,2,1,0:T(8,128)(2,1)} %base_ref.3, bf16[3,96,128]{2,1,0:T(8,128)(2,1)S(1)} %collective-permute-done.2.refs_0_.refs_2_), custom_call_target="tpu_custom_call" | custom-call | bytes 18874368 | tf_op jit(solution)/shard_map/load/pallas_call | solution.py:90
  15.5 0.0 collective-permute-done.1.refs_1_
  15.5 0.2 collective-permute-done.refs_0_
  15.7 0.0 collective-permute-done.5.refs_3_
  15.7 0.0 collective-permute-done.4.refs_1_
  15.8 0.1 collective-permute-start.6
  15.9 1.5 %collective-permute-start.3 = (bf16[3,192,128]{2,1,0:T(8,128)(2,1)S(1)}, bf16[3,192,128]{2,1,0:T(8,128)(2,1)S(1)}, u32[]{:S(2)}, u32[]{:S(2)}) collective-permute-start(bf16[3,192,128]{2,1,0:T(8,128)(2,1)S(1)} %pack.3.refs_4_.refs_2_.refs_0_), channel_id=1, source_target_pairs={{0,2},{1,3},{2,0},{3,1},{4,6},{5,7},{6,4},{7,5},{8,10},{9,11},{10,... | collective-permute-start | bytes 442376 | tf_op jit(solution)/shard_map/ppermute | solution.py:241
  17.4 0.6 %collective-permute-done.6.refs_1_ = bf16[3,896,128]{2,1,0:T(8,128)(2,1)S(1)} collective-permute-done((bf16[3,896,128]{2,1,0:T(8,128)(2,1)S(1)}, bf16[3,896,128]{2,1,0:T(8,128)(2,1)S(1)}, u32[]{:S(2)}, u32[]{:S(2)}) %collective-permute-start.6) | collective-permute-done | bytes 688160 | tf_op jit(solution)/shard_map/ppermute | solution.py:241
  18.0 4.7 %merge.2 = (bf16[2,3,1024,1536]{3,2,1,0:T(8,128)(2,1)}, f32[8,128]{1,0:T(8,128)S(1)}) custom-call(bf16[2,3,1024,1536]{3,2,1,0:T(8,128)(2,1)S(1)} %load.2.refs_2_.held_ref.refs_1_, bf16[3,896,128]{2,1,0:T(8,128)(2,1)S(1)} %pack.4.refs_0_, bf16[3,896,128]{2,1,0:T(8,128)(2,1)S(1)} %collective-permute-done.6.refs_1_, ...), custom_call_target="tpu_custom_call" | custom-call | flops 603979776 | bytes 18874368 | tf_op jit(solution)/shard_map/merge/pallas_call | solution.py:206
  22.7 0.0 collective-permute-done.3.refs_1_
  22.8 0.2 collective-permute-start.7
  23.0 1.5 %load.3.held_ref = bf16[2,3,1024,1536]{3,2,1,0:T(8,128)(2,1)S(1)} custom-call(bf16[2,3,1024,1536]{3,2,1,0:T(8,128)(2,1)} %base_ref.3, bf16[3,384,128]{2,1,0:T(8,128)(2,1)S(1)} %pack.5.refs_0_.refs_2_, bf16[2,3,1024,1536]{3,2,1,0:T(8,128)(2,1)S(1)} %load.2.refs_2_.held_ref.refs_1_), custom_call_target="tpu_custom_call", output_to_operand_aliasing={{}: (2, {})} | custom-call | bytes 18874368 | tf_op jit(solution)/shard_map/load/pallas_call | solution.py:90
  24.5 0.0 collective-permute-done.7.refs_3_
  24.5 5.4 %merge.3 = (bf16[2,3,1024,1536]{3,2,1,0:T(8,128)(2,1)}, f32[8,128]{1,0:T(8,128)}) custom-call(bf16[2,3,1024,1536]{3,2,1,0:T(8,128)(2,1)S(1)} %load.3.held_ref, bf16[3,896,128]{2,1,0:T(8,128)(2,1)S(1)} %pack.4.refs_0_, bf16[3,896,128]{2,1,0:T(8,128)(2,1)S(1)} %collective-permute-done.6.refs_1_, ...), custom_call_target="tpu_custom_call", output_to_operand_aliasing={{0}: (5, {})} | custom-call | flops 603979776 | bytes 18874368 | tf_op jit(solution)/shard_map/merge/pallas_call | solution.py:206
  (3 shorter events, 0.1 us)
Async XLA Ops:
  1.8 13.9 %collective-permute-start.4 = (bf16[3,352,128]{2,1,0:T(8,128)(2,1)S(1)}, bf16[3,352,128]{2,1,0:T(8,128)(2,1)S(1)}, u32[]{:S(2)}, u32[]{:S(2)}) collective-permute-start(bf16[3,352,128]{2,1,0:T(8,128)(2,1)S(1)} %get-tuple-element.11.refs_0_), channel_id=1, source_target_pairs={{0,2},{1,3},{2,0},{3,1},{4,6},{5,7},{6,4},{7,5},{8,10},{9,11},{10,... | collective-permute-start | bytes 811016 | tf_op jit(solution)/shard_map/ppermute | solution.py:241
  4.8 4.4 %collective-permute-start.2 = (bf16[3,96,128]{2,1,0:T(8,128)(2,1)S(1)}, bf16[3,96,128]{2,1,0:T(8,128)(2,1)S(1)}, u32[]{:S(2)}, u32[]{:S(2)}) collective-permute-start(bf16[3,96,128]{2,1,0:T(8,128)(2,1)S(1)} %get-tuple-element.10), channel_id=1, source_target_pairs={{0,4},{4,0},{8,12},{12,8},{1,5},{5,1},{9,13},{13,9},{2,6},{6,2},{1... | collective-permute-start | bytes 221192 | tf_op jit(solution)/shard_map/ppermute | solution.py:241
  6.4 9.1 %collective-permute-start.1 = (bf16[3,96,128]{2,1,0:T(8,128)(2,1)S(1)}, bf16[3,96,128]{2,1,0:T(8,128)(2,1)S(1)}, u32[]{:S(2)}, u32[]{:S(2)}) collective-permute-start(bf16[3,96,128]{2,1,0:T(8,128)(2,1)S(1)} %get-tuple-element.10), channel_id=1, source_target_pairs={{0,12},{4,8},{8,4},{12,0},{1,13},{5,9},{9,5},{13,1},{2,14},{6,10},... | collective-permute-start | bytes 221192 | tf_op jit(solution)/shard_map/ppermute | solution.py:241
  8.9 6.8 %collective-permute-start = (bf16[3,96,128]{2,1,0:T(8,128)(2,1)S(1)}, bf16[3,96,128]{2,1,0:T(8,128)(2,1)S(1)}, u32[]{:S(2)}, u32[]{:S(2)}) collective-permute-start(bf16[3,96,128]{2,1,0:T(8,128)(2,1)S(1)} %get-tuple-element.10), channel_id=1, source_target_pairs={{0,8},{4,12},{8,0},{12,4},{1,9},{5,13},{9,1},{13,5},{2,10},{6,14},... | collective-permute-start | bytes 221192 | tf_op jit(solution)/shard_map/ppermute | solution.py:241
  9.2 6.5 %collective-permute-start.5 = (bf16[3,96,128]{2,1,0:T(8,128)(2,1)S(1)}, bf16[3,96,128]{2,1,0:T(8,128)(2,1)S(1)}, u32[]{:S(2)}, u32[]{:S(2)}) collective-permute-start(bf16[3,96,128]{2,1,0:T(8,128)(2,1)S(1)} %collective-permute-done.2.refs_0_.refs_2_), channel_id=1, source_target_pairs={{0,2},{1,3},{2,0},{3,1},{4,6},{5,7},{6,4},{7,5},{8,10},{9,11},{10,... | collective-permute-start | bytes 221192 | tf_op jit(solution)/shard_map/ppermute | solution.py:241
  15.8 2.2 %collective-permute-start.6 = (bf16[3,896,128]{2,1,0:T(8,128)(2,1)S(1)}, bf16[3,896,128]{2,1,0:T(8,128)(2,1)S(1)}, u32[]{:S(2)}, u32[]{:S(2)}) collective-permute-start(bf16[3,896,128]{2,1,0:T(8,128)(2,1)S(1)} %pack.4.refs_0_), channel_id=1, source_target_pairs={{0,1},{1,0},{2,3},{3,2},{4,5},{5,4},{6,7},{7,6},{8,9},{9,8},{10,11... | collective-permute-start | bytes 2064392 | tf_op jit(solution)/shard_map/ppermute | solution.py:241
  15.9 6.9 %collective-permute-start.3 = (bf16[3,192,128]{2,1,0:T(8,128)(2,1)S(1)}, bf16[3,192,128]{2,1,0:T(8,128)(2,1)S(1)}, u32[]{:S(2)}, u32[]{:S(2)}) collective-permute-start(bf16[3,192,128]{2,1,0:T(8,128)(2,1)S(1)} %pack.3.refs_4_.refs_2_.refs_0_), channel_id=1, source_target_pairs={{0,2},{1,3},{2,0},{3,1},{4,6},{5,7},{6,4},{7,5},{8,10},{9,11},{10,... | collective-permute-start | bytes 442376 | tf_op jit(solution)/shard_map/ppermute | solution.py:241
  22.8 1.7 %collective-permute-start.7 = (bf16[3,384,128]{2,1,0:T(8,128)(2,1)S(1)}, bf16[3,384,128]{2,1,0:T(8,128)(2,1)S(1)}, u32[]{:S(2)}, u32[]{:S(2)}) collective-permute-start(bf16[3,384,128]{2,1,0:T(8,128)(2,1)S(1)} %pack.5.refs_0_.refs_2_), channel_id=1, source_target_pairs={{0,1},{1,0},{2,3},{3,2},{4,5},{5,4},{6,7},{7,6},{8,9},{9,8},{10,11... | collective-permute-start | bytes 884744 | tf_op jit(solution)/shard_map/ppermute | solution.py:241

commit v16 on v15

--- a/solution.py
+++ b/solution.py
@@ -9,7 +9,7 @@
 from jax.sharding import PartitionSpec as P
 
 adapter_scale = 0.5
-out_slots = 6
+out_slots = 3
 tile_rows = 256
 in_vmem = pl.BlockSpec(memory_space=pltpu.VMEM)
 in_hbm = pl.BlockSpec(memory_space=pltpu.HBM)

time: 30.1 us -> 29.9 us (level)
  no operation moved by 1% of the time
where the time goes in v16:
time: 29.9 us; the launch traced here: 29.7 us
  Pallas kernels  19.2 us (64%)
  starting transfers between devices  9.31 us (31%)
  waiting for transfers between devices  1.04 us (3%)
    pallas_call x2, Pallas kernels, merge(): pl.pallas_call(functools.partial(merge_kernel, plan), out_shape=[jax.Shap...  9.91 us
    ppermute x8, starting transfers between devices, swap(): return lax.ppermute(x, axis, [(i, i ^ bit) for i in range(4)])  9.31 us
    pallas_call x2, Pallas kernels, load(): pl.pallas_call(functools.partial(load_kernel, blocks), out_shape=jax.Shap...  7.42 us
    pallas_call x1, Pallas kernels, select(): pl.pallas_call(select_kernel, out_shape=(jax.ShapeDtypeStruct((projection...  1.81 us
    ppermute x8, waiting for transfers between devices, swap(): return lax.ppermute(x, axis, [(i, i ^ bit) for i in range(4)])  1.04 us
  transfers between devices with their start and end apart: 8, of which 3 were waited for; matrix products, arithmetic and copies ran while one was open for 0% of the time, Pallas kernels for 41%

profile of v16, /device:TPU:0, one launch (start us, length us, event | category | flops | bytes accessed | tf_op | source)
XLA Modules:
  0.0 29.7 jit_solution(11225763925228294521)
XLA Ops:
  0.0 1.8 %select.1 = (bf16[3,352,128]{2,1,0:T(8,128)(2,1)S(1)}, bf16[3,96,128]{2,1,0:T(8,128)(2,1)S(1)}) custom-call(s32[2]{0:T(128)} %index_ref.1, bf16[32,3,64,256]{3,2,1,0:T(8,128)(2,1)} %bitcast.1, bf16[32,3,64,96]{3,2,1,0:T(8,128)(2,1)} %wide_ref.1), custom_call_target="tpu_custom_call" | custom-call | tf_op jit(solution)/shard_map/select/pallas_call | solution.py:52
  1.8 3.0 %collective-permute-start.4 = (bf16[3,352,128]{2,1,0:T(8,128)(2,1)S(1)}, bf16[3,352,128]{2,1,0:T(8,128)(2,1)S(1)}, u32[]{:S(2)}, u32[]{:S(2)}) collective-permute-start(bf16[3,352,128]{2,1,0:T(8,128)(2,1)S(1)} %get-tuple-element.11.refs_0_), channel_id=1, source_target_pairs={{0,2},{1,3},{2,0},{3,1},{4,6},{5,7},{6,4},{7,5},{8,10},{9,11},{10,... | collective-permute-start | bytes 811016 | tf_op jit(solution)/shard_map/ppermute | solution.py:241
  4.8 1.6 %collective-permute-start.2 = (bf16[3,96,128]{2,1,0:T(8,128)(2,1)S(1)}, bf16[3,96,128]{2,1,0:T(8,128)(2,1)S(1)}, u32[]{:S(2)}, u32[]{:S(2)}) collective-permute-start(bf16[3,96,128]{2,1,0:T(8,128)(2,1)S(1)} %get-tuple-element.10), channel_id=1, source_target_pairs={{0,4},{4,0},{8,12},{12,8},{1,5},{5,1},{9,13},{13,9},{2,6},{6,2},{1... | collective-permute-start | bytes 221192 | tf_op jit(solution)/shard_map/ppermute | solution.py:241
  6.4 2.5 %collective-permute-start.1 = (bf16[3,96,128]{2,1,0:T(8,128)(2,1)S(1)}, bf16[3,96,128]{2,1,0:T(8,128)(2,1)S(1)}, u32[]{:S(2)}, u32[]{:S(2)}) collective-permute-start(bf16[3,96,128]{2,1,0:T(8,128)(2,1)S(1)} %get-tuple-element.10), channel_id=1, source_target_pairs={{0,12},{4,8},{8,4},{12,0},{1,13},{5,9},{9,5},{13,1},{2,14},{6,10},... | collective-permute-start | bytes 221192 | tf_op jit(solution)/shard_map/ppermute | solution.py:241
  8.9 0.1 collective-permute-start
  9.0 0.2 collective-permute-done.2.refs_0_.refs_2_
  9.2 0.4 %collective-permute-start.5 = (bf16[3,96,128]{2,1,0:T(8,128)(2,1)S(1)}, bf16[3,96,128]{2,1,0:T(8,128)(2,1)S(1)}, u32[]{:S(2)}, u32[]{:S(2)}) collective-permute-start(bf16[3,96,128]{2,1,0:T(8,128)(2,1)S(1)} %collective-permute-done.2.refs_0_.refs_2_), channel_id=1, source_target_pairs={{0,2},{1,3},{2,0},{3,1},{4,6},{5,7},{6,4},{7,5},{8,10},{9,11},{10,... | collective-permute-start | bytes 221192 | tf_op jit(solution)/shard_map/ppermute | solution.py:241
  9.5 5.9 %load.2.refs_2_.held_ref.refs_1_ = bf16[2,3,1024,1536]{3,2,1,0:T(8,128)(2,1)S(1)} custom-call(bf16[2,3,1024,1536]{3,2,1,0:T(8,128)(2,1)} %base_ref.3, bf16[3,96,128]{2,1,0:T(8,128)(2,1)S(1)} %collective-permute-done.2.refs_0_.refs_2_), custom_call_target="tpu_custom_call" | custom-call | bytes 18874368 | tf_op jit(solution)/shard_map/load/pallas_call | solution.py:90
  15.5 0.0 collective-permute-done.1.refs_1_
  15.5 0.2 collective-permute-done.refs_0_
  15.7 0.0 collective-permute-done.5.refs_3_
  15.7 0.0 collective-permute-done.4.refs_1_
  15.8 0.1 collective-permute-start.6
  15.9 1.5 %collective-permute-start.3 = (bf16[3,192,128]{2,1,0:T(8,128)(2,1)S(1)}, bf16[3,192,128]{2,1,0:T(8,128)(2,1)S(1)}, u32[]{:S(2)}, u32[]{:S(2)}) collective-permute-start(bf16[3,192,128]{2,1,0:T(8,128)(2,1)S(1)} %pack.3.refs_4_.refs_2_.refs_0_), channel_id=1, source_target_pairs={{0,2},{1,3},{2,0},{3,1},{4,6},{5,7},{6,4},{7,5},{8,10},{9,11},{10,... | collective-permute-start | bytes 442376 | tf_op jit(solution)/shard_map/ppermute | solution.py:241
  17.4 0.6 %collective-permute-done.6.refs_1_ = bf16[3,896,128]{2,1,0:T(8,128)(2,1)S(1)} collective-permute-done((bf16[3,896,128]{2,1,0:T(8,128)(2,1)S(1)}, bf16[3,896,128]{2,1,0:T(8,128)(2,1)S(1)}, u32[]{:S(2)}, u32[]{:S(2)}) %collective-permute-start.6) | collective-permute-done | bytes 688160 | tf_op jit(solution)/shard_map/ppermute | solution.py:241
  18.0 4.6 %merge.2 = (bf16[2,3,1024,1536]{3,2,1,0:T(8,128)(2,1)}, f32[8,128]{1,0:T(8,128)S(1)}) custom-call(bf16[2,3,1024,1536]{3,2,1,0:T(8,128)(2,1)S(1)} %load.2.refs_2_.held_ref.refs_1_, bf16[3,896,128]{2,1,0:T(8,128)(2,1)S(1)} %pack.4.refs_0_, bf16[3,896,128]{2,1,0:T(8,128)(2,1)S(1)} %collective-permute-done.6.refs_1_, ...), custom_call_target="tpu_custom_call" | custom-call | flops 603979776 | bytes 18874368 | tf_op jit(solution)/shard_map/merge/pallas_call | solution.py:206
  22.6 0.0 collective-permute-done.3.refs_1_
  22.7 0.2 collective-permute-start.7
  22.9 1.5 %load.3.held_ref = bf16[2,3,1024,1536]{3,2,1,0:T(8,128)(2,1)S(1)} custom-call(bf16[2,3,1024,1536]{3,2,1,0:T(8,128)(2,1)} %base_ref.3, bf16[3,384,128]{2,1,0:T(8,128)(2,1)S(1)} %pack.5.refs_0_.refs_2_, bf16[2,3,1024,1536]{3,2,1,0:T(8,128)(2,1)S(1)} %load.2.refs_2_.held_ref.refs_1_), custom_call_target="tpu_custom_call", output_to_operand_aliasing={{}: (2, {})} | custom-call | bytes 18874368 | tf_op jit(solution)/shard_map/load/pallas_call | solution.py:90
  24.4 0.0 collective-permute-done.7.refs_3_
  24.4 5.3 %merge.3 = (bf16[2,3,1024,1536]{3,2,1,0:T(8,128)(2,1)}, f32[8,128]{1,0:T(8,128)}) custom-call(bf16[2,3,1024,1536]{3,2,1,0:T(8,128)(2,1)S(1)} %load.3.held_ref, bf16[3,896,128]{2,1,0:T(8,128)(2,1)S(1)} %pack.4.refs_0_, bf16[3,896,128]{2,1,0:T(8,128)(2,1)S(1)} %collective-permute-done.6.refs_1_, ...), custom_call_target="tpu_custom_call", output_to_operand_aliasing={{0}: (5, {})} | custom-call | flops 603979776 | bytes 18874368 | tf_op jit(solution)/shard_map/merge/pallas_call | solution.py:206
  (3 shorter events, 0.1 us)
Async XLA Ops:
  1.8 13.9 %collective-permute-start.4 = (bf16[3,352,128]{2,1,0:T(8,128)(2,1)S(1)}, bf16[3,352,128]{2,1,0:T(8,128)(2,1)S(1)}, u32[]{:S(2)}, u32[]{:S(2)}) collective-permute-start(bf16[3,352,128]{2,1,0:T(8,128)(2,1)S(1)} %get-tuple-element.11.refs_0_), channel_id=1, source_target_pairs={{0,2},{1,3},{2,0},{3,1},{4,6},{5,7},{6,4},{7,5},{8,10},{9,11},{10,... | collective-permute-start | bytes 811016 | tf_op jit(solution)/shard_map/ppermute | solution.py:241
  4.8 4.4 %collective-permute-start.2 = (bf16[3,96,128]{2,1,0:T(8,128)(2,1)S(1)}, bf16[3,96,128]{2,1,0:T(8,128)(2,1)S(1)}, u32[]{:S(2)}, u32[]{:S(2)}) collective-permute-start(bf16[3,96,128]{2,1,0:T(8,128)(2,1)S(1)} %get-tuple-element.10), channel_id=1, source_target_pairs={{0,4},{4,0},{8,12},{12,8},{1,5},{5,1},{9,13},{13,9},{2,6},{6,2},{1... | collective-permute-start | bytes 221192 | tf_op jit(solution)/shard_map/ppermute | solution.py:241
  6.4 9.1 %collective-permute-start.1 = (bf16[3,96,128]{2,1,0:T(8,128)(2,1)S(1)}, bf16[3,96,128]{2,1,0:T(8,128)(2,1)S(1)}, u32[]{:S(2)}, u32[]{:S(2)}) collective-permute-start(bf16[3,96,128]{2,1,0:T(8,128)(2,1)S(1)} %get-tuple-element.10), channel_id=1, source_target_pairs={{0,12},{4,8},{8,4},{12,0},{1,13},{5,9},{9,5},{13,1},{2,14},{6,10},... | collective-permute-start | bytes 221192 | tf_op jit(solution)/shard_map/ppermute | solution.py:241
  8.9 6.8 %collective-permute-start = (bf16[3,96,128]{2,1,0:T(8,128)(2,1)S(1)}, bf16[3,96,128]{2,1,0:T(8,128)(2,1)S(1)}, u32[]{:S(2)}, u32[]{:S(2)}) collective-permute-start(bf16[3,96,128]{2,1,0:T(8,128)(2,1)S(1)} %get-tuple-element.10), channel_id=1, source_target_pairs={{0,8},{4,12},{8,0},{12,4},{1,9},{5,13},{9,1},{13,5},{2,10},{6,14},... | collective-permute-start | bytes 221192 | tf_op jit(solution)/shard_map/ppermute | solution.py:241
  9.2 6.5 %collective-permute-start.5 = (bf16[3,96,128]{2,1,0:T(8,128)(2,1)S(1)}, bf16[3,96,128]{2,1,0:T(8,128)(2,1)S(1)}, u32[]{:S(2)}, u32[]{:S(2)}) collective-permute-start(bf16[3,96,128]{2,1,0:T(8,128)(2,1)S(1)} %collective-permute-done.2.refs_0_.refs_2_), channel_id=1, source_target_pairs={{0,2},{1,3},{2,0},{3,1},{4,6},{5,7},{6,4},{7,5},{8,10},{9,11},{10,... | collective-permute-start | bytes 221192 | tf_op jit(solution)/shard_map/ppermute | solution.py:241
  15.8 2.2 %collective-permute-start.6 = (bf16[3,896,128]{2,1,0:T(8,128)(2,1)S(1)}, bf16[3,896,128]{2,1,0:T(8,128)(2,1)S(1)}, u32[]{:S(2)}, u32[]{:S(2)}) collective-permute-start(bf16[3,896,128]{2,1,0:T(8,128)(2,1)S(1)} %pack.4.refs_0_), channel_id=1, source_target_pairs={{0,1},{1,0},{2,3},{3,2},{4,5},{5,4},{6,7},{7,6},{8,9},{9,8},{10,11... | collective-permute-start | bytes 2064392 | tf_op jit(solution)/shard_map/ppermute | solution.py:241
  15.9 6.8 %collective-permute-start.3 = (bf16[3,192,128]{2,1,0:T(8,128)(2,1)S(1)}, bf16[3,192,128]{2,1,0:T(8,128)(2,1)S(1)}, u32[]{:S(2)}, u32[]{:S(2)}) collective-permute-start(bf16[3,192,128]{2,1,0:T(8,128)(2,1)S(1)} %pack.3.refs_4_.refs_2_.refs_0_), channel_id=1, source_target_pairs={{0,2},{1,3},{2,0},{3,1},{4,6},{5,7},{6,4},{7,5},{8,10},{9,11},{10,... | collective-permute-start | bytes 442376 | tf_op jit(solution)/shard_map/ppermute | solution.py:241
  22.7 1.7 %collective-permute-start.7 = (bf16[3,384,128]{2,1,0:T(8,128)(2,1)S(1)}, bf16[3,384,128]{2,1,0:T(8,128)(2,1)S(1)}, u32[]{:S(2)}, u32[]{:S(2)}) collective-permute-start(bf16[3,384,128]{2,1,0:T(8,128)(2,1)S(1)} %pack.5.refs_0_.refs_2_), channel_id=1, source_target_pairs={{0,1},{1,0},{2,3},{3,2},{4,5},{5,4},{6,7},{7,6},{8,9},{9,8},{10,11... | collective-permute-start | bytes 884744 | tf_op jit(solution)/shard_map/ppermute | solution.py:241

commit v17 on v16

--- a/solution.py
+++ b/solution.py
@@ -243,7 +243,7 @@
     both, w = select(narrow, wide, adapted_expert_index)
     w3, w2, w1 = [swap(w, "shard", k) for k in (3, 2, 1)]
     width = base.shape[2]
-    split = width * 13 // 16
+    split = width * 14 // 16
     span = 2 * columns * groups
     near_half, far_half = lambda s: s // 2, lambda s: 1 - s // 2
     held = load(base, [(near_half, span, 0, width), (far_half, span, 0, split)], w1)

time: 29.9 us -> 29.8 us (level)
  transfers between devices with their start and end apart: 8 -> 8, of which waited for: 3 -> 4; matrix products, arithmetic and copies ran while one was open for 0% -> 0% of each run, Pallas kernels for 41% -> 41%
where the time goes in v17:
time: 29.8 us; the launch traced here: 29.6 us
  Pallas kernels  19.1 us (64%)
  starting transfers between devices  9.48 us (32%)
  waiting for transfers between devices  0.86 us (3%)
    pallas_call x2, Pallas kernels, merge(): pl.pallas_call(functools.partial(merge_kernel, plan), out_shape=[jax.Shap...  9.87 us
    ppermute x8, starting transfers between devices, swap(): return lax.ppermute(x, axis, [(i, i ^ bit) for i in range(4)])  9.48 us
    pallas_call x2, Pallas kernels, load(): pl.pallas_call(functools.partial(load_kernel, blocks), out_shape=jax.Shap...  7.37 us
    pallas_call x1, Pallas kernels, select(): pl.pallas_call(select_kernel, out_shape=(jax.ShapeDtypeStruct((projection...  1.81 us
    ppermute x8, waiting for transfers between devices, swap(): return lax.ppermute(x, axis, [(i, i ^ bit) for i in range(4)])  0.86 us
  transfers between devices with their start and end apart: 8, of which 4 were waited for; matrix products, arithmetic and copies ran while one was open for 0% of the time, Pallas kernels for 41%

profile of v17, /device:TPU:0, one launch (start us, length us, event | category | flops | bytes accessed | tf_op | source)
XLA Modules:
  0.0 29.6 jit_solution(9354269796134940803)
XLA Ops:
  0.0 1.8 %select.1 = (bf16[3,352,128]{2,1,0:T(8,128)(2,1)S(1)}, bf16[3,96,128]{2,1,0:T(8,128)(2,1)S(1)}) custom-call(s32[2]{0:T(128)} %index_ref.1, bf16[32,3,64,256]{3,2,1,0:T(8,128)(2,1)} %bitcast.1, bf16[32,3,64,96]{3,2,1,0:T(8,128)(2,1)} %wide_ref.1), custom_call_target="tpu_custom_call" | custom-call | tf_op jit(solution)/shard_map/select/pallas_call | solution.py:52
  1.8 3.0 %collective-permute-start.4 = (bf16[3,352,128]{2,1,0:T(8,128)(2,1)S(1)}, bf16[3,352,128]{2,1,0:T(8,128)(2,1)S(1)}, u32[]{:S(2)}, u32[]{:S(2)}) collective-permute-start(bf16[3,352,128]{2,1,0:T(8,128)(2,1)S(1)} %get-tuple-element.11.refs_0_), channel_id=1, source_target_pairs={{0,2},{1,3},{2,0},{3,1},{4,6},{5,7},{6,4},{7,5},{8,10},{9,11},{10,... | collective-permute-start | bytes 811016 | tf_op jit(solution)/shard_map/ppermute | solution.py:241
  4.8 1.6 %collective-permute-start.2 = (bf16[3,96,128]{2,1,0:T(8,128)(2,1)S(1)}, bf16[3,96,128]{2,1,0:T(8,128)(2,1)S(1)}, u32[]{:S(2)}, u32[]{:S(2)}) collective-permute-start(bf16[3,96,128]{2,1,0:T(8,128)(2,1)S(1)} %get-tuple-element.10), channel_id=1, source_target_pairs={{0,4},{4,0},{8,12},{12,8},{1,5},{5,1},{9,13},{13,9},{2,6},{6,2},{1... | collective-permute-start | bytes 221192 | tf_op jit(solution)/shard_map/ppermute | solution.py:241
  6.4 2.5 %collective-permute-start.1 = (bf16[3,96,128]{2,1,0:T(8,128)(2,1)S(1)}, bf16[3,96,128]{2,1,0:T(8,128)(2,1)S(1)}, u32[]{:S(2)}, u32[]{:S(2)}) collective-permute-start(bf16[3,96,128]{2,1,0:T(8,128)(2,1)S(1)} %get-tuple-element.10), channel_id=1, source_target_pairs={{0,12},{4,8},{8,4},{12,0},{1,13},{5,9},{9,5},{13,1},{2,14},{6,10},... | collective-permute-start | bytes 221192 | tf_op jit(solution)/shard_map/ppermute | solution.py:241
  8.9 0.1 collective-permute-start
  9.0 0.2 collective-permute-done.2.refs_0_.refs_2_
  9.2 0.4 %collective-permute-start.5 = (bf16[3,96,128]{2,1,0:T(8,128)(2,1)S(1)}, bf16[3,96,128]{2,1,0:T(8,128)(2,1)S(1)}, u32[]{:S(2)}, u32[]{:S(2)}) collective-permute-start(bf16[3,96,128]{2,1,0:T(8,128)(2,1)S(1)} %collective-permute-done.2.refs_0_.refs_2_), channel_id=1, source_target_pairs={{0,2},{1,3},{2,0},{3,1},{4,6},{5,7},{6,4},{7,5},{8,10},{9,11},{10,... | collective-permute-start | bytes 221192 | tf_op jit(solution)/shard_map/ppermute | solution.py:241
  9.5 6.1 %load.2.refs_2_.held_ref.refs_1_ = bf16[2,3,1024,1536]{3,2,1,0:T(8,128)(2,1)S(1)} custom-call(bf16[2,3,1024,1536]{3,2,1,0:T(8,128)(2,1)} %base_ref.3, bf16[3,96,128]{2,1,0:T(8,128)(2,1)S(1)} %collective-permute-done.2.refs_0_.refs_2_), custom_call_target="tpu_custom_call" | custom-call | bytes 18874368 | tf_op jit(solution)/shard_map/load/pallas_call | solution.py:90
  15.6 0.0 collective-permute-done.1.refs_1_
  15.6 0.1 collective-permute-done.refs_0_
  15.7 0.0 collective-permute-done.5.refs_3_
  15.7 0.0 collective-permute-done.4.refs_1_
  15.8 0.1 collective-permute-start.6
  15.9 1.7 %collective-permute-start.3 = (bf16[3,192,128]{2,1,0:T(8,128)(2,1)S(1)}, bf16[3,192,128]{2,1,0:T(8,128)(2,1)S(1)}, u32[]{:S(2)}, u32[]{:S(2)}) collective-permute-start(bf16[3,192,128]{2,1,0:T(8,128)(2,1)S(1)} %pack.3.refs_4_.refs_2_.refs_0_), channel_id=1, source_target_pairs={{0,2},{1,3},{2,0},{3,1},{4,6},{5,7},{6,4},{7,5},{8,10},{9,11},{10,... | collective-permute-start | bytes 442376 | tf_op jit(solution)/shard_map/ppermute | solution.py:241
  17.6 0.4 %collective-permute-done.6.refs_1_ = bf16[3,896,128]{2,1,0:T(8,128)(2,1)S(1)} collective-permute-done((bf16[3,896,128]{2,1,0:T(8,128)(2,1)S(1)}, bf16[3,896,128]{2,1,0:T(8,128)(2,1)S(1)}, u32[]{:S(2)}, u32[]{:S(2)}) %collective-permute-start.6) | collective-permute-done | bytes 688160 | tf_op jit(solution)/shard_map/ppermute | solution.py:241
  18.0 4.6 %merge.2 = (bf16[2,3,1024,1536]{3,2,1,0:T(8,128)(2,1)}, f32[8,128]{1,0:T(8,128)S(1)}) custom-call(bf16[2,3,1024,1536]{3,2,1,0:T(8,128)(2,1)S(1)} %load.2.refs_2_.held_ref.refs_1_, bf16[3,896,128]{2,1,0:T(8,128)(2,1)S(1)} %pack.4.refs_0_, bf16[3,896,128]{2,1,0:T(8,128)(2,1)S(1)} %collective-permute-done.6.refs_1_, ...), custom_call_target="tpu_custom_call" | custom-call | flops 603979776 | bytes 18874368 | tf_op jit(solution)/shard_map/merge/pallas_call | solution.py:206
  22.6 0.0 collective-permute-done.3.refs_1_
  22.7 0.2 collective-permute-start.7
  22.9 1.3 %load.3.held_ref = bf16[2,3,1024,1536]{3,2,1,0:T(8,128)(2,1)S(1)} custom-call(bf16[2,3,1024,1536]{3,2,1,0:T(8,128)(2,1)} %base_ref.3, bf16[3,384,128]{2,1,0:T(8,128)(2,1)S(1)} %pack.5.refs_0_.refs_2_, bf16[2,3,1024,1536]{3,2,1,0:T(8,128)(2,1)S(1)} %load.2.refs_2_.held_ref.refs_1_), custom_call_target="tpu_custom_call", output_to_operand_aliasing={{}: (2, {})} | custom-call | bytes 18874368 | tf_op jit(solution)/shard_map/load/pallas_call | solution.py:90
  24.2 0.2 collective-permute-done.7.refs_3_
  24.3 5.2 %merge.3 = (bf16[2,3,1024,1536]{3,2,1,0:T(8,128)(2,1)}, f32[8,128]{1,0:T(8,128)}) custom-call(bf16[2,3,1024,1536]{3,2,1,0:T(8,128)(2,1)S(1)} %load.3.held_ref, bf16[3,896,128]{2,1,0:T(8,128)(2,1)S(1)} %pack.4.refs_0_, bf16[3,896,128]{2,1,0:T(8,128)(2,1)S(1)} %collective-permute-done.6.refs_1_, ...), custom_call_target="tpu_custom_call", output_to_operand_aliasing={{0}: (5, {})} | custom-call | flops 603979776 | bytes 18874368 | tf_op jit(solution)/shard_map/merge/pallas_call | solution.py:206
  (3 shorter events, 0.1 us)
Async XLA Ops:
  1.8 13.9 %collective-permute-start.4 = (bf16[3,352,128]{2,1,0:T(8,128)(2,1)S(1)}, bf16[3,352,128]{2,1,0:T(8,128)(2,1)S(1)}, u32[]{:S(2)}, u32[]{:S(2)}) collective-permute-start(bf16[3,352,128]{2,1,0:T(8,128)(2,1)S(1)} %get-tuple-element.11.refs_0_), channel_id=1, source_target_pairs={{0,2},{1,3},{2,0},{3,1},{4,6},{5,7},{6,4},{7,5},{8,10},{9,11},{10,... | collective-permute-start | bytes 811016 | tf_op jit(solution)/shard_map/ppermute | solution.py:241
  4.8 4.4 %collective-permute-start.2 = (bf16[3,96,128]{2,1,0:T(8,128)(2,1)S(1)}, bf16[3,96,128]{2,1,0:T(8,128)(2,1)S(1)}, u32[]{:S(2)}, u32[]{:S(2)}) collective-permute-start(bf16[3,96,128]{2,1,0:T(8,128)(2,1)S(1)} %get-tuple-element.10), channel_id=1, source_target_pairs={{0,4},{4,0},{8,12},{12,8},{1,5},{5,1},{9,13},{13,9},{2,6},{6,2},{1... | collective-permute-start | bytes 221192 | tf_op jit(solution)/shard_map/ppermute | solution.py:241
  6.4 9.2 %collective-permute-start.1 = (bf16[3,96,128]{2,1,0:T(8,128)(2,1)S(1)}, bf16[3,96,128]{2,1,0:T(8,128)(2,1)S(1)}, u32[]{:S(2)}, u32[]{:S(2)}) collective-permute-start(bf16[3,96,128]{2,1,0:T(8,128)(2,1)S(1)} %get-tuple-element.10), channel_id=1, source_target_pairs={{0,12},{4,8},{8,4},{12,0},{1,13},{5,9},{9,5},{13,1},{2,14},{6,10},... | collective-permute-start | bytes 221192 | tf_op jit(solution)/shard_map/ppermute | solution.py:241
  8.9 6.8 %collective-permute-start = (bf16[3,96,128]{2,1,0:T(8,128)(2,1)S(1)}, bf16[3,96,128]{2,1,0:T(8,128)(2,1)S(1)}, u32[]{:S(2)}, u32[]{:S(2)}) collective-permute-start(bf16[3,96,128]{2,1,0:T(8,128)(2,1)S(1)} %get-tuple-element.10), channel_id=1, source_target_pairs={{0,8},{4,12},{8,0},{12,4},{1,9},{5,13},{9,1},{13,5},{2,10},{6,14},... | collective-permute-start | bytes 221192 | tf_op jit(solution)/shard_map/ppermute | solution.py:241
  9.2 6.5 %collective-permute-start.5 = (bf16[3,96,128]{2,1,0:T(8,128)(2,1)S(1)}, bf16[3,96,128]{2,1,0:T(8,128)(2,1)S(1)}, u32[]{:S(2)}, u32[]{:S(2)}) collective-permute-start(bf16[3,96,128]{2,1,0:T(8,128)(2,1)S(1)} %collective-permute-done.2.refs_0_.refs_2_), channel_id=1, source_target_pairs={{0,2},{1,3},{2,0},{3,1},{4,6},{5,7},{6,4},{7,5},{8,10},{9,11},{10,... | collective-permute-start | bytes 221192 | tf_op jit(solution)/shard_map/ppermute | solution.py:241
  15.8 2.2 %collective-permute-start.6 = (bf16[3,896,128]{2,1,0:T(8,128)(2,1)S(1)}, bf16[3,896,128]{2,1,0:T(8,128)(2,1)S(1)}, u32[]{:S(2)}, u32[]{:S(2)}) collective-permute-start(bf16[3,896,128]{2,1,0:T(8,128)(2,1)S(1)} %pack.4.refs_0_), channel_id=1, source_target_pairs={{0,1},{1,0},{2,3},{3,2},{4,5},{5,4},{6,7},{7,6},{8,9},{9,8},{10,11... | collective-permute-start | bytes 2064392 | tf_op jit(solution)/shard_map/ppermute | solution.py:241
  15.9 6.8 %collective-permute-start.3 = (bf16[3,192,128]{2,1,0:T(8,128)(2,1)S(1)}, bf16[3,192,128]{2,1,0:T(8,128)(2,1)S(1)}, u32[]{:S(2)}, u32[]{:S(2)}) collective-permute-start(bf16[3,192,128]{2,1,0:T(8,128)(2,1)S(1)} %pack.3.refs_4_.refs_2_.refs_0_), channel_id=1, source_target_pairs={{0,2},{1,3},{2,0},{3,1},{4,6},{5,7},{6,4},{7,5},{8,10},{9,11},{10,... | collective-permute-start | bytes 442376 | tf_op jit(solution)/shard_map/ppermute | solution.py:241
  22.7 1.6 %collective-permute-start.7 = (bf16[3,384,128]{2,1,0:T(8,128)(2,1)S(1)}, bf16[3,384,128]{2,1,0:T(8,128)(2,1)S(1)}, u32[]{:S(2)}, u32[]{:S(2)}) collective-permute-start(bf16[3,384,128]{2,1,0:T(8,128)(2,1)S(1)} %pack.5.refs_0_.refs_2_), channel_id=1, source_target_pairs={{0,1},{1,0},{2,3},{3,2},{4,5},{5,4},{6,7},{7,6},{8,9},{9,8},{10,11... | collective-permute-start | bytes 884744 | tf_op jit(solution)/shard_map/ppermute | solution.py:241
